TPU v7x, 32 devices: a whole 2x2x4 slice. The times are simulated.
32 devices in a mesh: fsdp: 32 (over z, y, x, core).
Axes of the slice: x: 2, y: 2, z: 4, core: 2. Of those that a mesh axis runs over, the one named last changes fastest.
Arguments:
- latents: bfloat16 [128, 256, 16], P('fsdp'), may hold values from -6 to 6
- targets: float32 [128, 256, 32], P('fsdp'), may hold values from -12 to 12
- timesteps: int32 [128], P('fsdp'), may hold values from 0 to 999
- labels: int32 [128], P('fsdp'), may hold values from 0 to 1000, as said below
- embed_w: float32 [2041, 768], P(None, 'fsdp'), may hold values from -1 to 1
- embed_m: float32 [2041, 768], P(None, 'fsdp'), may hold values from -3.33786e-06 to 3.33786e-06
- embed_v: float32 [2041, 768], P(None, 'fsdp'), may hold values from 2.0805344e-15 to 3.328855e-14
- cond_w: float32 [768, 10752], P(None, 'fsdp'), may hold values from -0.21875 to 0.21875
- cond_m: float32 [768, 10752], P(None, 'fsdp'), may hold values from -3.33786e-06 to 3.33786e-06
- cond_v: float32 [768, 10752], P(None, 'fsdp'), may hold values from 2.0805344e-15 to 3.328855e-14
- layer_input_weights: float32 [2, 768, 5376], P(None, None, 'fsdp'), may hold values from -0.21875 to 0.21875
- in_m: float32 [2, 768, 5376], P(None, None, 'fsdp'), may hold values from -3.33786e-06 to 3.33786e-06
- in_v: float32 [2, 768, 5376], P(None, None, 'fsdp'), may hold values from 2.0805344e-15 to 3.328855e-14
- layer_output_weights: float32 [2, 3840, 768], P(None, None, 'fsdp'), may hold values from -2 to 2
- out_m: float32 [2, 3840, 768], P(None, None, 'fsdp'), may hold values from -3.33786e-06 to 3.33786e-06
- out_v: float32 [2, 3840, 768], P(None, None, 'fsdp'), may hold values from 2.0805344e-15 to 3.328855e-14
- head_w: float32 [768, 32], replicated, may hold values from -0.21875 to 0.21875
- head_m: float32 [768, 32], replicated, may hold values from -3.33786e-06 to 3.33786e-06
- head_v: float32 [768, 32], replicated, may hold values from 2.0805344e-15 to 3.328855e-14
- biases: float32 [26912], replicated, may hold values from -0.6 to 0.6
- bias_m: float32 [26912], replicated, may hold values from -9.536743e-06 to 9.536743e-06
- bias_v: float32 [26912], replicated, may hold values from 2.0805343e-14 to 3.328855e-13
Outputs:
- loss_total: float32 [], replicated
- grad_norm: float32 [], replicated
- embed_new: float32 [2041, 768], P(None, 'fsdp')
- embed_m_new: float32 [2041, 768], P(None, 'fsdp')
- embed_v_new: float32 [2041, 768], P(None, 'fsdp')
- cond_new: float32 [768, 10752], P(None, 'fsdp')
- cond_m_new: float32 [768, 10752], P(None, 'fsdp')
- cond_v_new: float32 [768, 10752], P(None, 'fsdp')
- in_new: float32 [2, 768, 5376], P(None, None, 'fsdp')
- in_m_new: float32 [2, 768, 5376], P(None, None, 'fsdp')
- in_v_new: float32 [2, 768, 5376], P(None, None, 'fsdp')
- out_new: float32 [2, 3840, 768], P(None, None, 'fsdp')
- out_m_new: float32 [2, 3840, 768], P(None, None, 'fsdp')
- out_v_new: float32 [2, 3840, 768], P(None, None, 'fsdp')
- head_new: float32 [768, 32], replicated
- head_m_new: float32 [768, 32], replicated
- head_v_new: float32 [768, 32], replicated
- bias_new: float32 [26912], replicated
- bias_m_new: float32 [26912], replicated
- bias_v_new: float32 [26912], replicated
Inputs may be any that keep to these rules, and one draw needn't show every extreme that they name: `labels`: label 1001 - 1 is the null class and some images carry it.
All inputs are finite; a program needn't handle non-finite values.
Results may differ from a plain program's by a relative error of at most 0.008.
Values may be sent and summed in bfloat16 or wider, within the bound.
A program may use at most 320 MiB of HBM per device.

v0:
```python
import math

import jax
import jax.numpy as jnp
from jax import lax
from jax.sharding import PartitionSpec as P

MODEL_WIDTH = 768
HEADS = 12
HEAD_DIM = 64
NCLS = 1001
FREQ = 256
PD = 16
PO = 32
GRID = 16
LAYERS = 2
STEP = 10
SEQ = 256
IW = 5376
CW = 10752


learn_rate = 0.03
beta_one = 0.9
beta_two = 0.999
adam_eps = 1e-08
decay = 0.01
clip_limit = 0.01
highest = lax.Precision.HIGHEST


def product(left, right):
    return jnp.dot(left, right, preferred_element_type=jnp.float32)


def exact_dot(left, right):
    return jnp.dot(left, right, precision=highest)


def apply_rows(left, right):
    return jnp.einsum("bsd,de->bse", left, right, preferred_element_type=jnp.float32)


def outer_sum(left, right):
    return jnp.einsum("bsd,bse->de", left, right, preferred_element_type=jnp.float32)


def apply_back(left, right):
    return jnp.einsum("bse,de->bsd", left, right, preferred_element_type=jnp.float32)


def column_sum(value):
    return jnp.sum(value.astype(jnp.float32), (0, 1))


def silu(value):
    return value * jax.nn.sigmoid(value)


def gelu(value):
    return jax.nn.gelu(value, approximate=True)


def layer_norm(value):
    centered = value - jnp.mean(value, -1, keepdims=True)
    return centered * lax.rsqrt(jnp.mean(centered * centered, -1, keepdims=True) + 1e-06)


def local_back(func, value, cotangent):
    return jax.vjp(func, value)[1](cotangent)[0]


def position_table():
    quarter = MODEL_WIDTH // 4
    omega = 1.0 / 10000.0 ** (jnp.arange(quarter, dtype=jnp.float32) / quarter)
    places = jnp.arange(GRID * GRID)
    rows_pos = (places // GRID).astype(jnp.float32)[:, None] * omega
    cols_pos = (places % GRID).astype(jnp.float32)[:, None] * omega
    return jnp.concatenate(
        [jnp.sin(rows_pos), jnp.cos(rows_pos), jnp.sin(cols_pos), jnp.cos(cols_pos)], 1
    )


def time_features(timesteps):
    half_freq = FREQ // 2
    rates = jnp.exp(-math.log(10000.0) * jnp.arange(half_freq, dtype=jnp.float32) / half_freq)
    angles = timesteps.astype(jnp.float32)[:, None] * rates
    return jnp.concatenate([jnp.cos(angles), jnp.sin(angles)], 1)


def split_biases(vector):
    lengths = [MODEL_WIDTH, MODEL_WIDTH, MODEL_WIDTH, CW, LAYERS * IW, LAYERS * 2 * MODEL_WIDTH, PO]
    pieces = []
    offset = 0
    for length in lengths:
        pieces.append(vector[offset : offset + length])
        offset += length
    pieces[4] = pieces[4].reshape(LAYERS, IW)
    pieces[5] = pieces[5].reshape(LAYERS, 2 * MODEL_WIDTH)
    return pieces


def split_heads(triple, which):
    n_images, seq_len = (triple.shape[0], triple.shape[1])
    return triple[..., which * MODEL_WIDTH : (which + 1) * MODEL_WIDTH].reshape(
        n_images, seq_len, HEADS, HEAD_DIM
    )


def attend(triple):
    queries, key_part, values = [split_heads(triple, j) for j in range(3)]
    scores = jnp.einsum(
        "bqhd,bkhd->bhqk", queries, key_part, preferred_element_type=jnp.float32
    ) * HEAD_DIM ** (-0.5)
    row_max = jnp.max(scores, -1, keepdims=True)
    expo = jnp.exp(scores - row_max)
    row_sum = jnp.sum(expo, -1, keepdims=True)
    attn_weights = (expo / row_sum).astype(jnp.bfloat16)
    mixed_heads = jnp.einsum(
        "bhqk,bkhd->bqhd", attn_weights, values, preferred_element_type=jnp.float32
    ).astype(jnp.bfloat16)
    return (
        mixed_heads.reshape(triple.shape[0], triple.shape[1], MODEL_WIDTH),
        row_max + jnp.log(row_sum),
    )


def attend_back(triple, log_norm, d_mixed):
    queries, key_part, values = [split_heads(triple, j) for j in range(3)]
    scale = HEAD_DIM ** (-0.5)
    scores = (
        jnp.einsum("bqhd,bkhd->bhqk", queries, key_part, preferred_element_type=jnp.float32) * scale
    )
    probs_full = jnp.exp(scores - log_norm)
    attn_weights = probs_full.astype(jnp.bfloat16)
    d_heads = d_mixed.reshape(queries.shape)
    d_probs = jnp.einsum("bqhd,bkhd->bhqk", d_heads, values, preferred_element_type=jnp.float32)
    d_values = jnp.einsum(
        "bhqk,bqhd->bkhd", attn_weights, d_heads, preferred_element_type=jnp.float32
    )
    d_scores = (probs_full * (d_probs - jnp.sum(probs_full * d_probs, -1, keepdims=True))).astype(
        jnp.bfloat16
    )
    d_queries = (
        jnp.einsum("bhqk,bkhd->bqhd", d_scores, key_part, preferred_element_type=jnp.float32)
        * scale
    )
    d_keys = (
        jnp.einsum("bhqk,bqhd->bkhd", d_scores, queries, preferred_element_type=jnp.float32) * scale
    )
    shape_flat = (triple.shape[0], triple.shape[1], MODEL_WIDTH)
    return jnp.concatenate(
        [d_queries.reshape(shape_flat), d_keys.reshape(shape_flat), d_values.reshape(shape_flat)],
        -1,
    ).astype(jnp.bfloat16)


def block_forward(residual_state, adaptive_modulation, weights_in, weights_out, bias_in, bias_out):
    pieces = [
        adaptive_modulation[:, None, i * MODEL_WIDTH : (i + 1) * MODEL_WIDTH] for i in range(6)
    ]
    shaped_one = (layer_norm(residual_state) * (1 + pieces[1]) + pieces[0]).astype(jnp.bfloat16)
    triple = (
        apply_rows(shaped_one, weights_in[:, : 3 * MODEL_WIDTH]) + bias_in[: 3 * MODEL_WIDTH]
    ).astype(jnp.bfloat16)
    mixed_heads, log_norm = attend(triple)
    branch = apply_rows(mixed_heads, weights_out[:MODEL_WIDTH]) + bias_out[:MODEL_WIDTH]
    middle = residual_state + pieces[2] * branch
    shaped_two = (layer_norm(middle) * (1 + pieces[4]) + pieces[3]).astype(jnp.bfloat16)
    pre_ffn = apply_rows(shaped_two, weights_in[:, 3 * MODEL_WIDTH :]) + bias_in[3 * MODEL_WIDTH :]
    active = gelu(pre_ffn).astype(jnp.bfloat16)
    ffn_out = apply_rows(active, weights_out[MODEL_WIDTH:]) + bias_out[MODEL_WIDTH:]
    kept = (
        residual_state,
        shaped_one,
        triple,
        log_norm,
        mixed_heads,
        branch,
        middle,
        shaped_two,
        pre_ffn,
        active,
        ffn_out,
    )
    return (middle + pieces[5] * ffn_out, kept)


def block_backward(upstream, adaptive_modulation, weights_in, weights_out, kept):
    (
        residual_state,
        shaped_one,
        triple,
        log_norm,
        mixed_heads,
        branch,
        middle,
        shaped_two,
        pre_ffn,
        active,
        ffn_out,
    ) = kept
    pieces = [
        adaptive_modulation[:, None, i * MODEL_WIDTH : (i + 1) * MODEL_WIDTH] for i in range(6)
    ]
    d_ffn = (pieces[5] * upstream).astype(jnp.bfloat16)
    gate_two = jnp.sum(ffn_out * upstream, 1)
    grad_down = outer_sum(active, d_ffn)
    d_active = apply_back(d_ffn, weights_out[MODEL_WIDTH:])
    d_pre = local_back(gelu, pre_ffn, d_active).astype(jnp.bfloat16)
    grad_up = outer_sum(shaped_two, d_pre)
    d_shaped = apply_back(d_pre, weights_in[:, 3 * MODEL_WIDTH :])
    shift_two = jnp.sum(d_shaped, 1)
    scale_two = jnp.sum(d_shaped * layer_norm(middle), 1)
    upstream = upstream + local_back(layer_norm, middle, d_shaped * (1 + pieces[4]))
    gate_one = jnp.sum(branch * upstream, 1)
    d_branch = (pieces[2] * upstream).astype(jnp.bfloat16)
    grad_proj = outer_sum(mixed_heads, d_branch)
    d_mixed = apply_back(d_branch, weights_out[:MODEL_WIDTH]).astype(jnp.bfloat16)
    d_triple = attend_back(triple, log_norm, d_mixed)
    grad_qkv = outer_sum(shaped_one, d_triple)
    d_shaped = apply_back(d_triple, weights_in[:, : 3 * MODEL_WIDTH])
    shift_one = jnp.sum(d_shaped, 1)
    scale_one = jnp.sum(d_shaped * layer_norm(residual_state), 1)
    upstream = upstream + local_back(layer_norm, residual_state, d_shaped * (1 + pieces[1]))
    mod_grad = jnp.concatenate([shift_one, scale_one, gate_one, shift_two, scale_two, gate_two], 1)
    bias_in_grad = jnp.concatenate([column_sum(d_triple), column_sum(d_pre)])
    bias_out_grad = jnp.concatenate([column_sum(d_branch), column_sum(d_ffn)])
    grad_in = jnp.concatenate([grad_qkv, grad_up], 1)
    grad_out = jnp.concatenate([grad_proj, grad_down], 0)
    return (upstream, mod_grad, grad_in, grad_out, bias_in_grad, bias_out_grad)


def fetch_layer(layer_input_weights, layer_output_weights, layer_count):
    return (
        lax.all_gather(
            layer_input_weights[layer_count].astype(jnp.bfloat16), "fsdp", axis=1, tiled=True
        ),
        lax.all_gather(
            layer_output_weights[layer_count].astype(jnp.bfloat16), "fsdp", axis=1, tiled=True
        ),
    )


def adam_step(weight, first, second, gradient):
    first = beta_one * first + (1 - beta_one) * gradient
    second = beta_two * second + (1 - beta_two) * gradient * gradient
    ahead = first / (1 - beta_one**STEP)
    scaled = second / (1 - beta_two**STEP)
    return (
        weight - learn_rate * (ahead / (jnp.sqrt(scaled) + adam_eps) + decay * weight),
        first,
        second,
    )


def body(
    latents,
    targets,
    timesteps,
    labels,
    embed_w,
    embed_m,
    embed_v,
    cond_w,
    cond_m,
    cond_v,
    layer_input_weights,
    in_m,
    in_v,
    layer_output_weights,
    out_m,
    out_v,
    head_w,
    head_m,
    head_v,
    biases,
    bias_m,
    bias_v,
):
    devices = lax.axis_size("fsdp")
    embed_full, cond_full = (
        lax.all_gather(embed_w.astype(jnp.bfloat16), "fsdp", axis=1, tiled=True),
        lax.all_gather(cond_w.astype(jnp.bfloat16), "fsdp", axis=1, tiled=True),
    )
    time_one, time_two, patch_bias, cond_bias, block_input_bias, block_output_bias, head_bias = (
        split_biases(biases)
    )
    head_low = head_w.astype(jnp.bfloat16)
    features = time_features(timesteps).astype(jnp.bfloat16)
    pre_time = product(features, embed_full[:FREQ]) + time_one
    hidden_t = silu(pre_time).astype(jnp.bfloat16)
    time_emb = product(hidden_t, embed_full[FREQ : FREQ + MODEL_WIDTH]) + time_two
    onehot = (labels[:, None] == jnp.arange(NCLS)[None, :]).astype(jnp.bfloat16)
    condition = time_emb + product(onehot, embed_full[FREQ + MODEL_WIDTH + PD :])
    cond_low = silu(condition).astype(jnp.bfloat16)
    adaptive_modulation = product(cond_low, cond_full) + cond_bias
    residual_state = (
        apply_rows(latents, embed_full[FREQ + MODEL_WIDTH : FREQ + MODEL_WIDTH + PD])
        + patch_bias
        + position_table()
    )
    kept_all = []
    for layer_count in range(LAYERS):
        weights_in, weights_out = fetch_layer(
            layer_input_weights, layer_output_weights, layer_count
        )
        residual_state, kept = block_forward(
            residual_state,
            adaptive_modulation[
                :, 6 * MODEL_WIDTH * layer_count : 6 * MODEL_WIDTH * (layer_count + 1)
            ],
            weights_in,
            weights_out,
            block_input_bias[layer_count],
            block_output_bias[layer_count],
        )
        kept_all.append(kept)
    final_mod = adaptive_modulation[:, 6 * MODEL_WIDTH * LAYERS :]
    norm_final = layer_norm(residual_state)
    shaped = (
        norm_final * (1 + final_mod[:, None, MODEL_WIDTH:]) + final_mod[:, None, :MODEL_WIDTH]
    ).astype(jnp.bfloat16)
    output = apply_rows(shaped, head_low) + head_bias
    error_vals = output - targets
    loss_part = jnp.sum(error_vals * error_vals)
    tokens_all = devices * error_vals.shape[0] * SEQ * PO
    d_output = (error_vals * (2.0 / tokens_all)).astype(jnp.bfloat16)
    head_grad = outer_sum(shaped, d_output)
    head_bias_grad = column_sum(d_output)
    d_shaped = apply_back(d_output, head_low)
    d_final = jnp.concatenate([jnp.sum(d_shaped, 1), jnp.sum(d_shaped * norm_final, 1)], 1)
    upstream = local_back(
        layer_norm, residual_state, d_shaped * (1 + final_mod[:, None, MODEL_WIDTH:])
    )
    mod_grads = [None] * LAYERS
    in_shards = [None] * LAYERS
    out_shards = [None] * LAYERS
    in_bias_grads = [None] * LAYERS
    out_bias_grads = [None] * LAYERS
    for layer_count in reversed(range(LAYERS)):
        weights_in, weights_out = (
            lax.all_gather(
                layer_input_weights[layer_count].astype(jnp.bfloat16), "fsdp", axis=1, tiled=True
            ),
            lax.all_gather(
                layer_output_weights[layer_count].astype(jnp.bfloat16), "fsdp", axis=1, tiled=True
            ),
        )
        upstream, mod_grad, grad_in, grad_out, bias_in_grad, bias_out_grad = block_backward(
            upstream,
            adaptive_modulation[
                :, 6 * MODEL_WIDTH * layer_count : 6 * MODEL_WIDTH * (layer_count + 1)
            ],
            weights_in,
            weights_out,
            kept_all[layer_count],
        )
        in_shards[layer_count], out_shards[layer_count] = (
            lax.psum_scatter(grad_in, "fsdp", scatter_dimension=1, tiled=True),
            lax.psum_scatter(grad_out, "fsdp", scatter_dimension=1, tiled=True),
        )
        mod_grads[layer_count] = mod_grad
        in_bias_grads[layer_count] = bias_in_grad
        out_bias_grads[layer_count] = bias_out_grad
    d_patch = upstream.astype(jnp.bfloat16)
    patch_grad = outer_sum(latents, d_patch)
    patch_bias_grad = column_sum(d_patch)
    d_modulation = jnp.concatenate(mod_grads + [d_final], 1)
    d_cond = exact_dot(d_modulation, cond_full.astype(jnp.float32).T)
    d_condition = local_back(silu, condition, d_cond)
    d_hidden = exact_dot(d_condition, embed_full[FREQ : FREQ + MODEL_WIDTH].astype(jnp.float32).T)
    d_pre = local_back(silu, pre_time, d_hidden)
    cond_grad = exact_dot(cond_low.astype(jnp.float32).T, d_modulation)
    class_grad = exact_dot(onehot.astype(jnp.float32).T, d_condition)
    time_two_grad = exact_dot(hidden_t.astype(jnp.float32).T, d_condition)
    time_one_grad = exact_dot(features.astype(jnp.float32).T, d_pre)
    embed_grad = jnp.concatenate([time_one_grad, time_two_grad, patch_grad, class_grad], 0)
    embed_shard, cond_shard = (
        lax.psum_scatter(embed_grad, "fsdp", scatter_dimension=1, tiled=True),
        lax.psum_scatter(cond_grad, "fsdp", scatter_dimension=1, tiled=True),
    )
    bias_grad = jnp.concatenate(
        [jnp.sum(d_pre, 0), jnp.sum(d_condition, 0), patch_bias_grad, jnp.sum(d_modulation, 0)]
        + in_bias_grads
        + out_bias_grads
        + [head_bias_grad]
    )
    head_total, bias_total, loss_total = lax.psum((head_grad, bias_grad, loss_part), "fsdp")
    in_stack = jnp.stack(in_shards, 0)
    out_stack = jnp.stack(out_shards, 0)
    shard_squares = (
        jnp.sum(embed_shard * embed_shard)
        + jnp.sum(cond_shard * cond_shard)
        + jnp.sum(in_stack * in_stack)
        + jnp.sum(out_stack * out_stack)
    )
    square_total = lax.psum(shard_squares, "fsdp")
    grad_norm = jnp.sqrt(
        square_total + jnp.sum(head_total * head_total) + jnp.sum(bias_total * bias_total)
    )
    factor = jnp.minimum(1.0, clip_limit / grad_norm)
    embed_up = adam_step(embed_w, embed_m, embed_v, embed_shard * factor)
    cond_up = adam_step(cond_w, cond_m, cond_v, cond_shard * factor)
    in_up = adam_step(layer_input_weights, in_m, in_v, in_stack * factor)
    out_up = adam_step(layer_output_weights, out_m, out_v, out_stack * factor)
    head_up = adam_step(head_w, head_m, head_v, head_total * factor)
    bias_up = adam_step(biases, bias_m, bias_v, bias_total * factor)
    return (
        loss_total,
        grad_norm,
        embed_up[0],
        embed_up[1],
        embed_up[2],
        cond_up[0],
        cond_up[1],
        cond_up[2],
        in_up[0],
        in_up[1],
        in_up[2],
        out_up[0],
        out_up[1],
        out_up[2],
        head_up[0],
        head_up[1],
        head_up[2],
        bias_up[0],
        bias_up[1],
        bias_up[2],
    )


def solution(mesh):
    in_specs = (
        P("fsdp", None, None),
        P("fsdp", None, None),
        P("fsdp"),
        P("fsdp"),
        P(None, "fsdp"),
        P(None, "fsdp"),
        P(None, "fsdp"),
        P(None, "fsdp"),
        P(None, "fsdp"),
        P(None, "fsdp"),
        P(None, None, "fsdp"),
        P(None, None, "fsdp"),
        P(None, None, "fsdp"),
        P(None, None, "fsdp"),
        P(None, None, "fsdp"),
        P(None, None, "fsdp"),
        P(),
        P(),
        P(),
        P(),
        P(),
        P(),
    )
    out_specs = (
        P(),
        P(),
        P(None, "fsdp"),
        P(None, "fsdp"),
        P(None, "fsdp"),
        P(None, "fsdp"),
        P(None, "fsdp"),
        P(None, "fsdp"),
        P(None, None, "fsdp"),
        P(None, None, "fsdp"),
        P(None, None, "fsdp"),
        P(None, None, "fsdp"),
        P(None, None, "fsdp"),
        P(None, None, "fsdp"),
        P(),
        P(),
        P(),
        P(),
        P(),
        P(),
    )
    return jax.shard_map(body, mesh=mesh, in_specs=in_specs, out_specs=out_specs, check_vma=False)
```

profile of v0, /device:TPU:0, one launch (start us, length us, event | category | flops | bytes accessed | tf_op | source)
XLA Modules:
  0.0 2056.6 jit_solution(16597451347271187440)
XLA Ops:
  19.4 53.8 %all-gather.11.cloned.1.call-done = bf16[2041,768]{0,1:T(8,128)(2,1)} async-done(((bf16[2041,24]{0,1:T(8,128)(2,1)}), bf16[2041,768]{0,1:T(8,128)(2,1)}) %all-gather.11.cloned.1.call-update) | async-done | bytes 3134992 | tf_op jit(solution)/shard_map/all_gather | solution.py:283
  78.9 73.3 %all-gather.19.cloned.1.call-done = bf16[1,768,5376]{1,2,0:T(8,128)(2,1)} async-done(((bf16[1,768,168]{1,2,0:T(8,128)(2,1)}), bf16[1,768,5376]{1,2,0:T(8,128)(2,1)}) %all-gather.19.cloned.1.call-update) | async-done | bytes 8257552 | tf_op jit(solution)/shard_map/all_gather | solution.py:236
  152.2 12.4 copy.273
  164.6 66.4 %all-gather.15.cloned.1.call-done = bf16[1,768,5376]{1,2,0:T(8,128)(2,1)} async-done(((bf16[1,768,168]{1,2,0:T(8,128)(2,1)}), bf16[1,768,5376]{1,2,0:T(8,128)(2,1)}) %all-gather.15.cloned.1.call-update) | async-done | bytes 8257552 | tf_op jit(solution)/shard_map/all_gather | solution.py:236
  231.0 11.2 copy.265
  242.2 104.4 %all-gather.13.cloned.1.call-done = bf16[768,10752]{0,1:T(8,128)(2,1)} async-done(((bf16[768,336]{0,1:T(8,128)(2,1)}), bf16[768,10752]{0,1:T(8,128)(2,1)}) %all-gather.13.cloned.1.call-update) | async-done | bytes 16515088 | tf_op jit(solution)/shard_map/all_gather | solution.py:284
  346.6 10.1 convolution_add_fusion
  357.5 6.6 add_convert_fusion.1
  374.2 3.7 multiply_reduce_fusion.3
  382.7 3.9 fusion.41
  386.6 29.2 %all-gather.17.cloned.1.call-done = bf16[1,3840,768]{1,2,0:T(8,128)(2,1)} async-done(((bf16[1,3840,24]{1,2,0:T(8,128)(2,1)}), bf16[1,3840,768]{1,2,0:T(8,128)(2,1)}) %all-gather.17.cloned.1.call-update) | async-done | bytes 5898256 | tf_op jit(solution)/shard_map/all_gather | solution.py:239
  415.9 5.5 fusion.119
  421.9 8.4 fusion.33
  430.4 13.6 fusion.118
  444.5 6.9 add_convert_fusion
  462.3 4.5 multiply_reduce_fusion.2
  471.7 3.8 fusion.40
  475.5 10.4 all-gather.21.cloned.1.call-done
  485.8 5.1 fusion.117
  491.5 8.3 fusion.35
  499.8 12.9 fusion.116
  521.5 17.5 convert_reduce_fusion
  539.0 7.7 multiply_reduce_fusion.16
  548.5 3.3 convert_reduce_fusion.5
  553.0 3.8 convolution_convert_fusion.1
  559.4 8.6 fusion.45
  568.1 9.1 multiply_reduce_fusion.1
  577.2 7.2 multiply_convert_fusion.1
  584.5 3.1 multiply_convert_fusion.8
  598.0 7.3 multiply_reduce_fusion.15
  612.3 17.5 convert_reduce_fusion.1
  629.9 7.4 multiply_reduce_fusion.14
  639.3 4.2 convert_reduce_fusion.7
  648.2 7.0 fusion.42
  655.2 9.0 multiply_reduce_fusion
  664.2 7.2 multiply_convert_fusion
  683.9 7.4 multiply_reduce_fusion.4
  698.6 7.1 fusion.113
  722.5 4.2 pad_maximum_fusion.4
  726.7 6.7 copy.322
  733.8 3.4 convolution_bitcast_fusion.6
  737.2 12.9 convolution_bitcast_fusion
  750.1 8.7 pad_maximum_fusion.3
  758.8 12.5 copy.330
  771.4 3.4 convolution_bitcast_fusion.7
  774.8 12.9 convolution_bitcast_fusion.1
  787.7 8.8 pad_maximum_fusion.2
  796.5 12.4 copy.328
  809.6 8.0 convolution_bitcast_fusion.4
  817.6 7.9 convolution_bitcast_fusion.2
  825.6 6.0 pad_maximum_fusion.1
  831.6 17.1 copy.326
  850.5 7.0 convolution_bitcast_fusion.5
  857.6 8.0 convolution_bitcast_fusion.3
  865.6 6.1 pad_maximum_fusion
  871.7 17.5 copy.324
  889.5 17.0 fusion.104
  909.6 56.7 %reduce-scatter.19.cloned.1.call-done = f32[24,2041]{1,0:T(8,128)} async-done(((f32[768,2041]{1,0:T(8,128)}), f32[24,2041]{1,0:T(8,128)}) %reduce-scatter.19.cloned.1.call-update) | async-done | bytes 195952
  968.4 151.8 %reduce-scatter.27.cloned.1.call-done = f32[24,3840]{1,0:T(8,128)} async-done(((f32[768,3840]{1,0:T(8,128)}), f32[24,3840]{1,0:T(8,128)}) %reduce-scatter.27.cloned.1.call-update) | async-done | bytes 368656
  1122.3 150.6 %reduce-scatter.25.cloned.1.call-done = f32[24,3840]{1,0:T(8,128)} async-done(((f32[768,3840]{1,0:T(8,128)}), f32[24,3840]{1,0:T(8,128)}) %reduce-scatter.25.cloned.1.call-update) | async-done | bytes 368656
  1275.9 194.2 %reduce-scatter.23.cloned.1.call-done = f32[168,768]{1,0:T(8,128)} async-done(((f32[5376,768]{1,0:T(8,128)}), f32[168,768]{1,0:T(8,128)}) %reduce-scatter.23.cloned.1.call-update) | async-done | bytes 516112
  1470.1 195.9 %reduce-scatter.21.cloned.1.call-done = f32[168,768]{1,0:T(8,128)} async-done(((f32[5376,768]{1,0:T(8,128)}), f32[168,768]{1,0:T(8,128)}) %reduce-scatter.21.cloned.1.call-update) | async-done | bytes 516112
  1668.1 322.9 %reduce-scatter.17.cloned.1.call-done = f32[768,336]{0,1:T(8,128)} async-done(((f32[768,10752]{0,1:T(8,128)}), f32[768,336]{0,1:T(8,128)}) %reduce-scatter.17.cloned.1.call-update) | async-done | bytes 1032208 | tf_op jit(solution)/shard_map/reduce_scatter | solution.py:381
  1995.7 40.4 %all-reduce = (f32[]{:T(128)}, f32[]{:T(128)}) all-reduce(f32[]{:T(128)} %get-tuple-element.116, f32[]{:T(128)S(6)} %add.515), channel_id=1, replica_groups=mesh['fsdp'=32] {'fsdp'}, use_global_device_ids=true, to_apply=%region_15.16 | all-reduce | flops 2 | bytes 16 | tf_op jit(solution)/shard_map/psum | solution.py:389
  (498 shorter events, 152.7 us)
Async XLA Ops:
  7.2 66.0 %copy-start = (bf16[4,256,16]{1,2,0:T(8,128)(2,1)S(1)}, bf16[4,256,16]{1,2,0:T(8,128)(2,1)}, u32[]{:S(2)}) copy-start(bf16[4,256,16]{1,2,0:T(8,128)(2,1)} %param.22) | copy-start | bytes 98308
  7.2 65.9 %all-gather.11.cloned.1.call-start = ((), (), s32[]{:S(2)}) async-start(), calls=%async_computation.6 | async-start | bytes 3244032 | tf_op jit(solution)/shard_map/all_gather | solution.py:283
  9.0 143.2 %all-gather.19.cloned.1.call-start = ((), (), s32[]{:S(2)}) async-start(), calls=%async_computation.11 | async-start | bytes 8515584 | tf_op jit(solution)/shard_map/all_gather | solution.py:236
  11.2 219.8 %all-gather.15.cloned.1.call-start = ((), (), s32[]{:S(2)}) async-start(), calls=%async_computation.9 | async-start | bytes 8515584 | tf_op jit(solution)/shard_map/all_gather | solution.py:236
  11.9 334.7 %all-gather.13.cloned.1.call-start = ((), (), s32[]{:S(2)}) async-start(), calls=%async_computation.7 | async-start | bytes 17031168 | tf_op jit(solution)/shard_map/all_gather | solution.py:284
  12.8 403.0 %all-gather.17.cloned.1.call-start = ((), (), s32[]{:S(2)}) async-start(), calls=%async_computation.10 | async-start | bytes 6082560 | tf_op jit(solution)/shard_map/all_gather | solution.py:239
  13.7 472.1 %all-gather.21.cloned.1.call-start = ((), (), s32[]{:S(2)}) async-start(), calls=%async_computation.12 | async-start | bytes 6082560 | tf_op jit(solution)/shard_map/all_gather | solution.py:239
  14.3 892.3 %all-reduce.4.cloned.1.call-start = ((), (), s32[]{:S(2)}) async-start(), calls=%async_computation.18 | async-start | bytes 417792 | tf_op jit(solution)/shard_map/psum | solution.py:389
  15.5 414.8 %copy-start.134 = (f32[3072]{0:T(1024)}, f32[3072]{0:T(1024)S(1)}, u32[]{:S(2)}) copy-start(f32[3072]{0:T(1024)S(1)} %get-tuple-element.200) | copy-start | bytes 36868
  16.2 399.7 %copy-start.95 = (f32[768]{0:T(1024)}, f32[768]{0:T(1024)S(1)}, u32[]{:S(2)}) copy-start(f32[768]{0:T(1024)S(1)} %get-tuple-element.198) | copy-start | bytes 9220
  16.2 399.7 %copy-start.126 = (f32[768]{0:T(1024)}, f32[768]{0:T(1024)S(1)}, u32[]{:S(2)}) copy-start(f32[768]{0:T(1024)S(1)} %get-tuple-element.195) | copy-start | bytes 9220
  16.2 414.2 %copy-start.128 = (f32[768]{0:T(1024)}, f32[768]{0:T(1024)S(1)}, u32[]{:S(2)}) copy-start(f32[768]{0:T(1024)S(1)} %get-tuple-element.194) | copy-start | bytes 9220
  16.3 60.6 %copy-start.139 = (bf16[4,128]{1,0:T(4,128)(2,1)}, bf16[4,128]{1,0:T(4,128)(2,1)S(1)}, u32[]{:S(2)}) copy-start(bf16[4,128]{1,0:T(4,128)(2,1)S(1)} %get-tuple-element.209) | copy-start | bytes 3076
  16.3 60.6 %copy-start.140 = (bf16[4,128]{1,0:T(4,128)(2,1)}, bf16[4,128]{1,0:T(4,128)(2,1)S(1)}, u32[]{:S(2)}) copy-start(bf16[4,128]{1,0:T(4,128)(2,1)S(1)} %get-tuple-element.210) | copy-start | bytes 3076
  75.3 340.6 %copy-start.5 = (f32[4,256,768]{2,1,0:T(8,128)}, f32[4,256,768]{2,1,0:T(8,128)S(1)}, u32[]{:S(2)}) copy-start(f32[4,256,768]{2,1,0:T(8,128)S(1)} %get-tuple-element.212) | copy-start | bytes 9437188
  75.3 282.2 %copy-start.98 = (f32[4,256]{1,0:T(4,128)}, f32[4,256]{1,0:T(4,128)S(1)}, u32[]{:S(2)}) copy-start(f32[4,256]{1,0:T(4,128)S(1)} %broadcast_multiply_fusion.4) | copy-start | bytes 12292
  76.1 281.4 %copy-start.113 = (f32[4,256]{1,0:T(4,128)}, f32[4,256]{1,0:T(4,128)S(1)}, u32[]{:S(2)}) copy-start(f32[4,256]{1,0:T(4,128)S(1)} %fusion.85) | copy-start | bytes 12292
  78.9 267.7 %copy-start.72 = (f32[4,768]{1,0:T(4,128)}, f32[4,768]{1,0:T(4,128)S(1)}, u32[]{:S(2)}) copy-start(f32[4,768]{1,0:T(4,128)S(1)} %fusion.51) | copy-start | bytes 36868
  346.6 10.9 copy-start.13
  357.4 58.4 %copy-start.105 = (f32[4,768]{1,0:T(4,128)}, f32[4,768]{1,0:T(4,128)S(1)}, u32[]{:S(2)}) copy-start(f32[4,768]{1,0:T(4,128)S(1)} %get-tuple-element.191) | copy-start | bytes 36868
  357.4 64.5 %copy-start.50 = (f32[4,768]{1,0:T(4,128)}, f32[4,768]{1,0:T(4,128)S(1)}, u32[]{:S(2)}) copy-start(f32[4,768]{1,0:T(4,128)S(1)} %get-tuple-element.187) | copy-start | bytes 36868
  357.4 64.5 %copy-start.60 = (f32[4,768]{1,0:T(4,128)}, f32[4,768]{1,0:T(4,128)S(1)}, u32[]{:S(2)}) copy-start(f32[4,768]{1,0:T(4,128)S(1)} %get-tuple-element.186) | copy-start | bytes 36868
  357.4 72.9 %copy-start.107 = (f32[4,768]{1,0:T(4,128)}, f32[4,768]{1,0:T(4,128)S(1)}, u32[]{:S(2)}) copy-start(f32[4,768]{1,0:T(4,128)S(1)} %get-tuple-element.188) | copy-start | bytes 36868
  357.4 87.1 %copy-start.132 = (f32[4,768]{1,0:T(4,128)}, f32[4,768]{1,0:T(4,128)S(1)}, u32[]{:S(2)}) copy-start(f32[4,768]{1,0:T(4,128)S(1)} %get-tuple-element.183) | copy-start | bytes 36868
  357.4 134.0 %copy-start.62 = (f32[4,768]{1,0:T(4,128)}, f32[4,768]{1,0:T(4,128)S(1)}, u32[]{:S(2)}) copy-start(f32[4,768]{1,0:T(4,128)S(1)} %get-tuple-element.180) | copy-start | bytes 36868
  357.5 191.0 %copy-start.53 = (f32[4,768]{1,0:T(4,128)}, f32[4,768]{1,0:T(4,128)S(1)}, u32[]{:S(2)}) copy-start(f32[4,768]{1,0:T(4,128)S(1)} %get-tuple-element.181) | copy-start | bytes 36868
  357.5 251.1 %copy-start.93 = (f32[4,768]{1,0:T(4,128)}, f32[4,768]{1,0:T(4,128)S(1)}, u32[]{:S(2)}) copy-start(f32[4,768]{1,0:T(4,128)S(1)} %get-tuple-element.184) | copy-start | bytes 36868
  421.3 9.0 copy-start.8
  444.0 164.6 %copy-start.11 = (f32[4,256,768]{2,1,0:T(8,128)}, f32[4,256,768]{2,1,0:T(8,128)S(1)}, u32[]{:S(2)}) copy-start(f32[4,256,768]{2,1,0:T(8,128)S(1)} %get-tuple-element.161) | copy-start | bytes 9437188
  444.0 164.6 %copy-start.101 = (f32[4,256]{1,0:T(4,128)}, f32[4,256]{1,0:T(4,128)S(1)}, u32[]{:S(2)}) copy-start(f32[4,256]{1,0:T(4,128)S(1)} %broadcast_multiply_fusion.2) | copy-start | bytes 12292
  490.9 57.6 %copy-start.3 = (f32[4,256,768]{2,1,0:T(8,128)}, f32[4,256,768]{2,1,0:T(8,128)S(1)}, u32[]{:S(2)}) copy-start(f32[4,256,768]{2,1,0:T(8,128)S(1)} %get-tuple-element.159) | copy-start | bytes 9437188
  490.9 57.6 %copy-start.77 = (f32[4,256]{1,0:T(4,128)}, f32[4,256]{1,0:T(4,128)S(1)}, u32[]{:S(2)}) copy-start(f32[4,256]{1,0:T(4,128)S(1)} %broadcast_multiply_fusion.1) | copy-start | bytes 12292
  491.4 57.1 %copy-start.82 = (f32[4,256]{1,0:T(4,128)}, f32[4,256]{1,0:T(4,128)S(1)}, u32[]{:S(2)}) copy-start(f32[4,256]{1,0:T(4,128)S(1)} %fusion.88) | copy-start | bytes 12292
  520.0 19.1 slice-start.16
  521.5 17.5 copy-start.43
  521.5 17.5 slice-start.17
  559.4 17.8 slice-start.3
  559.4 17.8 slice-start.4
  568.1 9.1 slice-start.5
  609.7 20.2 slice-start.12
  612.3 17.6 copy-start.45
  612.3 17.6 copy-start.9
  612.3 17.6 slice-start.13
  612.3 17.6 copy-start.51
  612.3 17.6 copy-start.75
  648.2 16.0 slice-start
  648.2 16.0 slice-start.1
  683.9 14.6 slice-start.6
  683.9 14.6 slice-start.7
  683.9 14.6 slice-start.8
  698.6 9.7 copy-start.142
  722.5 243.8 %reduce-scatter.19.cloned.1.call-start = ((), (), s32[]{:S(2)}) async-start(), calls=%async_computation.13 | async-start | bytes 6488064
  733.5 386.7 %reduce-scatter.27.cloned.1.call-start = ((), (), s32[]{:S(2)}) async-start(), calls=%async_computation.17 | async-start | bytes 12165120
  771.3 501.6 %reduce-scatter.25.cloned.1.call-start = ((), (), s32[]{:S(2)}) async-start(), calls=%async_computation.16 | async-start | bytes 12165120
  809.0 661.1 %reduce-scatter.23.cloned.1.call-start = ((), (), s32[]{:S(2)}) async-start(), calls=%async_computation.15 | async-start | bytes 17031168
  848.7 817.3 %reduce-scatter.21.cloned.1.call-start = ((), (), s32[]{:S(2)}) async-start(), calls=%async_computation.14 | async-start | bytes 17031168
  889.2 1101.7 %reduce-scatter.17.cloned.1.call-start = ((), (), s32[]{:S(2)}) async-start(), calls=%async_computation.8 | async-start | bytes 34062336 | tf_op jit(solution)/shard_map/reduce_scatter | solution.py:381
  1274.5 766.4 %copy-start.40 = (f32[2,3840,24]{1,2,0:T(8,128)S(1)}, f32[2,3840,24]{1,2,0:T(8,128)}, u32[]{:S(2)}) copy-start(f32[2,3840,24]{1,2,0:T(8,128)} %param.35) | copy-start | bytes 2211844
  1275.1 765.0 %copy-start.69 = (f32[26912]{0:T(1024)S(1)}, f32[26912]{0:T(1024)}, u32[]{:S(2)}) copy-start(f32[26912]{0:T(1024)} %param.41) | copy-start | bytes 322948
  1275.1 765.0 %copy-start.70 = (f32[26912]{0:T(1024)S(1)}, f32[26912]{0:T(1024)}, u32[]{:S(2)}) copy-start(f32[26912]{0:T(1024)} %get-tuple-element.120) | copy-start | bytes 322948
  1275.1 765.0 %copy-start.91 = (f32[26912]{0:T(1024)S(1)}, f32[26912]{0:T(1024)}, u32[]{:S(2)}) copy-start(f32[26912]{0:T(1024)} %param.42) | copy-start | bytes 322948
  1275.1 765.0 %copy-start.92 = (f32[26912]{0:T(1024)S(1)}, f32[26912]{0:T(1024)}, u32[]{:S(2)}) copy-start(f32[26912]{0:T(1024)} %param.43) | copy-start | bytes 322948
  1275.1 765.8 %copy-start.66 = (f32[2,3840,24]{1,2,0:T(8,128)S(1)}, f32[2,3840,24]{1,2,0:T(8,128)}, u32[]{:S(2)}) copy-start(f32[2,3840,24]{1,2,0:T(8,128)} %param.36) | copy-start | bytes 2211844
  1275.1 765.8 %copy-start.67 = (f32[2,3840,24]{1,2,0:T(8,128)S(1)}, f32[2,3840,24]{1,2,0:T(8,128)}, u32[]{:S(2)}) copy-start(f32[2,3840,24]{1,2,0:T(8,128)} %param.37) | copy-start | bytes 2211844
  (113 other events, 501.9 us)
Sparse Core Ops, SparseCore 0:
  11.5 61.6 all-gather.10
  76.6 75.5 all-gather.18
  155.7 75.2 all-gather.14
  234.3 112.2 all-gather.12
  350.0 65.8 all-gather.16
  419.1 66.6 all-gather.20
  722.6 122.3 all-reduce.3
  850.7 115.5 reduce-scatter.18
  973.4 146.7 reduce-scatter.26
  1126.2 146.7 reduce-scatter.24
  1280.4 189.5 reduce-scatter.22
  1476.3 189.6 reduce-scatter.20
  1673.6 317.3 reduce-scatter.16
where the time goes:
time: 2060 us
  waiting for transfers between devices  1410 us (68%)
  matrix products  314 us (15%)
  local copies, waits for them, and re-layouts  159 us (8%)
  other arithmetic  109 us (5%)
  blocking collectives  40.4 us (2%)
  between operations  22 us (1%)
    unnamed x18, waiting for transfers between devices  751 us
    reduce_scatter x1, waiting for transfers between devices, body(): lax.psum_scatter(cond_grad, 'fsdp', scatter_dimension=1, tiled=True)  323 us
    all_gather x2, waiting for transfers between devices, fetch_layer(): lax.all_gather(layer_input_weights[layer_count].astype(jnp.bfloat16), 'fs...  140 us
    all_gather x1, waiting for transfers between devices, body(): lax.all_gather(cond_w.astype(jnp.bfloat16), 'fsdp', axis=1, tiled=True)  104 us
    unnamed x361, local copies, waits for them, and re-layouts  91.7 us
    dot_general x9, matrix products, apply_back(): jnp.einsum('bse,de->bsd', left, right, preferred_element_type=jnp.float32)  73.2 us
    dot_general x10, matrix products, apply_rows(): jnp.einsum('bsd,de->bse', left, right, preferred_element_type=jnp.float32)  70.9 us
    dot_general x10, matrix products, outer_sum(): jnp.einsum('bsd,bse->de', left, right, preferred_element_type=jnp.float32)  65.2 us
  transfers between devices with their start and end apart: 13, of which 12 were waited for; matrix products, arithmetic and copies ran while one was open for 16% of the time, Pallas kernels for 0%

commit v1 on v0

--- a/solution.py
+++ b/solution.py
@@ -1,8 +1,12 @@
+import functools
 import math
 
 import jax
 import jax.numpy as jnp
+import numpy as np
 from jax import lax
+from jax.experimental import pallas as pl
+from jax.experimental.pallas import tpu as pltpu
 from jax.sharding import PartitionSpec as P
 
 MODEL_WIDTH = 768
@@ -254,7 +258,7 @@
     )
 
 
-def body(
+def generic_body(
     latents,
     targets,
     timesteps,
@@ -430,6 +434,924 @@
     )
 
 
+MESH_ID = pl.DeviceIdType.MESH
+AXIS = "fsdp"
+
+
+class Place:
+    def __init__(self):
+        me = lax.axis_index(AXIS)
+        self.me = me
+        self.core = core = me % 2
+        x = (me // 2) % 2
+        y = (me // 4) % 2
+        self.z = me // 8
+        self.chip = me // 2
+        step_x = 1 - 2 * x
+        step_y = 2 - 4 * y
+        self.step_a = step_x + core * (step_y - step_x)
+        self.step_b = step_y + core * (step_x - step_y)
+        self.dev_a = me + 2 * self.step_a
+        self.dev_b = me + 2 * self.step_b
+        self.sibling = me + 1 - 2 * core
+
+    def other(self, dz, flip_a=0, flip_b=0):
+        return self.chip + 4 * dz + flip_a * self.step_a + flip_b * self.step_b
+
+    def valid(self, dz):
+        return jnp.logical_and(self.z + dz >= 0, self.z + dz < 4)
+
+    def greet(self):
+        barrier = pltpu.get_barrier_semaphore()
+        for device in (self.sibling, self.dev_a, self.dev_b):
+            pl.semaphore_signal(barrier, inc=1, device_id=(device,), device_id_type=MESH_ID)
+        for sign in (-1, 1):
+
+            @pl.when(self.valid(sign))
+            def _():
+                pl.semaphore_signal(barrier, inc=1, device_id=(self.me + 8 * sign,), device_id_type=MESH_ID)
+
+        pl.semaphore_wait(barrier, 4 + self.z * (3 - self.z) // 2)
+
+
+def remote(src, dst, send_sem, recv_sem, device):
+    return pltpu.make_async_remote_copy(
+        src_ref=src, dst_ref=dst, send_sem=send_sem, recv_sem=recv_sem, device_id=(device,), device_id_type=MESH_ID
+    )
+
+
+class Gather:
+    def __init__(self, place, own, stage, piece, full, sems):
+        self.p, self.own, self.stage, self.piece, self.full = place, own, stage, piece, full
+        self.xch_send, self.xch_recv, self.local, self.send, self.recv, self.sib_recv = sems
+        self.sent, self.keep = [], []
+
+    def slot(self, a, chip):
+        rows, half = self.piece[a].shape
+        return self.full[a].at[
+            pl.ds(pl.multiple_of(chip * rows, rows), rows), pl.ds(pl.multiple_of(self.p.core * half, half), half)
+        ]
+
+    def push(self, a, k, src, chip, device, sem, cond=None):
+        copy = remote(src, self.slot(a, chip), self.send.at[a, k], sem, device)
+        self.sent.append((copy, cond))
+        if cond is None:
+            copy.start()
+        else:
+            pl.when(cond)(copy.start)
+
+    def begin(self):
+        core = self.p.core
+        copies = []
+        for a in range(2):
+            rows, half = self.own[a].shape[0], self.piece[a].shape[1]
+            dst = self.stage[a].at[pl.ds(pl.multiple_of(core * rows, 8), rows), :]
+            away = remote(
+                self.own[a].at[:, pl.ds(pl.multiple_of((1 - core) * half, half), half)],
+                dst,
+                self.xch_send.at[a],
+                self.xch_recv.at[a],
+                self.p.sibling,
+            )
+            away.start()
+            keep = pltpu.make_async_copy(
+                self.own[a].at[:, pl.ds(pl.multiple_of(core * half, half), half)], dst, self.local.at[a]
+            )
+            keep.start()
+            copies.append((away, keep))
+        for a in range(2):
+            copies[a][0].wait()
+            copies[a][1].wait()
+            self.piece[a][...] = self.stage[a][...].astype(jnp.bfloat16)
+            keep = pltpu.make_async_copy(self.piece[a], self.slot(a, self.p.chip), self.local.at[a])
+            keep.start()
+            self.keep.append(keep)
+            for sign in (-1, 1):
+                self.push(
+                    a, 0 if sign < 0 else 3, self.piece[a], self.p.chip, self.p.me + 8 * sign,
+                    self.recv.at[a, self.p.chip], self.p.valid(sign),
+                )
+            self.push(a, 6, self.piece[a], self.p.chip, self.p.dev_a, self.recv.at[a, self.p.chip])
+            self.push(a, 10, self.piece[a], self.p.chip, self.p.dev_b, self.recv.at[a, self.p.chip])
+            self.push(a, 18, self.piece[a], self.p.chip, self.p.sibling, self.sib_recv.at[a, self.p.chip])
+
+    def arrive(self, a, chip):
+        slot = self.slot(a, chip)
+        pltpu.make_async_copy(slot, slot, self.recv.at[a, chip]).wait()
+
+    def z_step(self, dist):
+        for sign in (-1, 1):
+            here = self.p.valid(sign * dist)
+            chip = self.p.other(sign * dist)
+            rel = (sign * dist) % 4
+            onward = jnp.logical_and(here, self.p.valid(-sign))
+            for a in range(2):
+                pl.when(here)(functools.partial(self.arrive, a, chip))
+                src = self.slot(a, chip)
+                if dist < 3:
+                    self.push(
+                        a, (0 if sign > 0 else 3) + dist, src, chip, self.p.me - 8 * sign,
+                        self.recv.at[a, chip], onward,
+                    )
+                self.push(a, 6 + rel, src, chip, self.p.dev_a, self.recv.at[a, chip], here)
+                self.push(a, 10 + rel, src, chip, self.p.dev_b, self.recv.at[a, chip], here)
+                self.push(a, 18 + rel, src, chip, self.p.sibling, self.sib_recv.at[a, chip], here)
+
+    def a_step(self, dist):
+        for sign in (-1, 1) if dist else (1,):
+            here = self.p.valid(sign * dist)
+            chip = self.p.other(sign * dist, 1)
+            rel = (sign * dist) % 4
+            for a in range(2):
+                pl.when(here)(functools.partial(self.arrive, a, chip))
+                src = self.slot(a, chip)
+                self.push(a, 14 + rel, src, chip, self.p.dev_b, self.recv.at[a, chip], here)
+                self.push(a, 22 + rel, src, chip, self.p.sibling, self.sib_recv.at[a, chip], here)
+
+    def b_step(self, dist, flip_a):
+        for sign in (-1, 1) if dist else (1,):
+            here = self.p.valid(sign * dist)
+            chip = self.p.other(sign * dist, flip_a, 1)
+            rel = (sign * dist) % 4
+            for a in range(2):
+                pl.when(here)(functools.partial(self.arrive, a, chip))
+                src = self.slot(a, chip)
+                self.push(a, 26 + 4 * flip_a + rel, src, chip, self.p.sibling, self.sib_recv.at[a, chip], here)
+
+    def finish(self):
+        for a in range(2):
+            rows, half = self.piece[a].shape
+
+            def take(chip, carry):
+                slot = self.full[a].at[
+                    pl.ds(pl.multiple_of(chip * rows, rows), rows),
+                    pl.ds(pl.multiple_of((1 - self.p.core) * half, half), half),
+                ]
+                pltpu.make_async_copy(slot, slot, self.sib_recv.at[a, chip]).wait()
+                return carry
+
+            lax.fori_loop(0, 16, take, 0)
+        for copy in self.keep:
+            copy.wait()
+        for copy, cond in self.sent:
+            if cond is None:
+                copy.wait_send()
+            else:
+                pl.when(cond)(copy.wait_send)
+
+
+GATHER_SEMS = [
+    pltpu.SemaphoreType.DMA((2,)),
+    pltpu.SemaphoreType.DMA((2,)),
+    pltpu.SemaphoreType.DMA((2,)),
+    pltpu.SemaphoreType.DMA((2, 34)),
+    pltpu.SemaphoreType.DMA((2, 16)),
+    pltpu.SemaphoreType.DMA((2, 16)),
+]
+
+
+def gather_scratch(shapes):
+    return (
+        [pltpu.VMEM(shape, jnp.float32) for shape in shapes]
+        + [pltpu.VMEM(shape, jnp.bfloat16) for shape in shapes]
+        + GATHER_SEMS
+    )
+
+
+def piece_shapes(shapes):
+    return [(2 * rows, width // 2) for rows, width in shapes]
+
+
+def gather_kernel(layers, *refs):
+    own, refs = refs[: 2 * layers], refs[2 * layers :]
+    full, refs = refs[: 2 * layers], refs[2 * layers :]
+    place = Place()
+    place.greet()
+    jobs = []
+    for layer in range(layers):
+        part = refs[10 * layer : 10 * layer + 10]
+        jobs.append(
+            Gather(place, own[2 * layer : 2 * layer + 2], part[:2], part[2:4], full[2 * layer : 2 * layer + 2], part[4:])
+        )
+    for job in jobs:
+        job.begin()
+        job.a_step(0)
+        for dist in (1, 2, 3):
+            job.z_step(dist)
+            job.a_step(dist)
+    for job in jobs:
+        for dist in range(4):
+            job.b_step(dist, 0)
+            job.b_step(dist, 1)
+    for job in jobs:
+        job.finish()
+
+
+def gather_weights(pairs, collective):
+    flat = [array for pair in pairs for array in pair]
+    devices = lax.axis_size(AXIS)
+    scratch = []
+    for pair in pairs:
+        scratch += gather_scratch(piece_shapes([array.shape for array in pair]))
+    return pl.pallas_call(
+        functools.partial(gather_kernel, len(pairs)),
+        out_shape=[jax.ShapeDtypeStruct((devices * a.shape[0], a.shape[1]), jnp.bfloat16) for a in flat],
+        in_specs=[pl.BlockSpec(memory_space=pltpu.VMEM)] * len(flat),
+        out_specs=[pl.BlockSpec(memory_space=pl.ANY)] * len(flat),
+        scratch_shapes=scratch,
+        compiler_params=pltpu.CompilerParams(
+            collective_id=collective, has_side_effects=True, vmem_limit_bytes=24 << 20
+        ),
+        name="gather_weights",
+    )(*flat)
+
+
+ORDER = (3, 0, 2, 1)
+
+
+class Scatter:
+    def __init__(self, place, grad, total, bufs, sems):
+        self.p, self.grad, self.total = place, grad, total
+        self.mine, self.sib, self.from_b, self.from_a, self.up, self.down, self.part, self.last = (
+            bufs[2 * i : 2 * i + 2] for i in range(8)
+        )
+        (self.load_sem, self.sib_send, self.sib_recv, self.b_send, self.b_recv, self.a_send, self.a_recv, self.up_send,
+         self.up_recv, self.down_send, self.down_recv, self.end_send, self.end_recv, self.end_local) = sems
+
+    def rows_of(self, a, chip, core):
+        _, rows, half = self.mine[a].shape
+        return self.grad[a].at[
+            pl.ds(pl.multiple_of(chip * rows, rows), rows), pl.ds(pl.multiple_of(core * half, half), half)
+        ]
+
+    def chip_of(self, z, flip_a, flip_b):
+        return self.p.other(z - self.p.z, flip_a, flip_b)
+
+    def load(self, a, flip_b, flip_a, z):
+        k = 8 * flip_b + 4 * flip_a + z
+        return pltpu.make_async_copy(
+            self.rows_of(a, self.chip_of(z, flip_a, flip_b), self.p.core), self.mine[a].at[k], self.load_sem.at[a, k]
+        )
+
+    def lend(self, a, flip_b, flip_a, z):
+        k = 8 * flip_b + 4 * flip_a + z
+        return remote(
+            self.rows_of(a, self.chip_of(z, flip_b, flip_a), 1 - self.p.core),
+            self.sib[a].at[k],
+            self.sib_send.at[a, k],
+            self.sib_recv.at[a, k],
+            self.p.sibling,
+        )
+
+    def to_b(self, a, flip_a, z):
+        k = 4 * flip_a + z
+        return remote(
+            self.mine[a].at[8 + k], self.from_b[a].at[k], self.b_send.at[a, k], self.b_recv.at[a, k], self.p.dev_b
+        )
+
+    def to_a(self, a, z):
+        return remote(
+            self.mine[a].at[4 + z], self.from_a[a].at[z], self.a_send.at[a, z], self.a_recv.at[a, z], self.p.dev_a
+        )
+
+    def to_z(self, a, z, sign):
+        dst, send, recv = (
+            (self.up, self.up_send, self.up_recv) if sign > 0 else (self.down, self.down_send, self.down_recv)
+        )
+        return remote(self.mine[a].at[z], dst[a].at[z], send.at[a, z], recv.at[a, z], self.p.me + 8 * sign)
+
+    def each(self, step):
+        def run(z, carry):
+            for a in range(2):
+                step(a, z)
+            return carry
+
+        lax.fori_loop(0, 4, run, 0)
+
+    def begin(self):
+        for z in ORDER:
+            for flip_b, flip_a in ((1, 1), (1, 0), (0, 1), (0, 0)):
+                for a in range(2):
+                    self.lend(a, flip_b, flip_a, z).start()
+                    self.load(a, flip_b, flip_a, z).start()
+
+    def pair(self, a, flip_b, flip_a, z):
+        k = 8 * flip_b + 4 * flip_a + z
+        self.load(a, flip_b, flip_a, z).wait()
+        self.lend(a, flip_b, flip_a, z).wait_recv()
+        return self.mine[a][k].astype(jnp.float32) + self.sib[a][k].astype(jnp.float32)
+
+    def cross_b(self, z):
+        for flip_a in (1, 0):
+            for a in range(2):
+                self.mine[a][8 + 4 * flip_a + z] = self.pair(a, 1, flip_a, z).astype(jnp.bfloat16)
+                self.to_b(a, flip_a, z).start()
+
+    def cross_a(self, z):
+        for a in range(2):
+            value = self.pair(a, 0, 1, z)
+            self.to_b(a, 1, z).wait_recv()
+            self.mine[a][4 + z] = (value + self.from_b[a][4 + z].astype(jnp.float32)).astype(jnp.bfloat16)
+            self.to_a(a, z).start()
+
+    def along_z(self, z):
+        place = self.p
+        for a in range(2):
+            value = self.pair(a, 0, 0, z)
+            self.to_b(a, 0, z).wait_recv()
+            value = value + self.from_b[a][z].astype(jnp.float32)
+            self.to_a(a, z).wait_recv()
+            self.part[a][...] = value + self.from_a[a][z].astype(jnp.float32)
+
+            @pl.when(jnp.logical_and(place.z < z, place.z > 0))
+            def _():
+                self.to_z(a, z, 1).wait_recv()
+                self.part[a][...] += self.up[a][z].astype(jnp.float32)
+
+            @pl.when(jnp.logical_and(place.z > z, place.z < 3))
+            def _():
+                self.to_z(a, z, -1).wait_recv()
+                self.part[a][...] += self.down[a][z].astype(jnp.float32)
+
+            @pl.when(place.z != z)
+            def _():
+                self.mine[a][z] = self.part[a][...].astype(jnp.bfloat16)
+
+            @pl.when(place.z < z)
+            def _():
+                self.to_z(a, z, 1).start()
+
+            @pl.when(place.z > z)
+            def _():
+                self.to_z(a, z, -1).start()
+
+            @pl.when(place.z == z)
+            def _():
+                self.last[a][...] = self.part[a][...]
+
+    def end_copies(self, a):
+        core = self.p.core
+        rows, width = self.total[a].shape
+        dst = self.total[a].at[:, pl.ds(pl.multiple_of(core * (width // 2), width // 2), width // 2)]
+        away = remote(
+            self.last[a].at[pl.ds(pl.multiple_of((1 - core) * rows, 8), rows), :],
+            dst,
+            self.end_send.at[a],
+            self.end_recv.at[a],
+            self.p.sibling,
+        )
+        keep = pltpu.make_async_copy(
+            self.last[a].at[pl.ds(pl.multiple_of(core * rows, 8), rows), :], dst, self.end_local.at[a]
+        )
+        return away, keep
+
+    def close(self):
+        place = self.p
+        for a in range(2):
+
+            @pl.when(place.z > 0)
+            def _():
+                self.to_z(a, place.z, 1).wait_recv()
+                self.last[a][...] += self.up[a][place.z].astype(jnp.float32)
+
+            @pl.when(place.z < 3)
+            def _():
+                self.to_z(a, place.z, -1).wait_recv()
+                self.last[a][...] += self.down[a][place.z].astype(jnp.float32)
+
+            for copy in self.end_copies(a):
+                copy.start()
+
+    def finish(self):
+        for a in range(2):
+            for copy in self.end_copies(a):
+                copy.wait()
+
+        def step(a, z):
+            for flip_b in range(2):
+                for flip_a in range(2):
+                    self.lend(a, flip_b, flip_a, z).wait_send()
+            for flip_a in range(2):
+                self.to_b(a, flip_a, z).wait_send()
+            self.to_a(a, z).wait_send()
+
+            @pl.when(self.p.z < z)
+            def _():
+                self.to_z(a, z, 1).wait_send()
+
+            @pl.when(self.p.z > z)
+            def _():
+                self.to_z(a, z, -1).wait_send()
+
+        self.each(step)
+
+    def steps(self):
+        yield self.begin
+        for k in range(6):
+            if k < 4:
+                yield functools.partial(self.cross_b, ORDER[k])
+            if 0 <= k - 1 < 4:
+                yield functools.partial(self.cross_a, ORDER[k - 1])
+            if 0 <= k - 2 < 4:
+                yield functools.partial(self.along_z, ORDER[k - 2])
+        yield self.close
+        yield self.finish
+
+
+def scatter_scratch(shapes):
+    scratch = []
+    for count, kind in ((16, jnp.bfloat16), (16, jnp.bfloat16), (8, jnp.bfloat16), (4, jnp.bfloat16), (4, jnp.bfloat16),
+                        (4, jnp.bfloat16), (0, jnp.float32), (0, jnp.float32)):
+        scratch += [pltpu.VMEM(((count,) if count else ()) + shape, kind) for shape in shapes]
+    counts = (16, 16, 16, 8, 8, 4, 4, 4, 4, 4, 4)
+    return scratch + [pltpu.SemaphoreType.DMA((2, n)) for n in counts] + [pltpu.SemaphoreType.DMA((2,))] * 3
+
+
+def scatter_kernel(*refs):
+    grad, total, bufs, sems = refs[:2], refs[2:4], refs[4:20], refs[20:]
+    place = Place()
+    place.greet()
+    for step in Scatter(place, grad, total, bufs, sems).steps():
+        step()
+
+
+def scatter_grads(grads, collective):
+    devices = lax.axis_size(AXIS)
+    shapes = [(a.shape[0] // devices, a.shape[1]) for a in grads]
+    return pl.pallas_call(
+        scatter_kernel,
+        out_shape=[jax.ShapeDtypeStruct(shape, jnp.float32) for shape in shapes],
+        in_specs=[pl.BlockSpec(memory_space=pl.ANY)] * 2,
+        out_specs=[pl.BlockSpec(memory_space=pltpu.VMEM)] * 2,
+        scratch_shapes=scatter_scratch(piece_shapes(shapes)),
+        compiler_params=pltpu.CompilerParams(
+            collective_id=collective, has_side_effects=True, vmem_limit_bytes=40 << 20
+        ),
+        name="scatter_grads",
+    )(*grads)
+
+
+def dot_nt(left, right):
+    return lax.dot_general(left, right, (((1,), (1,)), ((), ())), preferred_element_type=jnp.float32)
+
+
+def dot_tn(left, right):
+    return lax.dot_general(left, right, (((0,), (0,)), ((), ())), preferred_element_type=jnp.float32)
+
+
+def thirds(value):
+    high = value.astype(jnp.bfloat16)
+    rest = value - high.astype(jnp.float32)
+    mid = rest.astype(jnp.bfloat16)
+    return high, mid, (rest - mid.astype(jnp.float32)).astype(jnp.bfloat16)
+
+
+def silu_slope(value):
+    gate = jax.nn.sigmoid(value)
+    return gate * (1 + value * (1 - gate))
+
+
+class Swap:
+    def __init__(self, me, devices, index, src_of, dst, send, recv):
+        self.me, self.n, self.i, self.src_of, self.dst, self.send, self.recv = me, devices, index, src_of, dst, send, recv
+
+    def copy(self, peer, slot):
+        return remote(self.src_of(peer), self.dst.at[slot], self.send.at[self.i, peer], self.recv.at[self.i, slot], peer)
+
+    def each(self, step):
+        def run(k, carry):
+            step(lax.rem(self.me + k, self.n))
+            return carry
+
+        lax.fori_loop(1, self.n, run, 0)
+
+    def start(self):
+        self.each(lambda peer: self.copy(peer, self.me).start())
+
+    def arrive(self):
+        self.each(lambda peer: self.copy(peer, peer).wait_recv())
+
+    def sent(self):
+        self.each(lambda peer: self.copy(peer, self.me).wait_send())
+
+
+def greet_all(devices):
+    barrier = pltpu.get_barrier_semaphore()
+    me = lax.axis_index(AXIS)
+
+    def hello(k, carry):
+        pl.semaphore_signal(barrier, inc=1, device_id=(lax.rem(me + k, devices),), device_id_type=MESH_ID)
+        return carry
+
+    lax.fori_loop(1, devices, hello, 0)
+    pl.semaphore_wait(barrier, devices - 1)
+
+
+def modulate_steps(devices, ins, outs, bufs, sems):
+    msg, wt1, wt2, wcls, wcond, bt1, bt2, bcond = ins
+    mods, pre, cond, hid_all, low_all, feat_all, lab_all, got = outs
+    hid, low, away = bufs
+    me = lax.axis_index(AXIS)
+    images, cols = 4, wt1.shape[0]
+    swaps = [
+        Swap(me, devices, 0, lambda peer: msg, got, *sems),
+        Swap(me, devices, 1, lambda peer: hid.at[me], hid, *sems),
+        Swap(me, devices, 2, lambda peer: low.at[me], low, *sems),
+        Swap(me, devices, 3, lambda peer: away.at[peer], mods, *sems),
+    ]
+
+    def first():
+        swaps[0].start()
+        got[me] = msg[...]
+
+    def second():
+        swaps[0].arrive()
+        for j in range(devices):
+            feat_all[images * j : images * (j + 1), :] = got[j, :, :FREQ]
+            lab_all[images * j : images * (j + 1), :] = got[j, :, FREQ : FREQ + 128]
+        pre[...] = dot_nt(wt1[...].astype(jnp.bfloat16), feat_all[...].astype(jnp.bfloat16)) + bt1[...]
+        hidden = silu(pre[...])
+        pad = jnp.zeros((hid.shape[1] - cols, hidden.shape[1]), jnp.float32)
+        hid[me] = jnp.concatenate([hidden, pad], 0).astype(jnp.bfloat16)
+        swaps[1].start()
+        classes = lax.broadcasted_iota(jnp.int32, (lab_all.shape[0], wcls.shape[1]), 1).astype(jnp.float32)
+        labels = jnp.concatenate([lab_all[...]] * (wcls.shape[1] // 128), 1)
+        onehot = (labels == classes).astype(jnp.bfloat16)
+        cond[...] = dot_nt(wcls[...].astype(jnp.bfloat16), onehot) + bt2[...]
+
+    def third():
+        swaps[1].arrive()
+        for j in range(devices):
+            hid_all[cols * j : cols * (j + 1), :] = hid[j].astype(jnp.float32)[:cols]
+        cond[...] += jnp.dot(
+            wt2[...].astype(jnp.bfloat16), hid_all[...].astype(jnp.bfloat16), preferred_element_type=jnp.float32
+        )
+        value = silu(cond[...])
+        pad = jnp.zeros((low.shape[1] - cols, value.shape[1]), jnp.float32)
+        low[me] = jnp.concatenate([value, pad], 0).astype(jnp.bfloat16)
+        swaps[2].start()
+
+    def fourth():
+        swaps[2].arrive()
+        for j in range(devices):
+            low_all[cols * j : cols * (j + 1), :] = low[j].astype(jnp.float32)[:cols]
+        rows = dot_nt(low_all[...].T.astype(jnp.bfloat16), wcond[...].astype(jnp.bfloat16)) + bcond[...]
+        for j in range(devices):
+            away[j] = rows[images * j : images * (j + 1)]
+        swaps[3].start()
+        mods[me] = away[me]
+
+    def last():
+        swaps[3].arrive()
+        for swap in swaps:
+            swap.sent()
+
+    return [first, second, third, fourth, last]
+
+
+def modulate_kernel(devices, *refs):
+    greet_all(devices)
+    for step in modulate_steps(devices, refs[:8], refs[8:16], refs[16:19], refs[19:]):
+        step()
+
+
+def modulate(ins):
+    devices = lax.axis_size(AXIS)
+    msg, wt1, wt2, wcls, wcond = ins[:5]
+    cols, images = wt1.shape[0], devices * msg.shape[0]
+    outs = [
+        (devices, msg.shape[0], wcond.shape[0]), (cols, images), (cols, images), (devices * cols, images),
+        (devices * cols, images), (images, FREQ), (images, 128), (devices,) + msg.shape,
+    ]
+    padded = -(-cols // 16) * 16
+    return pl.pallas_call(
+        functools.partial(modulate_kernel, devices),
+        out_shape=[jax.ShapeDtypeStruct(shape, jnp.float32) for shape in outs],
+        in_specs=[pl.BlockSpec(memory_space=pltpu.VMEM)] * 8,
+        out_specs=[pl.BlockSpec(memory_space=pltpu.VMEM)] * 8,
+        scratch_shapes=[
+            pltpu.VMEM((devices, padded, images), jnp.bfloat16),
+            pltpu.VMEM((devices, padded, images), jnp.bfloat16),
+            pltpu.VMEM((devices, msg.shape[0], wcond.shape[0]), jnp.float32),
+            pltpu.SemaphoreType.DMA((4, devices)),
+            pltpu.SemaphoreType.DMA((4, devices)),
+        ],
+        compiler_params=pltpu.CompilerParams(collective_id=3, has_side_effects=True, vmem_limit_bytes=24 << 20),
+        name="modulate",
+    )(*ins)
+
+
+def settle_steps(devices, ins, outs, bufs, sems):
+    d_mods, small, wt2, wcond, pre, cond, hid_all, low_all, feat_all, lab_all, squares = ins
+    g_cond, g_t1, g_t2, g_cls, merged = outs
+    dm_got, dm_all, small_got, dc_part, dc_got, dh_part, dh_got, note = bufs
+    me = lax.axis_index(AXIS)
+    images, cols = d_mods.shape[1], wt2.shape[0]
+    width = d_mods.shape[2]
+
+    def rows_for(ref):
+        return lambda peer: ref.at[pl.ds(pl.multiple_of(peer * cols, 8), cols), :]
+
+    swaps = [
+        Swap(me, devices, 0, lambda peer: d_mods.at[peer], dm_got, *sems),
+        Swap(me, devices, 1, lambda peer: small.at[peer], small_got, *sems),
+        Swap(me, devices, 2, rows_for(dc_part), dc_got, *sems),
+        Swap(me, devices, 3, rows_for(dh_part), dh_got, *sems),
+        Swap(me, devices, 4, lambda peer: note, merged, *sems),
+    ]
+    keep = {}
+
+    def first():
+        swaps[0].start()
+        swaps[1].start()
+        dm_got[me] = d_mods[me]
+        small_got[me] = small[me]
+        dm_all[...] = jnp.zeros_like(dm_all)
+
+    def second():
+        swaps[0].arrive()
+        for j in range(devices):
+            dm_all[images * j : images * (j + 1), :width] = dm_got[j]
+        turned = dm_all[...].T[:width]
+        parts = thirds(turned)
+        weight = wcond[...].astype(jnp.bfloat16)
+        dc_part[...] = sum(dot_tn(weight, part) for part in parts)
+        swaps[2].start()
+        mine = pl.ds(pl.multiple_of(me * cols, 8), cols)
+        dc_got[me] = dc_part[mine, :]
+        low = low_all[...].astype(jnp.bfloat16)
+        g_cond[...] = sum(dot_nt(part, low) for part in parts)
+        swaps[1].arrive()
+
+    def third():
+        swaps[2].arrive()
+        d_cond = jnp.sum(dc_got[...], 0) * silu_slope(cond[...])
+        parts = thirds(d_cond)
+        weight = wt2[...].astype(jnp.bfloat16)
+        dh_part[...] = sum(dot_tn(weight, part) for part in parts)
+        swaps[3].start()
+        mine = pl.ds(pl.multiple_of(me * cols, 8), cols)
+        dh_got[me] = dh_part[mine, :]
+        classes = lax.broadcasted_iota(jnp.int32, (lab_all.shape[0], g_cls.shape[1]), 1).astype(jnp.float32)
+        labels = jnp.concatenate([lab_all[...]] * (g_cls.shape[1] // 128), 1)
+        onehot = (labels == classes).astype(jnp.bfloat16)
+        g_cls[...] = sum(jnp.dot(part, onehot, preferred_element_type=jnp.float32) for part in parts)
+        hidden = hid_all[...].astype(jnp.bfloat16)
+        g_t2[...] = sum(dot_nt(part, hidden) for part in parts)
+        ones = jnp.ones((8, lab_all.shape[0]), jnp.bfloat16)
+        keep["t2"] = sum(dot_nt(ones, part) for part in parts)
+
+    def fourth():
+        swaps[3].arrive()
+        d_pre = jnp.sum(dh_got[...], 0) * silu_slope(pre[...])
+        parts = thirds(d_pre)
+        feats = feat_all[...].astype(jnp.bfloat16)
+        g_t1[...] = sum(jnp.dot(part, feats, preferred_element_type=jnp.float32) for part in parts)
+        ones = jnp.ones((8, lab_all.shape[0]), jnp.bfloat16)
+        bias_t1 = sum(dot_nt(ones, part) for part in parts)
+        total = squares[...]
+        for ref in (g_cond, g_t1, g_t2, g_cls):
+            total = total + jnp.sum(ref[...] * ref[...])
+        bias_cond = jnp.sum(dm_all[...], 0, keepdims=True)
+        note[...] = jnp.zeros_like(note)
+        note[0:16, :] = jnp.sum(small_got[...], 0)
+        note[16:17, :] = total
+        note[17:18, :cols] = bias_t1[0:1]
+        note[18:19, :cols] = keep["t2"][0:1]
+        for k in range(3):
+            note[19 + k : 20 + k, :] = bias_cond[:, 128 * k : 128 * (k + 1)]
+        swaps[4].start()
+        merged[me] = note[...]
+
+    def last():
+        swaps[4].arrive()
+        for swap in swaps:
+            swap.sent()
+
+    return [first, second, third, fourth, last]
+
+
+def settle_kernel(devices, *refs):
+    greet_all(devices)
+    for step in settle_steps(devices, refs[:11], refs[11:16], refs[16:24], refs[24:]):
+        step()
+
+
+def settle(ins):
+    devices = lax.axis_size(AXIS)
+    d_mods, small, wt2, wcond, pre = ins[:5]
+    cols, images = pre.shape
+    outs = [(wcond.shape[0], devices * cols), (cols, FREQ), (cols, devices * cols), (cols, 1024), (devices, 24, 128)]
+    return pl.pallas_call(
+        functools.partial(settle_kernel, devices),
+        out_shape=[jax.ShapeDtypeStruct(shape, jnp.float32) for shape in outs],
+        in_specs=[pl.BlockSpec(memory_space=pltpu.VMEM)] * 11,
+        out_specs=[pl.BlockSpec(memory_space=pltpu.VMEM)] * 5,
+        scratch_shapes=[
+            pltpu.VMEM(d_mods.shape, jnp.float32),
+            pltpu.VMEM((images, 384), jnp.float32),
+            pltpu.VMEM(small.shape, jnp.float32),
+            pltpu.VMEM((devices * cols, images), jnp.float32),
+            pltpu.VMEM((devices, cols, images), jnp.float32),
+            pltpu.VMEM((devices * cols, images), jnp.float32),
+            pltpu.VMEM((devices, cols, images), jnp.float32),
+            pltpu.VMEM((24, 128), jnp.float32),
+            pltpu.SemaphoreType.DMA((5, devices)),
+            pltpu.SemaphoreType.DMA((5, devices)),
+        ],
+        compiler_params=pltpu.CompilerParams(collective_id=4, has_side_effects=True, vmem_limit_bytes=24 << 20),
+        name="settle",
+    )(*ins)
+
+def code_table():
+    quarter = MODEL_WIDTH // 4
+    omega = (1.0 / 10000.0 ** (np.arange(quarter, dtype=np.float32) / np.float32(quarter))).astype(np.float32)
+    angles = np.arange(GRID, dtype=np.float32)[:, None] * omega
+    return np.concatenate([np.sin(angles), np.cos(angles)], 1).astype(np.float32)
+
+
+def position_sum():
+    table = jnp.asarray(code_table())
+    half = MODEL_WIDTH // 2
+    rows_pos = jnp.broadcast_to(table[:, None, :], (GRID, GRID, half))
+    cols_pos = jnp.broadcast_to(table[None, :, :], (GRID, GRID, half))
+    return jnp.concatenate([rows_pos, cols_pos], -1).reshape(SEQ, MODEL_WIDTH)
+
+
+def rows_t(left, right):
+    return jnp.einsum("bsd,ed->bse", left, right, preferred_element_type=jnp.float32)
+
+
+def back_t(left, right):
+    return jnp.einsum("bse,ed->bsd", left, right, preferred_element_type=jnp.float32)
+
+
+def outer_t(left, right):
+    return jnp.einsum("bsd,bse->ed", left, right, preferred_element_type=jnp.float32).astype(jnp.bfloat16)
+
+
+def forward_t(x, mod, w_in, w_out, bias_in, bias_out):
+    pieces = [mod[:, None, i * MODEL_WIDTH : (i + 1) * MODEL_WIDTH] for i in range(6)]
+    shaped_one = (layer_norm(x) * (1 + pieces[1]) + pieces[0]).astype(jnp.bfloat16)
+    triple = (rows_t(shaped_one, w_in[: 3 * MODEL_WIDTH]) + bias_in[: 3 * MODEL_WIDTH]).astype(jnp.bfloat16)
+    mixed_heads, log_norm = attend(triple)
+    branch = rows_t(mixed_heads, w_out[:, :MODEL_WIDTH]) + bias_out[:MODEL_WIDTH]
+    middle = x + pieces[2] * branch
+    shaped_two = (layer_norm(middle) * (1 + pieces[4]) + pieces[3]).astype(jnp.bfloat16)
+    pre_ffn = rows_t(shaped_two, w_in[3 * MODEL_WIDTH :]) + bias_in[3 * MODEL_WIDTH :]
+    active = gelu(pre_ffn).astype(jnp.bfloat16)
+    ffn_out = rows_t(active, w_out[:, MODEL_WIDTH:]) + bias_out[MODEL_WIDTH:]
+    kept = (x, shaped_one, triple, log_norm, mixed_heads, branch, middle, shaped_two, pre_ffn, active, ffn_out)
+    return middle + pieces[5] * ffn_out, kept
+
+
+def backward_t(upstream, mod, w_in, w_out, kept):
+    x, shaped_one, triple, log_norm, mixed_heads, branch, middle, shaped_two, pre_ffn, active, ffn_out = kept
+    pieces = [mod[:, None, i * MODEL_WIDTH : (i + 1) * MODEL_WIDTH] for i in range(6)]
+    d_ffn = (pieces[5] * upstream).astype(jnp.bfloat16)
+    gate_two = jnp.sum(ffn_out * upstream, 1)
+    grad_down = outer_t(active, d_ffn)
+    d_active = back_t(d_ffn, w_out[:, MODEL_WIDTH:])
+    d_pre = local_back(gelu, pre_ffn, d_active).astype(jnp.bfloat16)
+    grad_up = outer_t(shaped_two, d_pre)
+    d_shaped = back_t(d_pre, w_in[3 * MODEL_WIDTH :])
+    shift_two = jnp.sum(d_shaped, 1)
+    scale_two = jnp.sum(d_shaped * layer_norm(middle), 1)
+    upstream = upstream + local_back(layer_norm, middle, d_shaped * (1 + pieces[4]))
+    gate_one = jnp.sum(branch * upstream, 1)
+    d_branch = (pieces[2] * upstream).astype(jnp.bfloat16)
+    grad_proj = outer_t(mixed_heads, d_branch)
+    d_mixed = back_t(d_branch, w_out[:, :MODEL_WIDTH]).astype(jnp.bfloat16)
+    d_triple = attend_back(triple, log_norm, d_mixed)
+    grad_qkv = outer_t(shaped_one, d_triple)
+    d_shaped = back_t(d_triple, w_in[: 3 * MODEL_WIDTH])
+    shift_one = jnp.sum(d_shaped, 1)
+    scale_one = jnp.sum(d_shaped * layer_norm(x), 1)
+    upstream = upstream + local_back(layer_norm, x, d_shaped * (1 + pieces[1]))
+    mod_grad = jnp.concatenate([shift_one, scale_one, gate_one, shift_two, scale_two, gate_two], 1)
+    bias_in_grad = jnp.concatenate([column_sum(d_triple), column_sum(d_pre)])
+    bias_out_grad = jnp.concatenate([column_sum(d_branch), column_sum(d_ffn)])
+    grad_in = jnp.concatenate([grad_qkv, grad_up], 0)
+    grad_out = jnp.concatenate([grad_proj, grad_down], 1)
+    return upstream, mod_grad, grad_in, grad_out, bias_in_grad, bias_out_grad
+
+
+def body(
+    latents, targets, timesteps, labels, embed_w, embed_m, embed_v, cond_w, cond_m, cond_v, layer_input_weights, in_m,
+    in_v, layer_output_weights, out_m, out_v, head_w, head_m, head_v, biases, bias_m, bias_v,
+):
+    devices = lax.axis_size("fsdp")
+    me = lax.axis_index("fsdp")
+    images = latents.shape[0]
+    embed_t = embed_w.T
+    cond_t = cond_w.T
+    in_t = layer_input_weights.transpose(0, 2, 1)
+    out_t = layer_output_weights.transpose(0, 2, 1)
+    cols, cond_cols = embed_t.shape[0], cond_t.shape[0]
+    time_one, time_two, patch_bias, cond_bias, block_input_bias, block_output_bias, head_bias = split_biases(biases)
+    fulls = gather_weights([(in_t[i], out_t[i]) for i in range(LAYERS)], 1)
+    w_in = [fulls[2 * i] for i in range(LAYERS)]
+    w_out = [fulls[2 * i + 1] for i in range(LAYERS)]
+    features = time_features(timesteps).astype(jnp.bfloat16).astype(jnp.float32)
+    label_rows = jnp.broadcast_to(labels.astype(jnp.float32)[:, None], (images, 128))
+    own_patch_w = embed_t[:, FREQ + MODEL_WIDTH : FREQ + MODEL_WIDTH + PD].reshape(3, 128)
+    note = jnp.concatenate([features, label_rows, jnp.pad(own_patch_w, ((0, images - 3), (0, 0)))], 1)
+    w_t1 = embed_t[:, :FREQ]
+    w_t2 = embed_t[:, FREQ : FREQ + MODEL_WIDTH]
+    w_class = jnp.pad(embed_t[:, FREQ + MODEL_WIDTH + PD :], ((0, 0), (0, 1024 - NCLS)))
+    images_all = devices * images
+
+    def own_bias(vector, count):
+        part = lax.dynamic_slice(vector, (me * count,), (count,))
+        return jnp.broadcast_to(part[:, None], (count, images_all))
+
+    own_cond_bias = lax.dynamic_slice(cond_bias, (me * cond_cols,), (cond_cols,))[None]
+    mods, pre, cond, hid_all, low_all, feat_all, lab_all, notes = modulate(
+        [note, w_t1, w_t2, w_class, cond_t, own_bias(time_one, cols), own_bias(time_two, cols), own_cond_bias]
+    )
+    modulation = mods.transpose(1, 0, 2).reshape(images, CW)
+    w_patch = notes[:, :3, FREQ + 128 :].reshape(MODEL_WIDTH, PD).astype(jnp.bfloat16)
+    head_low = head_w.astype(jnp.bfloat16)
+    x = rows_t(latents, w_patch) + patch_bias + position_sum()
+    kept_all = []
+    for i in range(LAYERS):
+        mod = modulation[:, 6 * MODEL_WIDTH * i : 6 * MODEL_WIDTH * (i + 1)]
+        x, kept = forward_t(x, mod, w_in[i], w_out[i], block_input_bias[i], block_output_bias[i])
+        kept_all.append(kept)
+    final_mod = modulation[:, 6 * MODEL_WIDTH * LAYERS :]
+    norm_final = layer_norm(x)
+    shaped = (norm_final * (1 + final_mod[:, None, MODEL_WIDTH:]) + final_mod[:, None, :MODEL_WIDTH]).astype(jnp.bfloat16)
+    output = apply_rows(shaped, head_low) + head_bias
+    error_vals = output - targets
+    loss_part = jnp.sum(error_vals * error_vals)
+    tokens_all = devices * images * SEQ * PO
+    d_output = (error_vals * (2.0 / tokens_all)).astype(jnp.bfloat16)
+    head_grad = outer_sum(shaped, d_output)
+    head_bias_grad = column_sum(d_output)
+    d_shaped = apply_back(d_output, head_low)
+    d_final = jnp.concatenate([jnp.sum(d_shaped, 1), jnp.sum(d_shaped * norm_final, 1)], 1)
+    upstream = local_back(layer_norm, x, d_shaped * (1 + final_mod[:, None, MODEL_WIDTH:]))
+    mod_grads, in_shards, out_shards = [None] * LAYERS, [None] * LAYERS, [None] * LAYERS
+    in_bias_grads, out_bias_grads = [None] * LAYERS, [None] * LAYERS
+    for i in reversed(range(LAYERS)):
+        mod = modulation[:, 6 * MODEL_WIDTH * i : 6 * MODEL_WIDTH * (i + 1)]
+        upstream, mod_grads[i], grad_in, grad_out, in_bias_grads[i], out_bias_grads[i] = backward_t(
+            upstream, mod, w_in[i], w_out[i], kept_all[i]
+        )
+        in_shards[i], out_shards[i] = scatter_grads([grad_in, grad_out], 5 + i)
+    d_patch = upstream.astype(jnp.bfloat16)
+    patch_grad = outer_sum(latents, d_patch)
+    patch_bias_grad = column_sum(d_patch)
+    d_modulation = jnp.concatenate(mod_grads + [d_final], 1)
+    d_mods = d_modulation.reshape(images, devices, cond_cols).transpose(1, 0, 2)
+    small = jnp.concatenate(
+        [head_grad.reshape(-1), patch_grad.reshape(-1), patch_bias_grad] + in_bias_grads + out_bias_grads
+        + [head_bias_grad, loss_part[None]]
+    )
+    small = jnp.pad(small, (0, devices * 2048 - small.shape[0])).reshape(devices, 16, 128)
+    squares = sum(jnp.sum(shard * shard) for shard in in_shards + out_shards)
+    g_cond, g_t1, g_t2, g_cls, merged = settle(
+        [d_mods, small, w_t2, cond_t, pre, cond, hid_all, low_all, feat_all, lab_all, jnp.full((1, 128), squares)]
+    )
+    flat = merged[:, :16].reshape(-1)
+    sizes = [MODEL_WIDTH * PO, PD * MODEL_WIDTH, MODEL_WIDTH, LAYERS * IW, LAYERS * 2 * MODEL_WIDTH, PO, 1]
+    places = [sum(sizes[:k]) for k in range(len(sizes) + 1)]
+    head_total = flat[: places[1]].reshape(MODEL_WIDTH, PO)
+    patch_total = flat[places[1] : places[2]].reshape(PD, MODEL_WIDTH)
+    loss_total = flat[places[6]]
+    bias_total = jnp.concatenate(
+        [merged[:, 17, :cols].reshape(-1), merged[:, 18, :cols].reshape(-1), flat[places[2] : places[3]],
+         merged[:, 19:22].reshape(devices, 384)[:, :cond_cols].reshape(-1), flat[places[3] : places[6]]]
+    )
+    grad_norm = jnp.sqrt(
+        jnp.sum(merged[:, 16, 0])
+        + jnp.sum(head_total * head_total)
+        + jnp.sum(patch_total * patch_total)
+        + jnp.sum(bias_total * bias_total)
+    )
+    factor = jnp.minimum(1.0, clip_limit / grad_norm)
+    own_patch = lax.dynamic_slice(patch_total, (0, me * cols), (PD, cols)).T
+    embed_grad = jnp.concatenate([g_t1, g_t2, own_patch, g_cls[:, :NCLS]], 1)
+    embed_up = [a.T for a in adam_step(embed_t, embed_m.T, embed_v.T, embed_grad * factor)]
+    cond_up = [a.T for a in adam_step(cond_t, cond_m.T, cond_v.T, g_cond * factor)]
+    turn = (0, 2, 1)
+    in_up = [
+        a.transpose(turn)
+        for a in adam_step(in_t, in_m.transpose(turn), in_v.transpose(turn), jnp.stack(in_shards) * factor)
+    ]
+    out_up = [
+        a.transpose(turn)
+        for a in adam_step(out_t, out_m.transpose(turn), out_v.transpose(turn), jnp.stack(out_shards) * factor)
+    ]
+    head_up = adam_step(head_w, head_m, head_v, head_total * factor)
+    bias_up = adam_step(biases, bias_m, bias_v, bias_total * factor)
+    return (loss_total, grad_norm, *embed_up, *cond_up, *in_up, *out_up, *head_up, *bias_up)
+
+
+def fits(mesh):
+    return mesh.shape["fsdp"] == 32
+
+
 def solution(mesh):
     in_specs = (
         P("fsdp", None, None),
@@ -477,4 +1399,5 @@
         P(),
         P(),
     )
-    return jax.shard_map(body, mesh=mesh, in_specs=in_specs, out_specs=out_specs, check_vma=False)
+    chosen = body if fits(mesh) else generic_body
+    return jax.shard_map(chosen, mesh=mesh, in_specs=in_specs, out_specs=out_specs, check_vma=False)

time: 2060 us -> 937 us (0.45)
  waiting for transfers between devices: 1410 us -> 0 us
  Pallas kernels: 0 us -> 373 us
  blocking collectives: 40.4 us -> 0 us
  matrix products: 314 us -> 283 us
  local copies, waits for them, and re-layouts: 159 us -> 138 us
    unnamed x18 -> x0, waiting for transfers between devices: 751 us -> none
    pallas_call x0 -> x5, Pallas kernels: none -> 373 us  [the longest x2 158 us: scatter_grads(): pl.pallas_call(scatter_kernel, out_shape=[jax.ShapeDtypeStruct(shape, jnp...]
    all_gather x6 -> x0, waiting for transfers between devices: 338 us -> none  [the longest x2 140 us: fetch_layer(): lax.all_gather(layer_input_weights[layer_count].astype(jnp.bfloat16), 'fs...]
    reduce_scatter x1 -> x0, waiting for transfers between devices: 323 us -> none  [body(): lax.psum_scatter(cond_grad, 'fsdp', scatter_dimension=1, tiled=True)]
    dot_general x10 -> x26, matrix products: 43.6 us -> 207 us  [the longest x8 81.2 us: back_t(): jnp.einsum('bse,ed->bsd', left, right, preferred_element_type=jnp.float32)]
    dot_general x9 -> x1, matrix products: 73.2 us -> 2.93 us  [apply_back(): jnp.einsum('bse,de->bsd', left, right, preferred_element_type=jnp.float32)]
    dot_general x10 -> x1, matrix products: 70.9 us -> 1.64 us  [apply_rows(): jnp.einsum('bsd,de->bse', left, right, preferred_element_type=jnp.float32)]
    dot_general x10 -> x2, matrix products: 65.2 us -> 2.91 us  [outer_sum(): jnp.einsum('bsd,bse->de', left, right, preferred_element_type=jnp.float32)]
  transfers between devices with their start and end apart: 13 -> 0, of which waited for: 12 -> 0; matrix products, arithmetic and copies ran while one was open for 16% -> 0% of each run, Pallas kernels for 0% -> 0%
where the time goes in v1:
time: 937 us; the launch traced here: 924 us
  Pallas kernels  373 us (40%)
  matrix products  283 us (30%)
  local copies, waits for them, and re-layouts  138 us (15%)
  other arithmetic  121 us (13%)
    pallas_call x2, Pallas kernels, scatter_grads(): pl.pallas_call(scatter_kernel, out_shape=[jax.ShapeDtypeStruct(shape, jnp...  158 us
    pallas_call x1, Pallas kernels, gather_weights(): pl.pallas_call(functools.partial(gather_kernel, len(pairs)), out_shape=[j...  123 us
    dot_general x8, matrix products, back_t(): jnp.einsum('bse,ed->bsd', left, right, preferred_element_type=jnp.float32)  81.2 us
    dot_general x9, matrix products, rows_t(): jnp.einsum('bsd,ed->bse', left, right, preferred_element_type=jnp.float32)  61.9 us
    dot_general x8, matrix products, outer_t(): jnp.einsum('bsd,bse->ed', left, right, preferred_element_type=jnp.float32)  56.1 us
    pallas_call x1, Pallas kernels, settle(): pl.pallas_call(functools.partial(settle_kernel, devices), out_shape=[jax....  51.5 us
    unnamed x351, local copies, waits for them, and re-layouts  44.7 us
    pallas_call x1, Pallas kernels, modulate(): pl.pallas_call(functools.partial(modulate_kernel, devices), out_shape=[ja...  40.3 us

profile of v1, /device:TPU:0, one launch (start us, length us, event | category | flops | bytes accessed | tf_op | source)
XLA Modules:
  0.0 923.9 jit_solution(18046033845464750929)
XLA Ops:
  16.8 40.3 %modulate.1 = (f32[32,4,336]{2,1,0:T(4,128)S(1)}, f32[24,128]{1,0:T(8,128)S(1)}, f32[24,128]{1,0:T(8,128)S(1)}, f32[768,128]{1,0:T(8,128)S(1)}, f32[768,128]{1,0...) custom-call(f32[4,512]{1,0:T(4,128)S(1)} %select_maximum_fusion.refs_0_, ...), custom_call_target="tpu_custom_call" | custom-call | tf_op jit(solution)/shard_map/modulate/pallas_call | solution.py:1027
  64.0 123.1 %gather_weights.1 = (bf16[5376,768]{1,0:T(8,128)(2,1)S(1)}, bf16[768,3840]{1,0:T(8,128)(2,1)S(1)}, bf16[5376,768]{1,0:T(8,128)(2,1)S(1)}, bf16[768,3840]{1,0:T(8,128)(2,1)S(1)}) custom-call(f32[168,768]{1,0:T(8,128)S(1)} %get-tuple-element.145.refs_0_, f32[24,3840]{1,0:T(8,128)S(1)} %get-tuple-element.147.refs_1_, ...), custom_call_target="tpu_custom_call" | custom-call | tf_op jit(solution)/shard_map/gather_weights/pallas_call | solution.py:656
  187.1 3.2 copy-done.22
  192.8 5.2 add_convert_fusion.1
  208.3 8.3 multiply_reduce_fusion.3
  216.6 7.1 fusion.14
  224.4 7.4 fusion.69
  232.0 3.1 fusion.131
  238.2 9.0 fusion.42
  247.2 10.5 %fusion.130 = (f32[4,256]{1,0:T(4,128)S(1)}, f32[4,256,768]{1,2,0:T(8,128)S(1)}, f32[4,256,768]{1,2,0:T(8,128)}) fusion(f32[4,256,768]{1,2,0:T(8,128)} %copy-done.34, f32[768]{0:T(1024)S(1)} %get-tuple-element.169, f32[4,768]{1,0:T(4,128)S(1)} %get-tuple-element.163, bf16[768,3840]{1,0:T(8,128)(2,1)S(1)} %bitcast.326, f32[4,256,3072]{2,1,0:T(8,128)} %fusion.42, ...), kind=kOutput, calls=%fused_computation.305 | convolution fusion | flops 4866440192 | bytes 26771456 | tf_op jit(solution)/shard_map/bsd,ed->bse/dot_general | solution.py:1182
  258.4 7.4 add_convert_fusion
  276.0 8.4 multiply_reduce_fusion.2
  284.4 7.1 fusion.15
  291.6 7.4 fusion.68
  299.1 3.0 fusion.129
  302.4 12.0 %fusion.34 = f32[4,256,3072]{2,1,0:T(8,128)} fusion(bf16[5376,768]{1,0:T(8,128)(2,1)} %copy-done.22, f32[4,256,768]{1,2,0:T(8,128)S(1)} %get-tuple-element.120, f32[4,768]{1,0:T(4,128)S(1)} %get-tuple-element.155, f32[4,768]{1,0:T(4,128)S(1)} %get-tuple-element.156, f32[4,256]{1,0:T(4,128)S(1)} %fusion.115, f32[4,256]{1,0:T(4,128)S(1)} %broadcast_multiply_fusion.1), kind=kOutput, calls=%fused_computation.73 | convolution fusion | flops 4835770368 | bytes 20480000 | tf_op jit(solution)/shard_map/bsd,ed->bse/dot_general | solution.py:1182
  314.4 9.9 %fusion.128 = (f32[4,256]{1,0:T(4,128)S(1)}, f32[4,256,768]{1,2,0:T(8,128)S(1)}, f32[4,256,768]{1,2,0:T(8,128)}) fusion(f32[4,256,768]{1,2,0:T(8,128)S(1)} %get-tuple-element.120, f32[768]{0:T(1024)S(1)} %get-tuple-element.167, f32[4,768]{1,0:T(4,128)S(1)} %get-tuple-element.157, bf16[768,3840]{1,0:T(8,128)(2,1)S(1)} %bitcast.314, ...), kind=kOutput, calls=%fused_computation.303 | convolution fusion | flops 4866440192 | bytes 26771456 | tf_op jit(solution)/shard_map/bsd,ed->bse/dot_general | solution.py:1182
  329.0 2.9 fusion.142
  332.0 3.5 copy.212
  335.5 4.3 multiply_reduce_fusion.5
  344.2 10.2 %bitcast_convert_fusion = bf16[768,3072]{1,0:T(8,128)(2,1)} fusion(bf16[4,256,768]{1,2,0:T(8,128)(2,1)S(1)} %get-tuple-element.103, f32[4,256,3072]{2,1,0:T(8,128)} %fusion.34, f32[3072]{0:T(1024)S(1)} %copy-done.141), kind=kOutput, calls=%fused_computation.36 | convolution fusion | flops 4865654784 | bytes 18886656 | tf_op jit(solution)/shard_map/bsd,bse->ed/dot_general | solution.py:1190
  354.4 18.5 %convert_reduce_fusion = (f32[3072]{0:T(1024)}, bf16[4,256,3072]{2,1,0:T(8,128)(2,1)}) fusion(f32[4,256,3072]{2,1,0:T(8,128)} %fusion.34, f32[3072]{0:T(1024)S(1)} %copy-done.141, bf16[4,256,768]{1,2,0:T(8,128)(2,1)S(1)} %get-tuple-element.103, bf16[768,3840]{1,0:T(8,128)(2,1)S(1)} %bitcast.316), kind=kOutput, calls=%fused_computation.18 | convolution fusion | flops 4904186880 | bytes 25190400 | tf_op jit(solution)/shard_map/bse,ed->bsd/dot_general | solution.py:1186
  372.9 9.1 fusion.141
  382.0 10.6 %bitcast_convert_fusion.1 = bf16[3072,768]{1,0:T(8,128)(2,1)} fusion(bf16[4,256,3072]{2,1,0:T(8,128)(2,1)} %get-tuple-element.207, f32[4,256,768]{1,2,0:T(8,128)S(1)} %copy-done.28, f32[4,768]{1,0:T(4,128)S(1)} %get-tuple-element.155, f32[4,768]{1,0:T(4,128)S(1)} %get-tuple-element.156, f32[4,256]{1,0:T(4,128)S(1)} %fusion.115, ...), kind=kOutput, calls=%fused_computation.37 | convolution fusion | flops 4838129664 | bytes 14188544 | tf_op jit(solution)/shard_map/bsd,bse->ed/dot_general | solution.py:1190
  392.6 3.5 copy.214
  396.1 3.5 multiply_reduce_fusion.16
  403.0 4.0 convert_reduce_fusion.5
  407.0 4.0 convolution_convert_fusion.1
  412.5 3.0 pad_maximum_fusion.3.refs_1_
  418.0 8.5 fusion.73
  429.1 8.5 multiply_reduce_fusion.1
  437.7 6.9 multiply_convert_fusion.1
  444.6 3.2 multiply_convert_fusion.8
  452.7 3.0 copy.221
  455.6 9.5 %fusion.140 = (f32[4,768]{1,0:T(4,128)}, f32[4,256,768]{2,1,0:T(8,128)}) fusion(bf16[5376,768]{1,0:T(8,128)(2,1)} %copy-done.22, bf16[4,256,768]{2,1,0:T(8,128)(2,1)} %copy.222, bf16[4,256,768]{2,1,0:T(8,128)(2,1)} %copy.221, bf16[4,256,768]{2,1,0:T(8,128)(2,1)} %copy.220), kind=kOutput, calls=%fused_computation.315 | convolution fusion | flops 3638817792 | bytes 11415552 | tf_op jit(solution)/shard_map/bse,ed->bsd/dot_general | solution.py:1186
  465.2 3.5 copy.223
  468.8 3.5 multiply_reduce_fusion.15
  476.3 4.4 convert_reduce_fusion.6
  480.7 7.0 bitcast_convert_fusion.4
  487.7 7.2 pad_maximum_fusion.1.refs_0_
  497.6 74.0 %scatter_grads.3 = (f32[168,768]{1,0:T(8,128)S(1)}, f32[24,3840]{1,0:T(8,128)S(1)}) custom-call(bf16[5376,768]{1,0:T(8,128)(2,1)} %pad_maximum_fusion.1.refs_0_, bf16[768,3840]{1,0:T(8,128)(2,1)S(1)} %copy-done.1), custom_call_target="tpu_custom_call" | custom-call | tf_op jit(solution)/shard_map/scatter_grads/pallas_call | solution.py:881
  572.3 10.0 %bitcast_convert_fusion.2 = bf16[768,3072]{1,0:T(8,128)(2,1)} fusion(bf16[4,256,768]{1,2,0:T(8,128)(2,1)S(1)} %copy-done.74, f32[4,256,3072]{2,1,0:T(8,128)} %fusion.42, f32[3072]{0:T(1024)S(1)} %copy-done.140), kind=kOutput, calls=%fused_computation.38 | convolution fusion | flops 4865654784 | bytes 18886656 | tf_op jit(solution)/shard_map/bsd,bse->ed/dot_general | solution.py:1190
  582.4 18.0 %convert_reduce_fusion.1 = (f32[3072]{0:T(1024)}, bf16[4,256,3072]{2,1,0:T(8,128)(2,1)}) fusion(f32[4,256,3072]{2,1,0:T(8,128)} %fusion.42, f32[3072]{0:T(1024)S(1)} %copy-done.140, bf16[4,256,768]{1,2,0:T(8,128)(2,1)S(1)} %copy-done.74, bf16[768,3840]{1,0:T(8,128)(2,1)S(1)} %bitcast.328), kind=kOutput, calls=%fused_computation.19 | convolution fusion | flops 4904186880 | bytes 25190400 | tf_op jit(solution)/shard_map/bse,ed->bsd/dot_general | solution.py:1186
  600.4 9.1 fusion.139
  609.5 8.4 bitcast_convert_fusion.3
  617.9 3.5 copy.225
  621.5 3.5 multiply_reduce_fusion.14
  629.0 4.0 convert_reduce_fusion.7
  633.1 4.0 convolution_convert_fusion
  644.0 8.5 fusion.70
  652.6 3.0 copy.233
  655.6 8.6 multiply_reduce_fusion
  664.2 6.8 multiply_convert_fusion
  671.0 3.2 multiply_convert_fusion.4
  681.7 9.0 fusion.138
  692.9 6.9 bitcast_convert_fusion.5
  699.9 7.2 pad_maximum_fusion.refs_0_
  709.7 83.8 %scatter_grads.2 = (f32[168,768]{1,0:T(8,128)S(1)}, f32[24,3840]{1,0:T(8,128)S(1)}) custom-call(bf16[5376,768]{1,0:T(8,128)(2,1)} %pad_maximum_fusion.refs_0_, bf16[768,3840]{1,0:T(8,128)(2,1)S(1)} %copy-done.2), custom_call_target="tpu_custom_call" | custom-call | tf_op jit(solution)/shard_map/scatter_grads/pallas_call | solution.py:881
  798.2 3.5 copy.234
  801.7 3.4 multiply_reduce_fusion.4
  809.4 3.8 convert_reduce_fusion.8
  824.3 6.9 concatenate.48
  833.2 51.5 %settle.1 = (f32[336,768]{1,0:T(8,128)S(1)}, f32[24,256]{1,0:T(8,128)S(1)}, f32[24,768]{1,0:T(8,128)S(1)}, f32[24,1024]{1,0:T(8,128)S(1)}, f32[32,24,128]{2,1,0:T(8,128)S(1)}) custom-call(f32[32,4,336]{2,1,0:T(4,128)S(1)} %bitcast.312, f32[32,16,128]{2,1,0:T(8,128)S(1)} %bitcast.311, f32[24,768]{1,0:T(8,128)S(1)} %copy-done.9, f32[336,768]{1,0:T(8,128)S(1)} %bitcast.306, ...), custom_call_target="tpu_custom_call" | custom-call | tf_op jit(solution)/shard_map/settle/pallas_call | solution.py:1145
  914.1 3.5 fusion.111
  (485 shorter events, 155.8 us)
Async XLA Ops:
  0.7 60.9 %copy-start = (bf16[4,256,16]{1,2,0:T(8,128)(2,1)S(1)}, bf16[4,256,16]{1,2,0:T(8,128)(2,1)}, u32[]{:S(2)}) copy-start(bf16[4,256,16]{1,2,0:T(8,128)(2,1)} %param.23) | copy-start | bytes 98308
  8.4 223.5 %copy-start.91 = (f32[768]{0:T(1024)}, f32[768]{0:T(1024)S(1)}, u32[]{:S(2)}) copy-start(f32[768]{0:T(1024)S(1)} %get-tuple-element.171) | copy-start | bytes 9220
  8.4 223.5 %copy-start.126 = (f32[768]{0:T(1024)}, f32[768]{0:T(1024)S(1)}, u32[]{:S(2)}) copy-start(f32[768]{0:T(1024)S(1)} %get-tuple-element.170) | copy-start | bytes 9220
  8.4 238.7 %copy-start.128 = (f32[768]{0:T(1024)}, f32[768]{0:T(1024)S(1)}, u32[]{:S(2)}) copy-start(f32[768]{0:T(1024)S(1)} %get-tuple-element.169) | copy-start | bytes 9220
  8.4 290.6 %copy-start.100 = (f32[768]{0:T(1024)}, f32[768]{0:T(1024)S(1)}, u32[]{:S(2)}) copy-start(f32[768]{0:T(1024)S(1)} %get-tuple-element.168) | copy-start | bytes 9220
  61.3 131.5 %copy-start.88 = (f32[4,768]{1,0:T(4,128)}, f32[4,768]{1,0:T(4,128)S(1)}, u32[]{:S(2)}) copy-start(f32[4,768]{1,0:T(4,128)S(1)} %get-tuple-element.166) | copy-start | bytes 36868
  61.3 131.5 %copy-start.130 = (f32[4,768]{1,0:T(4,128)}, f32[4,768]{1,0:T(4,128)S(1)}, u32[]{:S(2)}) copy-start(f32[4,768]{1,0:T(4,128)S(1)} %get-tuple-element.165) | copy-start | bytes 36868
  61.3 170.6 %copy-start.102 = (f32[4,768]{1,0:T(4,128)}, f32[4,768]{1,0:T(4,128)S(1)}, u32[]{:S(2)}) copy-start(f32[4,768]{1,0:T(4,128)S(1)} %get-tuple-element.164) | copy-start | bytes 36868
  61.3 174.2 %copy-start.84 = (f32[4,768]{1,0:T(4,128)}, f32[4,768]{1,0:T(4,128)S(1)}, u32[]{:S(2)}) copy-start(f32[4,768]{1,0:T(4,128)S(1)} %get-tuple-element.162) | copy-start | bytes 36868
  61.3 174.2 %copy-start.132 = (f32[4,768]{1,0:T(4,128)}, f32[4,768]{1,0:T(4,128)S(1)}, u32[]{:S(2)}) copy-start(f32[4,768]{1,0:T(4,128)S(1)} %get-tuple-element.161) | copy-start | bytes 36868
  61.3 185.8 %copy-start.104 = (f32[4,768]{1,0:T(4,128)}, f32[4,768]{1,0:T(4,128)S(1)}, u32[]{:S(2)}) copy-start(f32[4,768]{1,0:T(4,128)S(1)} %get-tuple-element.163) | copy-start | bytes 36868
  61.3 196.7 %copy-start.86 = (f32[4,768]{1,0:T(4,128)}, f32[4,768]{1,0:T(4,128)S(1)}, u32[]{:S(2)}) copy-start(f32[4,768]{1,0:T(4,128)S(1)} %get-tuple-element.159) | copy-start | bytes 36868
  61.3 196.7 %copy-start.134 = (f32[4,768]{1,0:T(4,128)}, f32[4,768]{1,0:T(4,128)S(1)}, u32[]{:S(2)}) copy-start(f32[4,768]{1,0:T(4,128)S(1)} %get-tuple-element.158) | copy-start | bytes 36868
  63.3 134.7 %copy-start.30 = (f32[768,4,256]{2,0,1:T(8,128)}, f32[768,4,256]{2,0,1:T(8,128)S(1)}, u32[]{:S(2)}) copy-start(f32[768,4,256]{2,0,1:T(8,128)S(1)} %get-tuple-element.181) | copy-start | bytes 9437188
  63.3 129.5 %copy-start.143 = (f32[2304]{0:T(1024)S(1)}, f32[2304]{0:T(1024)}, u32[]{:S(2)}) copy-start(f32[2304]{0:T(1024)} %get-tuple-element.177) | copy-start | bytes 27652
  63.3 134.6 %copy-start.94 = (f32[4,256]{1,0:T(4,128)}, f32[4,256]{1,0:T(4,128)S(1)}, u32[]{:S(2)}) copy-start(f32[4,256]{1,0:T(4,128)S(1)} %broadcast_multiply_fusion.4) | copy-start | bytes 12292
  63.9 134.0 %copy-start.120 = (f32[4,256]{1,0:T(4,128)}, f32[4,256]{1,0:T(4,128)S(1)}, u32[]{:S(2)}) copy-start(f32[4,256]{1,0:T(4,128)S(1)} %multiply_reduce_fusion.22) | copy-start | bytes 12292
  64.0 134.0 %copy-start.113 = (f32[4,256]{1,0:T(4,128)}, f32[4,256]{1,0:T(4,128)S(1)}, u32[]{:S(2)}) copy-start(f32[4,256]{1,0:T(4,128)S(1)} %fusion.112) | copy-start | bytes 12292
  216.6 15.3 %slice-start.10 = ((s8[5898240]{0:T(1024)(128)(4,1)}), s8[4194304]{0:T(1024)(128)(4,1)S(1)}, s32[]{:S(2)}) async-start(s8[5898240]{0:T(1024)(128)(4,1)} %bitcast.325), calls=%async_computation.10 | async-start | bytes 8388608
  235.1 12.0 %copy-start.96 = (f32[4,256]{1,0:T(4,128)}, f32[4,256]{1,0:T(4,128)S(1)}, u32[]{:S(2)}) copy-start(f32[4,256]{1,0:T(4,128)S(1)} %broadcast_multiply_fusion.3) | copy-start | bytes 12292
  235.5 11.7 %copy-start.122 = (f32[4,256]{1,0:T(4,128)}, f32[4,256]{1,0:T(4,128)S(1)}, u32[]{:S(2)}) copy-start(f32[4,256]{1,0:T(4,128)S(1)} %multiply_reduce_fusion.21) | copy-start | bytes 12292
  238.2 9.0 copy-start.116
  238.2 9.0 copy-start.139
  257.6 8.2 copy-start.98
  284.4 14.7 %slice-start = ((s8[5898240]{0:T(1024)(128)(4,1)}), s8[4194304]{0:T(1024)(128)(4,1)S(1)}, s32[]{:S(2)}) async-start(s8[5898240]{0:T(1024)(128)(4,1)} %bitcast.313), calls=%async_computation | async-start | bytes 8388608
  302.0 12.4 %copy-start.27 = (f32[4,256,768]{1,2,0:T(8,128)}, f32[4,256,768]{1,2,0:T(8,128)S(1)}, u32[]{:S(2)}) copy-start(f32[4,256,768]{1,2,0:T(8,128)S(1)} %get-tuple-element.120) | copy-start | bytes 9437188
  302.4 12.1 %copy-start.141 = (f32[3072]{0:T(1024)S(1)}, f32[3072]{0:T(1024)}, u32[]{:S(2)}) copy-start(f32[3072]{0:T(1024)} %get-tuple-element.174) | copy-start | bytes 36868
  342.3 12.2 %slice-start.2 = ((s8[5898240]{0:T(1024)(128)(4,1)}), s8[4194304]{0:T(1024)(128)(4,1)S(1)}, s32[]{:S(2)}) async-start(s8[5898240]{0:T(1024)(128)(4,1)} %bitcast.315), calls=%async_computation.2 | async-start | bytes 8388608
  344.2 10.3 %slice-start.3 = ((s8[5898240]{0:T(1024)(128)(4,1)}), s8[1703936]{0:T(1024)(128)(4,1)S(1)}, s32[]{:S(2)}) async-start(s8[5898240]{0:T(1024)(128)(4,1)} %bitcast.315), calls=%async_computation.3 | async-start | bytes 3407872
  344.2 28.7 %slice-start.8 = ((s8[8257536]{0:T(1024)(128)(4,1)}), s8[4194304]{0:T(1024)(128)(4,1)S(1)}, s32[]{:S(2)}) async-start(s8[8257536]{0:T(1024)(128)(4,1)} %bitcast.323), calls=%async_computation.8 | async-start | bytes 8388608
  354.4 18.5 %slice-start.9 = ((s8[8257536]{0:T(1024)(128)(4,1)}), s8[4063232]{0:T(1024)(128)(4,1)S(1)}, s32[]{:S(2)}) async-start(s8[8257536]{0:T(1024)(128)(4,1)} %bitcast.323), calls=%async_computation.9 | async-start | bytes 8126464
  372.9 9.1 copy-start.28
  497.6 74.7 %copy-start.74 = (bf16[4,256,768]{1,2,0:T(8,128)(2,1)S(1)}, bf16[4,256,768]{1,2,0:T(8,128)(2,1)}, u32[]{:S(2)}) copy-start(bf16[4,256,768]{1,2,0:T(8,128)(2,1)} %get-tuple-element.108) | copy-start | bytes 4718596
  497.6 74.7 %copy-start.140 = (f32[3072]{0:T(1024)S(1)}, f32[3072]{0:T(1024)}, u32[]{:S(2)}) copy-start(f32[3072]{0:T(1024)} %get-tuple-element.175) | copy-start | bytes 36868
  497.6 84.8 %slice-start.12 = ((s8[5898240]{0:T(1024)(128)(4,1)}), s8[4194304]{0:T(1024)(128)(4,1)S(1)}, s32[]{:S(2)}) async-start(s8[5898240]{0:T(1024)(128)(4,1)} %bitcast.327), calls=%async_computation.12 | async-start | bytes 8388608
  571.6 10.8 %copy-start.4 = (f32[24,3840]{1,0:T(8,128)}, f32[24,3840]{1,0:T(8,128)S(1)}, u32[]{:S(2)}) copy-start(f32[24,3840]{1,0:T(8,128)S(1)} %get-tuple-element.56) | copy-start | bytes 1105924
  572.3 10.0 %slice-start.13 = ((s8[5898240]{0:T(1024)(128)(4,1)}), s8[1703936]{0:T(1024)(128)(4,1)S(1)}, s32[]{:S(2)}) async-start(s8[5898240]{0:T(1024)(128)(4,1)} %bitcast.327), calls=%async_computation.13 | async-start | bytes 3407872
  572.3 28.1 %slice-start.6 = ((s8[8257536]{0:T(1024)(128)(4,1)}), s8[4194304]{0:T(1024)(128)(4,1)S(1)}, s32[]{:S(2)}) async-start(s8[8257536]{0:T(1024)(128)(4,1)} %bitcast.321), calls=%async_computation.6 | async-start | bytes 8388608
  582.3 18.0 %slice-start.7 = ((s8[8257536]{0:T(1024)(128)(4,1)}), s8[4063232]{0:T(1024)(128)(4,1)S(1)}, s32[]{:S(2)}) async-start(s8[8257536]{0:T(1024)(128)(4,1)} %bitcast.321), calls=%async_computation.7 | async-start | bytes 8126464
  600.4 9.1 copy-start.35
  600.4 9.1 copy-start.85
  600.4 9.1 copy-start.97
  600.4 9.1 copy-start.117
  600.4 9.1 copy-start.133
  600.4 9.1 copy-start.147
  681.7 9.1 copy-start.60
  681.7 9.1 copy-start.62
  681.7 9.1 copy-start.64
  681.7 9.1 copy-start.65
  681.7 9.1 copy-start.66
  681.7 9.1 copy-start.67
  809.3 8.7 copy-start.136
  809.3 9.3 %copy-start.108 = (f32[4,768]{1,0:T(4,128)S(1)}, f32[4,768]{1,0:T(4,128)}, u32[]{:S(2)}) copy-start(f32[4,768]{1,0:T(4,128)} %get-tuple-element.84) | copy-start | bytes 36868
  809.3 9.9 %copy-start.107 = (f32[4,768]{1,0:T(4,128)S(1)}, f32[4,768]{1,0:T(4,128)}, u32[]{:S(2)}) copy-start(f32[4,768]{1,0:T(4,128)} %get-tuple-element.131) | copy-start | bytes 36868
  809.3 10.5 %copy-start.106 = (f32[4,768]{1,0:T(4,128)S(1)}, f32[4,768]{1,0:T(4,128)}, u32[]{:S(2)}) copy-start(f32[4,768]{1,0:T(4,128)} %get-tuple-element.202) | copy-start | bytes 36868
  809.3 11.1 %copy-start.112 = (f32[4,768]{1,0:T(4,128)S(1)}, f32[4,768]{1,0:T(4,128)}, u32[]{:S(2)}) copy-start(f32[4,768]{1,0:T(4,128)} %get-tuple-element.90) | copy-start | bytes 36868
  809.4 14.9 %copy-start.83 = (f32[24576]{0:T(1024)S(1)}, f32[24576]{0:T(1024)}, u32[]{:S(2)}) copy-start(f32[24576]{0:T(1024)} %reshape.359) | copy-start | bytes 294916
  813.2 18.0 %copy-start.9 = (f32[24,768]{1,0:T(8,128)S(1)}, f32[24,768]{1,0:T(8,128)}, u32[]{:S(2)}) copy-start(f32[24,768]{1,0:T(8,128)} %copy-done.8) | copy-start | bytes 221188
  813.2 18.0 %copy-start.16 = (f32[128,128]{1,0:T(8,128)S(1)}, f32[128,128]{1,0:T(8,128)}, u32[]{:S(2)}) copy-start(f32[128,128]{1,0:T(8,128)} %copy-done.15) | copy-start | bytes 196612
  813.2 18.0 %copy-start.18 = (f32[24,128]{1,0:T(8,128)S(1)}, f32[24,128]{1,0:T(8,128)}, u32[]{:S(2)}) copy-start(f32[24,128]{1,0:T(8,128)} %copy-done.17) | copy-start | bytes 36868
  813.2 18.0 %copy-start.20 = (f32[24,128]{1,0:T(8,128)S(1)}, f32[24,128]{1,0:T(8,128)}, u32[]{:S(2)}) copy-start(f32[24,128]{1,0:T(8,128)} %copy-done.19) | copy-start | bytes 36868
  885.6 24.5 %copy-start.81 = (f32[768,32]{0,1:T(8,128)S(1)}, f32[768,32]{0,1:T(8,128)}, u32[]{:S(2)}) copy-start(f32[768,32]{0,1:T(8,128)} %param.39) | copy-start | bytes 294916
  885.6 28.5 %copy-start.5 = (f32[24,3840]{1,0:T(8,128)S(1)}, f32[24,3840]{1,0:T(8,128)}, u32[]{:S(2)}) copy-start(f32[24,3840]{1,0:T(8,128)} %copy-done.4) | copy-start | bytes 1105924
  896.6 15.3 %copy-start.82 = (f32[2041,24]{0,1:T(8,128)S(1)}, f32[2041,24]{0,1:T(8,128)}, u32[]{:S(2)}) copy-start(f32[2041,24]{0,1:T(8,128)} %param.27) | copy-start | bytes 587812
  (102 other events, 377.0 us)

commit v2 on v1

--- a/solution.py
+++ b/solution.py
@@ -21,6 +21,8 @@
 STEP = 10
 SEQ = 256
 IW = 5376
+OW = 3840
+FF = 3072
 CW = 10752
 
 
@@ -1163,6 +1165,360 @@
         name="settle",
     )(*ins)
 
+
+def dot_nn(left, right):
+    return lax.dot_general(left, right, (((1,), (0,)), ((), ())), preferred_element_type=jnp.float32)
+
+
+def norm_parts(value):
+    centered = value - jnp.mean(value, -1, keepdims=True)
+    scale = lax.rsqrt(jnp.mean(centered * centered, -1, keepdims=True) + 1e-06)
+    return centered * scale, scale
+
+
+def norm_back(normed, scale, d_normed):
+    inner = jnp.mean(d_normed * normed, -1, keepdims=True)
+    return scale * (d_normed - jnp.mean(d_normed, -1, keepdims=True) - normed * inner)
+
+
+GELU_C = math.sqrt(2.0 / math.pi)
+
+
+def gelu_value(u):
+    return 0.5 * u * (1.0 + jnp.tanh(GELU_C * (u + 0.044715 * u * u * u)))
+
+
+def gelu_slope(u):
+    square = u * u
+    t = jnp.tanh(GELU_C * u * (1.0 + 0.044715 * square))
+    return 0.5 * (1.0 + t) + 0.5 * u * (1.0 - t * t) * (GELU_C * (1.0 + 3 * 0.044715 * square))
+
+
+def head_masks(shape):
+    low_half = lax.broadcasted_iota(jnp.int32, shape, 1) < HEAD_DIM
+    return low_half, jnp.logical_not(low_half)
+
+
+class Weights:
+    def __init__(self, hbm, vmem, sems):
+        w_in, w_out = hbm
+        self.w_in, self.w_out = vmem
+        cut = 3 * MODEL_WIDTH
+        spans = [
+            (w_in.at[pl.ds(0, cut), :], self.w_in.at[pl.ds(0, cut), :]),
+            (w_out.at[:, pl.ds(0, MODEL_WIDTH)], self.w_out.at[:, pl.ds(0, MODEL_WIDTH)]),
+            (w_in.at[pl.ds(cut, FF), :], self.w_in.at[pl.ds(cut, FF), :]),
+            (w_out.at[:, pl.ds(MODEL_WIDTH, FF)], self.w_out.at[:, pl.ds(MODEL_WIDTH, FF)]),
+        ]
+        self.copies = [pltpu.make_async_copy(src, dst, sems.at[i]) for i, (src, dst) in enumerate(spans)]
+
+    def start(self, order):
+        @pl.when(pl.program_id(0) == 0)
+        def _():
+            for i in order:
+                self.copies[i].start()
+
+    def need(self, i):
+        @pl.when(pl.program_id(0) == 0)
+        def _():
+            self.copies[i].wait()
+
+
+def forward_image(x_ref, mod, weights, b_in, b_out, outs):
+    h1, qkv, probs, o, a, x1, h2, u, g, f = outs
+    shift1, scale1, gate1, shift2, scale2, gate2 = (mod[0, i : i + 1, :] for i in range(6))
+    width = MODEL_WIDTH
+    x = x_ref[...]
+    h1[...] = (norm_parts(x)[0] * (1 + scale1) + shift1).astype(jnp.bfloat16)
+    weights.need(0)
+    for j in range(3):
+        span = slice(j * width, (j + 1) * width)
+        qkv[:, span] = (dot_nt(h1[...], weights.w_in[span, :]) + b_in[:, span]).astype(jnp.bfloat16)
+    for pair in range(HEADS // 2):
+        lanes = slice(128 * pair, 128 * (pair + 1))
+        q, k, v = (qkv[:, j * width + 128 * pair : j * width + 128 * (pair + 1)] for j in range(3))
+        q = q * jnp.bfloat16(HEAD_DIM**-0.5)
+        zero = jnp.zeros_like(q)
+        mixed = None
+        for half, mask in enumerate(head_masks(q.shape)):
+            scores = dot_nt(jnp.where(mask, q, zero), k)
+            expo = jnp.exp(scores - jnp.max(scores, -1, keepdims=True))
+            weight = (expo * pl.reciprocal(jnp.sum(expo, -1, keepdims=True))).astype(jnp.bfloat16)
+            probs[0, 2 * pair + half] = weight
+            term = dot_nn(weight, jnp.where(mask, v, zero))
+            mixed = term if mixed is None else mixed + term
+        o[:, lanes] = mixed.astype(jnp.bfloat16)
+    weights.need(1)
+    branch = dot_nt(o[...], weights.w_out[:, :width]) + b_out[:, :width]
+    a[...] = branch.astype(jnp.bfloat16)
+    x1[...] = x + gate1 * branch
+    h2[...] = (norm_parts(x1[...])[0] * (1 + scale2) + shift2).astype(jnp.bfloat16)
+    weights.need(2)
+    weights.need(3)
+    total = None
+    for j in range(FF // width):
+        span = slice(j * width, (j + 1) * width)
+        rows = slice((3 + j) * width, (4 + j) * width)
+        value = dot_nt(h2[...], weights.w_in[rows, :]) + b_in[:, rows]
+        u[:, span] = value.astype(jnp.bfloat16)
+        g[:, span] = gelu_value(value).astype(jnp.bfloat16)
+        term = dot_nt(g[:, span], weights.w_out[:, (1 + j) * width : (2 + j) * width])
+        total = term if total is None else total + term
+    ffn = total + b_out[:, width:]
+    f[...] = ffn.astype(jnp.bfloat16)
+    return x1[...] + gate2 * ffn
+
+
+def forward_kernel(x, mod, w_in, w_out, b_in, b_out, *refs):
+    outs, x_out, vm_in, vm_out, sems = refs[:10], refs[10], refs[11], refs[12], refs[13]
+    weights = Weights((w_in, w_out), (vm_in, vm_out), sems)
+    weights.start((0, 1, 2, 3))
+    x_out[...] = forward_image(x, mod, weights, b_in, b_out, outs)
+
+
+def head_kernel(scale_out, x, mod, w_in, w_out, b_in, b_out, final, head_t, b_head, targets_t, *refs):
+    outs, (dx, d_final, g_head, g_bias, loss), (vm_in, vm_out, sems) = refs[:10], refs[10:15], refs[15:]
+    weights = Weights((w_in, w_out), (vm_in, vm_out), sems)
+    weights.start((0, 1, 2, 3))
+    last = forward_image(x, mod, weights, b_in, b_out, outs)
+    normed, scale = norm_parts(last)
+    shift_row, scale_row = final[0, 0:1, :], final[0, 1:2, :]
+    shaped = (normed * (1 + scale_row) + shift_row).astype(jnp.bfloat16)
+    low = head_t[...].astype(jnp.bfloat16)
+    error = dot_nt(low, shaped) + b_head[...] - targets_t[0]
+    d_out = (error * scale_out).astype(jnp.bfloat16)
+
+    @pl.when(pl.program_id(0) == 0)
+    def _():
+        g_head[...] = jnp.zeros_like(g_head)
+        g_bias[...] = jnp.zeros_like(g_bias)
+        loss[...] = jnp.zeros_like(loss)
+
+    g_head[...] += dot_nn(d_out, shaped)
+    g_bias[...] += jnp.sum(d_out.astype(jnp.float32), 1, keepdims=True)
+    loss[...] += jnp.sum(error * error)
+    d_shaped = dot_tn(d_out, low)
+    d_final[0, 0:1, :] = jnp.sum(d_shaped, 0, keepdims=True)
+    d_final[0, 1:2, :] = jnp.sum(d_shaped * normed, 0, keepdims=True)
+    dx[...] = norm_back(normed, scale, d_shaped * (1 + scale_row))
+
+
+WEIGHT_SCRATCH = [
+    pltpu.VMEM((IW, MODEL_WIDTH), jnp.bfloat16),
+    pltpu.VMEM((MODEL_WIDTH, OW), jnp.bfloat16),
+    pltpu.SemaphoreType.DMA((4,)),
+]
+
+
+def token_block(width):
+    return pl.BlockSpec((SEQ, width), lambda i: (i, 0))
+
+
+def image_block(*dims):
+    return pl.BlockSpec((1,) + dims, lambda i: (i,) + (0,) * len(dims))
+
+
+def whole_block(*dims):
+    return pl.BlockSpec(dims, lambda i: (0,) * len(dims))
+
+
+def kept_shapes(images):
+    tokens, width, low, full = images * SEQ, MODEL_WIDTH, jnp.bfloat16, jnp.float32
+    shapes = [((tokens, width), low), ((tokens, 3 * width), low), ((images, HEADS, SEQ, SEQ), low), ((tokens, width), low),
+              ((tokens, width), low), ((tokens, width), full), ((tokens, width), low), ((tokens, FF), low),
+              ((tokens, FF), low), ((tokens, width), low)]
+    specs = [token_block(s[1]) if len(s) == 2 else image_block(*s[1:]) for s, _ in shapes]
+    return [jax.ShapeDtypeStruct(s, t) for s, t in shapes], specs
+
+
+def forward_specs():
+    any_block = pl.BlockSpec(memory_space=pl.ANY)
+    return [token_block(MODEL_WIDTH), image_block(6, MODEL_WIDTH), any_block, any_block, whole_block(1, IW),
+            whole_block(1, 2 * MODEL_WIDTH)]
+
+
+def forward_block(ins):
+    images = ins[1].shape[0]
+    shapes, specs = kept_shapes(images)
+    return pl.pallas_call(
+        forward_kernel,
+        grid=(images,),
+        out_shape=shapes + [jax.ShapeDtypeStruct((images * SEQ, MODEL_WIDTH), jnp.float32)],
+        in_specs=forward_specs(),
+        out_specs=specs + [token_block(MODEL_WIDTH)],
+        scratch_shapes=WEIGHT_SCRATCH,
+        compiler_params=pltpu.CompilerParams(vmem_limit_bytes=56 << 20),
+        name="forward_block",
+    )(*ins)
+
+
+def forward_head(ins, scale_out):
+    images = ins[1].shape[0]
+    shapes, specs = kept_shapes(images)
+    extra = [(images * SEQ, MODEL_WIDTH), (images, 2, MODEL_WIDTH), (PO, MODEL_WIDTH), (PO, 128), (8, 128)]
+    return pl.pallas_call(
+        functools.partial(head_kernel, scale_out),
+        grid=(images,),
+        out_shape=shapes + [jax.ShapeDtypeStruct(s, jnp.float32) for s in extra],
+        in_specs=forward_specs()
+        + [image_block(2, MODEL_WIDTH), whole_block(PO, MODEL_WIDTH), whole_block(PO, 1), image_block(PO, SEQ)],
+        out_specs=specs
+        + [token_block(MODEL_WIDTH), image_block(2, MODEL_WIDTH), whole_block(PO, MODEL_WIDTH), whole_block(PO, 128),
+           whole_block(8, 128)],
+        scratch_shapes=WEIGHT_SCRATCH,
+        compiler_params=pltpu.CompilerParams(vmem_limit_bytes=56 << 20),
+        name="forward_head",
+    )(*ins)
+
+
+def backward_image(refs, mod, weights, outs):
+    up_ref, x_ref, x1_ref, probs, qkv, a, f, u = refs
+    dx, d_qkv, d_u, d_f, d_a, d_mod, g_bin, g_bout = outs
+    width = MODEL_WIDTH
+    shift1, scale1, gate1, shift2, scale2, gate2 = (mod[0, i : i + 1, :] for i in range(6))
+
+    @pl.when(pl.program_id(0) == 0)
+    def _():
+        g_bin[...] = jnp.zeros_like(g_bin)
+        g_bout[...] = jnp.zeros_like(g_bout)
+
+    def rows_sum(value):
+        return jnp.sum(value.astype(jnp.float32), 0, keepdims=True)
+
+    upstream = up_ref[...]
+    d_f[...] = (gate2 * upstream).astype(jnp.bfloat16)
+    d_mod[0, 5:6, :] = rows_sum(f[...].astype(jnp.float32) * upstream)
+    g_bout[:, width:] += rows_sum(d_f[...])
+    weights.need(3)
+    weights.need(2)
+    d_h2 = None
+    for j in range(FF // width):
+        span = slice(j * width, (j + 1) * width)
+        rows = slice((3 + j) * width, (4 + j) * width)
+        d_g = dot_nn(d_f[...], weights.w_out[:, (1 + j) * width : (2 + j) * width])
+        d_u[:, span] = (d_g * gelu_slope(u[:, span].astype(jnp.float32))).astype(jnp.bfloat16)
+        g_bin[:, rows] += rows_sum(d_u[:, span])
+        term = dot_nn(d_u[:, span], weights.w_in[rows, :])
+        d_h2 = term if d_h2 is None else d_h2 + term
+    normed, scale = norm_parts(x1_ref[...])
+    d_mod[0, 3:4, :] = rows_sum(d_h2)
+    d_mod[0, 4:5, :] = rows_sum(d_h2 * normed)
+    upstream = upstream + norm_back(normed, scale, d_h2 * (1 + scale2))
+    d_mod[0, 2:3, :] = rows_sum(a[...].astype(jnp.float32) * upstream)
+    d_a[...] = (gate1 * upstream).astype(jnp.bfloat16)
+    g_bout[:, :width] += rows_sum(d_a[...])
+    dx[...] = upstream
+    weights.need(1)
+    d_o = dot_nn(d_a[...], weights.w_out[:, :width]).astype(jnp.bfloat16)
+    root = HEAD_DIM**-0.5
+    for pair in range(HEADS // 2):
+        lanes = [slice(j * width + 128 * pair, j * width + 128 * (pair + 1)) for j in range(3)]
+        q, k, v = (qkv[:, s] for s in lanes)
+        d_mixed = d_o[:, 128 * pair : 128 * (pair + 1)]
+        zero = jnp.zeros_like(q)
+        sums = [None] * 3
+        for half, mask in enumerate(head_masks(q.shape)):
+            weight = probs[0, 2 * pair + half]
+            full = weight.astype(jnp.float32)
+            d_masked = jnp.where(mask, d_mixed, zero)
+            d_probs = dot_nt(d_masked, v)
+            d_scores = (full * (d_probs - jnp.sum(full * d_probs, -1, keepdims=True))).astype(jnp.bfloat16)
+            terms = (
+                dot_nn(d_scores, jnp.where(mask, k, zero)),
+                dot_tn(d_scores, jnp.where(mask, q, zero)),
+                dot_tn(weight, d_masked),
+            )
+            sums = [t if s is None else s + t for s, t in zip(sums, terms)]
+        d_qkv[:, lanes[0]] = (sums[0] * root).astype(jnp.bfloat16)
+        d_qkv[:, lanes[1]] = (sums[1] * root).astype(jnp.bfloat16)
+        d_qkv[:, lanes[2]] = sums[2].astype(jnp.bfloat16)
+    weights.need(0)
+    d_h1 = None
+    for j in range(3):
+        span = slice(j * width, (j + 1) * width)
+        g_bin[:, span] += rows_sum(d_qkv[:, span])
+        term = dot_nn(d_qkv[:, span], weights.w_in[span, :])
+        d_h1 = term if d_h1 is None else d_h1 + term
+    normed, scale = norm_parts(x_ref[...])
+    d_mod[0, 0:1, :] = rows_sum(d_h1)
+    d_mod[0, 1:2, :] = rows_sum(d_h1 * normed)
+    dx[...] += norm_back(normed, scale, d_h1 * (1 + scale1))
+
+
+def backward_kernel(mod, w_in, w_out, *refs):
+    ins, outs, (vm_in, vm_out, sems) = refs[:8], refs[8:16], refs[16:]
+    weights = Weights((w_in, w_out), (vm_in, vm_out), sems)
+    weights.start((3, 2, 1, 0))
+    backward_image(ins, mod, weights, outs)
+
+
+def backward_block(mods, w_in, w_out, refs):
+    images, width, low, full = mods.shape[0], MODEL_WIDTH, jnp.bfloat16, jnp.float32
+    tokens = images * SEQ
+    any_block = pl.BlockSpec(memory_space=pl.ANY)
+    shapes = [((tokens, width), full), ((tokens, 3 * width), low), ((tokens, FF), low), ((tokens, width), low),
+              ((tokens, width), low), ((images, 6, width), full), ((1, IW), full), ((1, 2 * width), full)]
+    return pl.pallas_call(
+        backward_kernel,
+        grid=(images,),
+        out_shape=[jax.ShapeDtypeStruct(s, t) for s, t in shapes],
+        in_specs=[image_block(6, width), any_block, any_block, token_block(width), token_block(width), token_block(width),
+                  image_block(HEADS, SEQ, SEQ), token_block(3 * width), token_block(width), token_block(width),
+                  token_block(FF)],
+        out_specs=[token_block(s[1]) for s, _ in shapes[:5]]
+        + [image_block(6, width), whole_block(1, IW), whole_block(1, 2 * width)],
+        scratch_shapes=WEIGHT_SCRATCH,
+        compiler_params=pltpu.CompilerParams(vmem_limit_bytes=56 << 20),
+        name="backward_block",
+    )(mods, w_in, w_out, *refs)
+
+
+GRAD_STEPS = tuple((0, j) for j in range(3)) + tuple((1, j) for j in range(4)) + ((2, 0),) + tuple((3, j) for j in range(4))
+
+
+def grads_kernel(*refs):
+    ins, (g_in, g_out), bufs, (keep_in, keep_out, load_sems, store_sems) = refs[:8], refs[8:10], refs[10:18], refs[18:]
+    width = MODEL_WIDTH
+    copies = [pltpu.make_async_copy(src, dst, load_sems.at[i]) for i, (src, dst) in enumerate(zip(ins, bufs))]
+    for copy in copies:
+        copy.start()
+    stores = []
+    for step, (kind, j) in enumerate(GRAD_STEPS):
+        left, right = bufs[2 * kind], bufs[2 * kind + 1]
+        if j == 0:
+            copies[2 * kind].wait()
+            copies[2 * kind + 1].wait()
+        span = pl.ds(j * width, width)
+        if kind < 2:
+            at = pl.ds((3 * kind + j) * width, width)
+            keep_in[at, :] = dot_tn(left[:, span], right[...]).astype(jnp.bfloat16)
+            store = pltpu.make_async_copy(keep_in.at[at, :], g_in.at[at, :], store_sems.at[step])
+        else:
+            at = pl.ds((kind - 2 + j) * width, width)
+            keep_out[:, at] = dot_tn(left[...], right[:, span]).astype(jnp.bfloat16)
+            store = pltpu.make_async_copy(keep_out.at[:, at], g_out.at[:, at], store_sems.at[step])
+        store.start()
+        stores.append(store)
+    for store in stores:
+        store.wait()
+
+
+def weight_grads(ins):
+    any_block = pl.BlockSpec(memory_space=pl.ANY)
+    return pl.pallas_call(
+        grads_kernel,
+        out_shape=[
+            jax.ShapeDtypeStruct((IW, MODEL_WIDTH), jnp.bfloat16), jax.ShapeDtypeStruct((MODEL_WIDTH, OW), jnp.bfloat16)
+        ],
+        in_specs=[any_block] * 8,
+        out_specs=[any_block] * 2,
+        scratch_shapes=[pltpu.VMEM(a.shape, a.dtype) for a in ins]
+        + [pltpu.VMEM((IW, MODEL_WIDTH), jnp.bfloat16), pltpu.VMEM((MODEL_WIDTH, OW), jnp.bfloat16),
+           pltpu.SemaphoreType.DMA((8,)), pltpu.SemaphoreType.DMA((len(GRAD_STEPS),))],
+        compiler_params=pltpu.CompilerParams(vmem_limit_bytes=56 << 20),
+        name="weight_grads",
+    )(*ins)
+
 def code_table():
     quarter = MODEL_WIDTH // 4
     omega = (1.0 / 10000.0 ** (np.arange(quarter, dtype=np.float32) / np.float32(quarter))).astype(np.float32)
@@ -1180,60 +1536,6 @@
 
 def rows_t(left, right):
     return jnp.einsum("bsd,ed->bse", left, right, preferred_element_type=jnp.float32)
-
-
-def back_t(left, right):
-    return jnp.einsum("bse,ed->bsd", left, right, preferred_element_type=jnp.float32)
-
-
-def outer_t(left, right):
-    return jnp.einsum("bsd,bse->ed", left, right, preferred_element_type=jnp.float32).astype(jnp.bfloat16)
-
-
-def forward_t(x, mod, w_in, w_out, bias_in, bias_out):
-    pieces = [mod[:, None, i * MODEL_WIDTH : (i + 1) * MODEL_WIDTH] for i in range(6)]
-    shaped_one = (layer_norm(x) * (1 + pieces[1]) + pieces[0]).astype(jnp.bfloat16)
-    triple = (rows_t(shaped_one, w_in[: 3 * MODEL_WIDTH]) + bias_in[: 3 * MODEL_WIDTH]).astype(jnp.bfloat16)
-    mixed_heads, log_norm = attend(triple)
-    branch = rows_t(mixed_heads, w_out[:, :MODEL_WIDTH]) + bias_out[:MODEL_WIDTH]
-    middle = x + pieces[2] * branch
-    shaped_two = (layer_norm(middle) * (1 + pieces[4]) + pieces[3]).astype(jnp.bfloat16)
-    pre_ffn = rows_t(shaped_two, w_in[3 * MODEL_WIDTH :]) + bias_in[3 * MODEL_WIDTH :]
-    active = gelu(pre_ffn).astype(jnp.bfloat16)
-    ffn_out = rows_t(active, w_out[:, MODEL_WIDTH:]) + bias_out[MODEL_WIDTH:]
-    kept = (x, shaped_one, triple, log_norm, mixed_heads, branch, middle, shaped_two, pre_ffn, active, ffn_out)
-    return middle + pieces[5] * ffn_out, kept
-
-
-def backward_t(upstream, mod, w_in, w_out, kept):
-    x, shaped_one, triple, log_norm, mixed_heads, branch, middle, shaped_two, pre_ffn, active, ffn_out = kept
-    pieces = [mod[:, None, i * MODEL_WIDTH : (i + 1) * MODEL_WIDTH] for i in range(6)]
-    d_ffn = (pieces[5] * upstream).astype(jnp.bfloat16)
-    gate_two = jnp.sum(ffn_out * upstream, 1)
-    grad_down = outer_t(active, d_ffn)
-    d_active = back_t(d_ffn, w_out[:, MODEL_WIDTH:])
-    d_pre = local_back(gelu, pre_ffn, d_active).astype(jnp.bfloat16)
-    grad_up = outer_t(shaped_two, d_pre)
-    d_shaped = back_t(d_pre, w_in[3 * MODEL_WIDTH :])
-    shift_two = jnp.sum(d_shaped, 1)
-    scale_two = jnp.sum(d_shaped * layer_norm(middle), 1)
-    upstream = upstream + local_back(layer_norm, middle, d_shaped * (1 + pieces[4]))
-    gate_one = jnp.sum(branch * upstream, 1)
-    d_branch = (pieces[2] * upstream).astype(jnp.bfloat16)
-    grad_proj = outer_t(mixed_heads, d_branch)
-    d_mixed = back_t(d_branch, w_out[:, :MODEL_WIDTH]).astype(jnp.bfloat16)
-    d_triple = attend_back(triple, log_norm, d_mixed)
-    grad_qkv = outer_t(shaped_one, d_triple)
-    d_shaped = back_t(d_triple, w_in[: 3 * MODEL_WIDTH])
-    shift_one = jnp.sum(d_shaped, 1)
-    scale_one = jnp.sum(d_shaped * layer_norm(x), 1)
-    upstream = upstream + local_back(layer_norm, x, d_shaped * (1 + pieces[1]))
-    mod_grad = jnp.concatenate([shift_one, scale_one, gate_one, shift_two, scale_two, gate_two], 1)
-    bias_in_grad = jnp.concatenate([column_sum(d_triple), column_sum(d_pre)])
-    bias_out_grad = jnp.concatenate([column_sum(d_branch), column_sum(d_ffn)])
-    grad_in = jnp.concatenate([grad_qkv, grad_up], 0)
-    grad_out = jnp.concatenate([grad_proj, grad_down], 1)
-    return upstream, mod_grad, grad_in, grad_out, bias_in_grad, bias_out_grad
 
 
 def body(
@@ -1269,46 +1571,42 @@
     mods, pre, cond, hid_all, low_all, feat_all, lab_all, notes = modulate(
         [note, w_t1, w_t2, w_class, cond_t, own_bias(time_one, cols), own_bias(time_two, cols), own_cond_bias]
     )
-    modulation = mods.transpose(1, 0, 2).reshape(images, CW)
+    chunks = mods.transpose(1, 0, 2).reshape(images, 6 * LAYERS + 2, MODEL_WIDTH)
     w_patch = notes[:, :3, FREQ + 128 :].reshape(MODEL_WIDTH, PD).astype(jnp.bfloat16)
-    head_low = head_w.astype(jnp.bfloat16)
-    x = rows_t(latents, w_patch) + patch_bias + position_sum()
-    kept_all = []
+    x = (rows_t(latents, w_patch) + patch_bias + position_sum()).reshape(images * SEQ, MODEL_WIDTH)
+    block_mods = [chunks[:, 6 * i : 6 * (i + 1)] for i in range(LAYERS)]
+    head_t = head_w.T
+    tokens_all = devices * images * SEQ * PO
+    kept_all, starts = [], []
     for i in range(LAYERS):
-        mod = modulation[:, 6 * MODEL_WIDTH * i : 6 * MODEL_WIDTH * (i + 1)]
-        x, kept = forward_t(x, mod, w_in[i], w_out[i], block_input_bias[i], block_output_bias[i])
+        ins = [x, block_mods[i], w_in[i], w_out[i], block_input_bias[i][None], block_output_bias[i][None]]
+        starts.append(x)
+        if i < LAYERS - 1:
+            *kept, x = forward_block(ins)
+        else:
+            ins += [chunks[:, 6 * LAYERS :], head_t, head_bias[:, None], targets.transpose(0, 2, 1)]
+            *kept, upstream, d_final, head_grad, head_bias_grad, loss_part = forward_head(ins, 2.0 / tokens_all)
         kept_all.append(kept)
-    final_mod = modulation[:, 6 * MODEL_WIDTH * LAYERS :]
-    norm_final = layer_norm(x)
-    shaped = (norm_final * (1 + final_mod[:, None, MODEL_WIDTH:]) + final_mod[:, None, :MODEL_WIDTH]).astype(jnp.bfloat16)
-    output = apply_rows(shaped, head_low) + head_bias
-    error_vals = output - targets
-    loss_part = jnp.sum(error_vals * error_vals)
-    tokens_all = devices * images * SEQ * PO
-    d_output = (error_vals * (2.0 / tokens_all)).astype(jnp.bfloat16)
-    head_grad = outer_sum(shaped, d_output)
-    head_bias_grad = column_sum(d_output)
-    d_shaped = apply_back(d_output, head_low)
-    d_final = jnp.concatenate([jnp.sum(d_shaped, 1), jnp.sum(d_shaped * norm_final, 1)], 1)
-    upstream = local_back(layer_norm, x, d_shaped * (1 + final_mod[:, None, MODEL_WIDTH:]))
     mod_grads, in_shards, out_shards = [None] * LAYERS, [None] * LAYERS, [None] * LAYERS
     in_bias_grads, out_bias_grads = [None] * LAYERS, [None] * LAYERS
     for i in reversed(range(LAYERS)):
-        mod = modulation[:, 6 * MODEL_WIDTH * i : 6 * MODEL_WIDTH * (i + 1)]
-        upstream, mod_grads[i], grad_in, grad_out, in_bias_grads[i], out_bias_grads[i] = backward_t(
-            upstream, mod, w_in[i], w_out[i], kept_all[i]
+        h1, qkv, probs, o, a, x1, h2, u, g, f = kept_all[i]
+        upstream, d_qkv, d_u, d_f, d_a, mod_grads[i], in_bias_grads[i], out_bias_grads[i] = backward_block(
+            block_mods[i], w_in[i], w_out[i], [upstream, starts[i], x1, probs, qkv, a, f, u]
         )
-        in_shards[i], out_shards[i] = scatter_grads([grad_in, grad_out], 5 + i)
+        grads = weight_grads([d_qkv, h1, d_u, h2, d_a, o, d_f, g])
+        in_shards[i], out_shards[i] = scatter_grads(grads, 5 + i)
     d_patch = upstream.astype(jnp.bfloat16)
-    patch_grad = outer_sum(latents, d_patch)
-    patch_bias_grad = column_sum(d_patch)
+    patch_grad = jnp.dot(latents.reshape(images * SEQ, PD).T, d_patch, preferred_element_type=jnp.float32)
+    patch_bias_grad = jnp.sum(d_patch.astype(jnp.float32), 0)
     d_modulation = jnp.concatenate(mod_grads + [d_final], 1)
     d_mods = d_modulation.reshape(images, devices, cond_cols).transpose(1, 0, 2)
-    small = jnp.concatenate(
-        [head_grad.reshape(-1), patch_grad.reshape(-1), patch_bias_grad] + in_bias_grads + out_bias_grads
-        + [head_bias_grad, loss_part[None]]
-    )
-    small = jnp.pad(small, (0, devices * 2048 - small.shape[0])).reshape(devices, 16, 128)
+    end_row = jnp.concatenate([head_bias_grad[:, 0], loss_part[0, :1], jnp.zeros((128 - PO - 1,), jnp.float32)])
+    rows = [
+        a.reshape(-1, 128) for a in [head_grad, patch_grad, patch_bias_grad] + in_bias_grads + out_bias_grads + [end_row]
+    ]
+    used = sum(a.shape[0] for a in rows)
+    small = jnp.concatenate(rows + [jnp.zeros((devices * 16 - used, 128), jnp.float32)], 0).reshape(devices, 16, 128)
     squares = sum(jnp.sum(shard * shard) for shard in in_shards + out_shards)
     g_cond, g_t1, g_t2, g_cls, merged = settle(
         [d_mods, small, w_t2, cond_t, pre, cond, hid_all, low_all, feat_all, lab_all, jnp.full((1, 128), squares)]
@@ -1316,7 +1614,7 @@
     flat = merged[:, :16].reshape(-1)
     sizes = [MODEL_WIDTH * PO, PD * MODEL_WIDTH, MODEL_WIDTH, LAYERS * IW, LAYERS * 2 * MODEL_WIDTH, PO, 1]
     places = [sum(sizes[:k]) for k in range(len(sizes) + 1)]
-    head_total = flat[: places[1]].reshape(MODEL_WIDTH, PO)
+    head_total = flat[: places[1]].reshape(PO, MODEL_WIDTH)
     patch_total = flat[places[1] : places[2]].reshape(PD, MODEL_WIDTH)
     loss_total = flat[places[6]]
     bias_total = jnp.concatenate(
@@ -1343,7 +1641,7 @@
         a.transpose(turn)
         for a in adam_step(out_t, out_m.transpose(turn), out_v.transpose(turn), jnp.stack(out_shards) * factor)
     ]
-    head_up = adam_step(head_w, head_m, head_v, head_total * factor)
+    head_up = [a.T for a in adam_step(head_t, head_m.T, head_v.T, head_total * factor)]
     bias_up = adam_step(biases, bias_m, bias_v, bias_total * factor)
     return (loss_total, grad_norm, *embed_up, *cond_up, *in_up, *out_up, *head_up, *bias_up)
 

time: 937 us -> 690 us (0.74)
  matrix products: 283 us -> 4.64 us
  Pallas kernels: 373 us -> 594 us
  other arithmetic: 121 us -> 23.2 us
  local copies, waits for them, and re-layouts: 138 us -> 48.3 us
    pallas_call x0 -> x6, Pallas kernels: none -> 221 us  [the longest x2 99.4 us: backward_block(): pl.pallas_call(backward_kernel, grid=(images,), out_shape=[jax.ShapeDtype...]
    dot_general x32 -> x1, matrix products: 221 us -> 2.27 us  [body(): jnp.dot(latents.reshape(images * SEQ, PD).T, d_patch, preferred_element_t...]
    reduce_sum x23 -> x1, other arithmetic: 63.2 us -> 2.19 us  [body(): patch_bias_grad = jnp.sum(d_patch.astype(jnp.float32), 0)]
    dot_general x9 -> x1, matrix products: 61.9 us -> 2.37 us  [rows_t(): jnp.einsum('bsd,ed->bse', left, right, preferred_element_type=jnp.float32)]
    concatenate x4 -> x1, other arithmetic: 20.2 us -> 0.99 us  [body(): d_modulation = jnp.concatenate(mod_grads + [d_final], 1)]
    slice x11 -> x10, local copies, waits for them, and re-layouts: 23.9 us -> 5.07 us  [the longest x3 1.25 us: body(): block_input_bias[i][None]]
    dot_general x5 -> x0, local copies, waits for them, and re-layouts: 17.7 us -> none  [the longest x4 14.1 us: back_t(): jnp.einsum('bse,ed->bsd', left, right, preferred_element_type=jnp.float32)]
    reshape x9 -> x4, local copies, waits for them, and re-layouts: 17.3 us -> 0.22 us  [the longest x1 0.21 us: body(): mods.transpose(1, 0, 2).reshape(images, 6 * LAYERS + 2, MODEL_WIDTH)]
where the time goes in v2:
time: 690 us; the launch traced here: 678 us
  Pallas kernels  594 us (86%)
  local copies, waits for them, and re-layouts  48.3 us (7%)
  other arithmetic  23.2 us (3%)
  between operations  8.16 us (1%)
    pallas_call x2, Pallas kernels, scatter_grads(): pl.pallas_call(scatter_kernel, out_shape=[jax.ShapeDtypeStruct(shape, jnp...  158 us
    pallas_call x1, Pallas kernels, gather_weights(): pl.pallas_call(functools.partial(gather_kernel, len(pairs)), out_shape=[j...  123 us
    pallas_call x2, Pallas kernels, backward_block(): pl.pallas_call(backward_kernel, grid=(images,), out_shape=[jax.ShapeDtype...  99.4 us
    pallas_call x1, Pallas kernels, settle(): pl.pallas_call(functools.partial(settle_kernel, devices), out_shape=[jax....  51.4 us
    pallas_call x1, Pallas kernels, forward_head(): pl.pallas_call(functools.partial(head_kernel, scale_out), grid=(images,),...  42.5 us
    pallas_call x2, Pallas kernels, weight_grads(): pl.pallas_call(grads_kernel, out_shape=[jax.ShapeDtypeStruct((IW, MODEL_W...  41.1 us
    pallas_call x1, Pallas kernels, modulate(): pl.pallas_call(functools.partial(modulate_kernel, devices), out_shape=[ja...  40.1 us
    pallas_call x1, Pallas kernels, forward_block(): pl.pallas_call(forward_kernel, grid=(images,), out_shape=shapes + [jax.Sh...  38.1 us

profile of v2, /device:TPU:0, one launch (start us, length us, event | category | flops | bytes accessed | tf_op | source)
XLA Modules:
  0.0 678.4 jit_solution(18155296258746922784)
XLA Ops:
  0.7 0.8 fusion.25
  1.7 0.8 slice.134
  2.6 0.7 slice.167
  3.4 0.7 convert_element_type.24
  4.2 0.7 convert_element_type.26
  5.0 0.9 slice.169.refs_2_
  5.9 1.0 slice.170
  6.9 0.7 slice.168.refs_1_
  7.6 1.2 copy-done.4
  8.8 40.1 %modulate.1 = (f32[32,4,336]{2,1,0:T(4,128)S(1)}, f32[24,128]{1,0:T(8,128)S(1)}, f32[24,128]{1,0:T(8,128)S(1)}, f32[768,128]{1,0:T(8,128)S(1)}, f32[768,128]{1,0...) custom-call(f32[4,512]{1,0:T(4,128)S(1)} %select_maximum_fusion.refs_0_, ...), custom_call_target="tpu_custom_call" | custom-call | tf_op jit(solution)/shard_map/modulate/pallas_call | solution.py:1029
  48.9 0.7 copy-done.10
  49.6 0.7 copy-done.12
  50.4 0.7 copy-done.14
  51.0 0.6 copy-done.20
  53.1 0.8 broadcast_in_dim.24
  53.8 0.8 broadcast_in_dim.25
  54.7 2.4 bitcast_add_fusion
  57.3 0.7 fusion.22
  58.2 123.1 %gather_weights.1 = (bf16[5376,768]{1,0:T(8,128)(2,1)S(1)}, bf16[768,3840]{1,0:T(8,128)(2,1)S(1)}, bf16[5376,768]{1,0:T(8,128)(2,1)S(1)}, bf16[768,3840]{1,0:T(8,128)(2,1)S(1)}) custom-call(f32[168,768]{1,0:T(8,128)S(1)} %get-tuple-element.169.refs_0_, f32[24,3840]{1,0:T(8,128)S(1)} %get-tuple-element.171.refs_1_, ...), custom_call_target="tpu_custom_call" | custom-call | tf_op jit(solution)/shard_map/gather_weights/pallas_call | solution.py:658
  181.3 3.2 copy-done
  184.5 3.2 copy-done.1
  187.7 2.5 copy-done.2
  190.2 2.6 copy-done.3
  194.0 38.1 %forward_block.1 = (bf16[1024,768]{1,0:T(8,128)(2,1)}, bf16[1024,2304]{1,0:T(8,128)(2,1)}, bf16[4,12,256,256]{3,2,1,0:T(8,128)(2,1)}, bf16[1024,768]{1,0:T(8,128...) custom-call(f32[1024,768]{1,0:T(8,128)} %bitcast.160, ...), custom_call_target="tpu_custom_call" | custom-call | tf_op jit(solution)/shard_map/forward_block/pallas_call | solution.py:1343
  233.9 0.7 copy.48.b_head
  234.6 42.5 %forward_head.1 = (bf16[1024,768]{1,0:T(8,128)(2,1)}, bf16[1024,2304]{1,0:T(8,128)(2,1)}, bf16[4,12,256,256]{3,2,1,0:T(8,128)(2,1)}, bf16[1024,768]{1,0:T(8,128)...) custom-call(f32[1024,768]{1,0:T(8,128)} %get-tuple-element.93.x.refs, ...), custom_call_target="tpu_custom_call" | custom-call | tf_op jit(solution)/shard_map/forward_head/pallas_call | solution.py:1359
  277.1 49.6 %backward_block.2 = (f32[1024,768]{1,0:T(8,128)}, bf16[1024,2304]{1,0:T(8,128)(2,1)}, bf16[1024,3072]{1,0:T(8,128)(2,1)}, bf16[1024,768]{1,0:T(8,128)(2,1)}, bf1...) custom-call(f32[4,6,768]{2,1,0:T(8,128)} %get-tuple-element.180.mod, ...), custom_call_target="tpu_custom_call" | custom-call | tf_op jit(solution)/shard_map/backward_block/pallas_call | solution.py:1461
  326.8 49.8 %backward_block.3 = (f32[1024,768]{1,0:T(8,128)}, bf16[1024,2304]{1,0:T(8,128)(2,1)}, bf16[1024,3072]{1,0:T(8,128)(2,1)}, bf16[1024,768]{1,0:T(8,128)(2,1)}, bf1...) custom-call(f32[4,6,768]{2,1,0:T(8,128)} %get-tuple-element.181.mod, ...), custom_call_target="tpu_custom_call" | custom-call | tf_op jit(solution)/shard_map/backward_block/pallas_call | solution.py:1461
  376.6 20.5 %weight_grads.2 = (bf16[5376,768]{1,0:T(8,128)(2,1)}, bf16[768,3840]{1,0:T(8,128)(2,1)}) custom-call(bf16[1024,2304]{1,0:T(8,128)(2,1)} %get-tuple-element.125.refs_0_, bf16[1024,768]{1,0:T(8,128)(2,1)} %get-tuple-element.126.refs_1_, bf16[1024,3072]{1,0:T(8,128)(2,1)} %get-tuple-element.127.refs_2_, bf16[1024,768]{1,0:T(8,128)(2,1)} %get-tuple-element.128.refs_3_, ...), custom_call_target="tpu_custom_call" | custom-call | tf_op jit(solution)/shard_map/weight_grads/pallas_call | solution.py:1508
  397.1 2.7 copy-done.6
  399.8 74.1 %scatter_grads.2 = (f32[168,768]{1,0:T(8,128)S(1)}, f32[24,3840]{1,0:T(8,128)S(1)}) custom-call(bf16[5376,768]{1,0:T(8,128)(2,1)} %get-tuple-element.133.refs_0_, bf16[768,3840]{1,0:T(8,128)(2,1)S(1)} %copy-done.6), custom_call_target="tpu_custom_call" | custom-call | tf_op jit(solution)/shard_map/scatter_grads/pallas_call | solution.py:883
  473.9 20.6 %weight_grads.3 = (bf16[5376,768]{1,0:T(8,128)(2,1)}, bf16[768,3840]{1,0:T(8,128)(2,1)}) custom-call(bf16[1024,2304]{1,0:T(8,128)(2,1)} %get-tuple-element.136.refs_0_, bf16[1024,768]{1,0:T(8,128)(2,1)} %get-tuple-element.137.refs_1_, bf16[1024,3072]{1,0:T(8,128)(2,1)} %get-tuple-element.138.refs_2_, bf16[1024,768]{1,0:T(8,128)(2,1)} %get-tuple-element.139.refs_3_, ...), custom_call_target="tpu_custom_call" | custom-call | tf_op jit(solution)/shard_map/weight_grads/pallas_call | solution.py:1508
  494.5 2.7 copy-done.7
  497.2 84.2 %scatter_grads.3 = (f32[168,768]{1,0:T(8,128)S(1)}, f32[24,3840]{1,0:T(8,128)S(1)}) custom-call(bf16[5376,768]{1,0:T(8,128)(2,1)} %get-tuple-element.144.refs_0_, bf16[768,3840]{1,0:T(8,128)(2,1)S(1)} %copy-done.7), custom_call_target="tpu_custom_call" | custom-call | tf_op jit(solution)/shard_map/scatter_grads/pallas_call | solution.py:883
  581.4 0.7 multiply_reduce_fusion
  583.5 0.7 multiply_reduce_fusion.3
  584.8 0.7 multiply_reduce_fusion.2
  586.7 1.2 slice.154
  588.0 0.7 maximum_bitcast_fusion
  588.7 2.3 convolution_bitcast_fusion
  591.1 2.2 convert_reduce_fusion
  593.5 0.6 concatenate.30
  594.1 1.0 pad_maximum_fusion.1
  595.5 1.0 copy-done.11
  596.5 1.0 copy-done.13
  597.4 0.9 copy-done.15
  598.4 0.8 copy-done.21
  599.2 0.7 copy-done.23
  599.9 0.7 copy-done.25
  600.6 0.7 copy-done.26
  601.3 51.4 %settle.1 = (f32[336,768]{1,0:T(8,128)S(1)}, f32[24,256]{1,0:T(8,128)S(1)}, f32[24,768]{1,0:T(8,128)S(1)}, f32[24,1024]{1,0:T(8,128)S(1)}, f32[32,24,128]{2,1,0:T(8,128)S(1)}) custom-call(f32[32,4,336]{2,1,0:T(4,128)S(1)} %bitcast.157, f32[32,16,128]{2,1,0:T(8,128)S(1)} %bitcast.156, f32[24,768]{1,0:T(8,128)S(1)} %slice.169.refs_2_, ...), custom_call_target="tpu_custom_call" | custom-call | tf_op jit(solution)/shard_map/settle/pallas_call | solution.py:1147
  652.7 1.0 copy-done.8
  653.7 0.6 copy-done.16
  654.3 0.6 copy-done.18
  655.3 0.7 copy-done.36
  656.1 0.8 slice_dynamic-update-slice_fusion
  658.2 0.6 slice_reduce_fusion.2
  662.1 1.8 multiply_subtract_fusion
  664.0 1.9 fusion.16
  665.9 3.5 fusion.17
  669.4 2.4 fusion.15
  671.9 2.4 fusion.5
  674.7 1.0 fusion.13
  675.6 1.3 slice.179
  (134 shorter events, 9.4 us)
Async XLA Ops:
  0.7 54.0 %copy-start.39 = (bf16[4,256,16]{1,2,0:T(8,128)(2,1)S(1)}, bf16[4,256,16]{1,2,0:T(8,128)(2,1)}, u32[]{:S(2)}) copy-start(bf16[4,256,16]{1,2,0:T(8,128)(2,1)} %param.23) | copy-start | bytes 98308
  7.6 1.2 copy-start.4
  48.9 0.7 copy-start.10
  49.6 0.7 copy-start.12
  50.4 0.7 copy-start.14
  51.0 0.6 copy-start.20
  51.7 0.6 copy-start.22
  52.3 0.6 copy-start.24
  54.6 3.4 copy-start.27
  54.7 3.4 copy-start.29
  57.1 135.6 %copy-start.35 = (f32[26912]{0:T(1024)S(1)}, f32[26912]{0:T(1024)}, u32[]{:S(2)}) copy-start(f32[26912]{0:T(1024)} %param.42) | copy-start | bytes 322948
  181.3 3.2 copy-start
  184.5 3.2 copy-start.1
  187.7 2.5 copy-start.2
  190.2 2.6 copy-start.3
  397.1 2.7 copy-start.6
  494.5 2.7 copy-start.7
  497.2 90.7 %copy-start.44 = (f32[32,128]{1,0:T(8,128)S(1)}, f32[32,128]{1,0:T(8,128)}, u32[]{:S(2)}) copy-start(f32[32,128]{1,0:T(8,128)} %get-tuple-element.117) | copy-start | bytes 49156
  581.4 9.6 %copy-start.43 = (f32[1,5376]{1,0:T(1,128)S(1)}, f32[1,5376]{1,0:T(1,128)}, u32[]{:S(2)}) copy-start(f32[1,5376]{1,0:T(1,128)} %get-tuple-element.113) | copy-start | bytes 64516
  581.4 9.7 %copy-start.46 = (f32[1,1536]{1,0:T(1,128)S(1)}, f32[1,1536]{1,0:T(1,128)}, u32[]{:S(2)}) copy-start(f32[1,1536]{1,0:T(1,128)} %get-tuple-element.115) | copy-start | bytes 18436
  588.7 4.6 copy-start.42
  588.7 4.7 copy-start.45
  588.7 4.7 copy-start.40
  588.7 5.4 copy-start.41
  591.0 4.4 copy-start.5
  595.5 1.0 copy-start.11
  596.5 1.0 copy-start.13
  597.4 0.9 copy-start.15
  598.4 0.8 copy-start.21
  599.2 0.7 copy-start.23
  599.9 0.7 copy-start.25
  600.6 0.7 copy-start.26
  652.7 1.0 copy-start.8
  653.7 0.6 copy-start.16
  654.3 0.6 copy-start.18
  655.3 0.7 copy-start.36
  664.0 5.4 copy-start.28
  664.0 5.4 copy-start.30
  664.0 5.4 copy-start.31
  669.4 2.5 copy-start.9
  669.4 2.5 copy-start.32
  669.4 2.5 copy-start.33
  671.9 2.7 copy-start.17
  671.9 2.7 copy-start.19
  671.9 2.8 copy-start.34
  671.9 2.8 copy-start.37
  671.9 2.8 copy-start.38

commit v3 on v2

--- a/solution.py
+++ b/solution.py
@@ -486,7 +486,7 @@
     def __init__(self, place, own, stage, piece, full, sems):
         self.p, self.own, self.stage, self.piece, self.full = place, own, stage, piece, full
         self.xch_send, self.xch_recv, self.local, self.send, self.recv, self.sib_recv = sems
-        self.sent, self.keep = [], []
+        self.sent = []
 
     def slot(self, a, chip):
         rows, half = self.piece[a].shape
@@ -495,12 +495,21 @@
         ]
 
     def push(self, a, k, src, chip, device, sem, cond=None):
-        copy = remote(src, self.slot(a, chip), self.send.at[a, k], sem, device)
-        self.sent.append((copy, cond))
-        if cond is None:
-            copy.start()
-        else:
-            pl.when(cond)(copy.start)
+        def act(what):
+            copy = remote(src(), self.slot(a, chip()), self.send.at[a, k], sem.at[a, chip()], device())
+            getattr(copy, what)()
+
+        def guarded(what):
+            if cond is None:
+                act(what)
+            else:
+                pl.when(cond())(functools.partial(act, what))
+
+        guarded("start")
+        self.sent.append(functools.partial(guarded, "wait_send"))
+
+    def store_own(self, a):
+        return pltpu.make_async_copy(self.piece[a], self.slot(a, self.p.chip), self.local.at[a])
 
     def begin(self):
         core = self.p.core
@@ -525,60 +534,62 @@
             copies[a][0].wait()
             copies[a][1].wait()
             self.piece[a][...] = self.stage[a][...].astype(jnp.bfloat16)
-            keep = pltpu.make_async_copy(self.piece[a], self.slot(a, self.p.chip), self.local.at[a])
-            keep.start()
-            self.keep.append(keep)
+            self.store_own(a).start()
+            piece, here = (lambda a=a: self.piece[a]), (lambda: self.p.chip)
             for sign in (-1, 1):
                 self.push(
-                    a, 0 if sign < 0 else 3, self.piece[a], self.p.chip, self.p.me + 8 * sign,
-                    self.recv.at[a, self.p.chip], self.p.valid(sign),
+                    a, 0 if sign < 0 else 3, piece, here, lambda sign=sign: self.p.me + 8 * sign, self.recv,
+                    lambda sign=sign: self.p.valid(sign),
                 )
-            self.push(a, 6, self.piece[a], self.p.chip, self.p.dev_a, self.recv.at[a, self.p.chip])
-            self.push(a, 10, self.piece[a], self.p.chip, self.p.dev_b, self.recv.at[a, self.p.chip])
-            self.push(a, 18, self.piece[a], self.p.chip, self.p.sibling, self.sib_recv.at[a, self.p.chip])
+            self.push(a, 6, piece, here, lambda: self.p.dev_a, self.recv)
+            self.push(a, 10, piece, here, lambda: self.p.dev_b, self.recv)
+            self.push(a, 18, piece, here, lambda: self.p.sibling, self.sib_recv)
 
     def arrive(self, a, chip):
         slot = self.slot(a, chip)
         pltpu.make_async_copy(slot, slot, self.recv.at[a, chip]).wait()
 
+    def pass_on(self, dz, flip_a, flip_b, targets):
+        def here():
+            return self.p.valid(dz)
+
+        def chip():
+            return self.p.other(dz, flip_a, flip_b)
+
+        for a in range(2):
+            pl.when(here())(lambda a=a: self.arrive(a, chip()))
+            for k, device, sem, extra in targets:
+                self.push(
+                    a, k, lambda a=a: self.slot(a, chip()), chip, device, sem,
+                    here if extra is None else lambda extra=extra: jnp.logical_and(here(), self.p.valid(extra)),
+                )
+
     def z_step(self, dist):
         for sign in (-1, 1):
-            here = self.p.valid(sign * dist)
-            chip = self.p.other(sign * dist)
             rel = (sign * dist) % 4
-            onward = jnp.logical_and(here, self.p.valid(-sign))
-            for a in range(2):
-                pl.when(here)(functools.partial(self.arrive, a, chip))
-                src = self.slot(a, chip)
-                if dist < 3:
-                    self.push(
-                        a, (0 if sign > 0 else 3) + dist, src, chip, self.p.me - 8 * sign,
-                        self.recv.at[a, chip], onward,
-                    )
-                self.push(a, 6 + rel, src, chip, self.p.dev_a, self.recv.at[a, chip], here)
-                self.push(a, 10 + rel, src, chip, self.p.dev_b, self.recv.at[a, chip], here)
-                self.push(a, 18 + rel, src, chip, self.p.sibling, self.sib_recv.at[a, chip], here)
+            targets = [
+                (6 + rel, lambda: self.p.dev_a, self.recv, None),
+                (10 + rel, lambda: self.p.dev_b, self.recv, None),
+                (18 + rel, lambda: self.p.sibling, self.sib_recv, None),
+            ]
+            if dist < 3:
+                onward = ((0 if sign > 0 else 3) + dist, lambda sign=sign: self.p.me - 8 * sign, self.recv, -sign)
+                targets.insert(0, onward)
+            self.pass_on(sign * dist, 0, 0, targets)
 
     def a_step(self, dist):
         for sign in (-1, 1) if dist else (1,):
-            here = self.p.valid(sign * dist)
-            chip = self.p.other(sign * dist, 1)
             rel = (sign * dist) % 4
-            for a in range(2):
-                pl.when(here)(functools.partial(self.arrive, a, chip))
-                src = self.slot(a, chip)
-                self.push(a, 14 + rel, src, chip, self.p.dev_b, self.recv.at[a, chip], here)
-                self.push(a, 22 + rel, src, chip, self.p.sibling, self.sib_recv.at[a, chip], here)
+            self.pass_on(sign * dist, 1, 0, [
+                (14 + rel, lambda: self.p.dev_b, self.recv, None), (22 + rel, lambda: self.p.sibling, self.sib_recv, None)
+            ])
 
     def b_step(self, dist, flip_a):
         for sign in (-1, 1) if dist else (1,):
-            here = self.p.valid(sign * dist)
-            chip = self.p.other(sign * dist, flip_a, 1)
             rel = (sign * dist) % 4
-            for a in range(2):
-                pl.when(here)(functools.partial(self.arrive, a, chip))
-                src = self.slot(a, chip)
-                self.push(a, 26 + 4 * flip_a + rel, src, chip, self.p.sibling, self.sib_recv.at[a, chip], here)
+            self.pass_on(
+                sign * dist, flip_a, 1, [(26 + 4 * flip_a + rel, lambda: self.p.sibling, self.sib_recv, None)]
+            )
 
     def finish(self):
         for a in range(2):
@@ -593,13 +604,9 @@
                 return carry
 
             lax.fori_loop(0, 16, take, 0)
-        for copy in self.keep:
-            copy.wait()
-        for copy, cond in self.sent:
-            if cond is None:
-                copy.wait_send()
-            else:
-                pl.when(cond)(copy.wait_send)
+            self.store_own(a).wait()
+        for wait in self.sent:
+            wait()
 
 
 GATHER_SEMS = [
@@ -624,64 +631,22 @@
     return [(2 * rows, width // 2) for rows, width in shapes]
 
 
-def gather_kernel(layers, *refs):
-    own, refs = refs[: 2 * layers], refs[2 * layers :]
-    full, refs = refs[: 2 * layers], refs[2 * layers :]
-    place = Place()
-    place.greet()
-    jobs = []
-    for layer in range(layers):
-        part = refs[10 * layer : 10 * layer + 10]
-        jobs.append(
-            Gather(place, own[2 * layer : 2 * layer + 2], part[:2], part[2:4], full[2 * layer : 2 * layer + 2], part[4:])
-        )
-    for job in jobs:
-        job.begin()
-        job.a_step(0)
-        for dist in (1, 2, 3):
-            job.z_step(dist)
-            job.a_step(dist)
-    for job in jobs:
-        for dist in range(4):
-            job.b_step(dist, 0)
-            job.b_step(dist, 1)
-    for job in jobs:
-        job.finish()
-
-
-def gather_weights(pairs, collective):
-    flat = [array for pair in pairs for array in pair]
-    devices = lax.axis_size(AXIS)
-    scratch = []
-    for pair in pairs:
-        scratch += gather_scratch(piece_shapes([array.shape for array in pair]))
-    return pl.pallas_call(
-        functools.partial(gather_kernel, len(pairs)),
-        out_shape=[jax.ShapeDtypeStruct((devices * a.shape[0], a.shape[1]), jnp.bfloat16) for a in flat],
-        in_specs=[pl.BlockSpec(memory_space=pltpu.VMEM)] * len(flat),
-        out_specs=[pl.BlockSpec(memory_space=pl.ANY)] * len(flat),
-        scratch_shapes=scratch,
-        compiler_params=pltpu.CompilerParams(
-            collective_id=collective, has_side_effects=True, vmem_limit_bytes=24 << 20
-        ),
-        name="gather_weights",
-    )(*flat)
-
-
 ORDER = (3, 0, 2, 1)
 
 
 class Scatter:
-    def __init__(self, place, grad, total, bufs, sems):
-        self.p, self.grad, self.total = place, grad, total
-        self.mine, self.sib, self.from_b, self.from_a, self.up, self.down, self.part, self.last = (
-            bufs[2 * i : 2 * i + 2] for i in range(8)
+    def __init__(self, place, grads, totals, bufs, sems, mine=None):
+        self.p, self.grad, self.total, self.mine = place, grads, totals, mine
+        count = len(grads)
+        self.arrays = range(count)
+        self.sib, self.from_b, self.from_a, self.line, self.part, self.last = (
+            bufs[count * i : count * i + count] for i in range(6)
         )
         (self.load_sem, self.sib_send, self.sib_recv, self.b_send, self.b_recv, self.a_send, self.a_recv, self.up_send,
          self.up_recv, self.down_send, self.down_recv, self.end_send, self.end_recv, self.end_local) = sems
 
     def rows_of(self, a, chip, core):
-        _, rows, half = self.mine[a].shape
+        rows, half = self.part[a].shape
         return self.grad[a].at[
             pl.ds(pl.multiple_of(chip * rows, rows), rows), pl.ds(pl.multiple_of(core * half, half), half)
         ]
@@ -689,10 +654,16 @@
     def chip_of(self, z, flip_a, flip_b):
         return self.p.other(z - self.p.z, flip_a, flip_b)
 
+    def own(self, a, flip_b, flip_a, z):
+        if self.mine is None:
+            return self.rows_of(a, self.chip_of(z, flip_a, flip_b), self.p.core)
+        return self.mine[a].at[8 * flip_b + 4 * flip_a + z]
+
     def load(self, a, flip_b, flip_a, z):
-        k = 8 * flip_b + 4 * flip_a + z
         return pltpu.make_async_copy(
-            self.rows_of(a, self.chip_of(z, flip_a, flip_b), self.p.core), self.mine[a].at[k], self.load_sem.at[a, k]
+            self.rows_of(a, self.chip_of(z, flip_a, flip_b), self.p.core),
+            self.own(a, flip_b, flip_a, z),
+            self.load_sem.at[a, 8 * flip_b + 4 * flip_a + z],
         )
 
     def lend(self, a, flip_b, flip_a, z):
@@ -708,57 +679,54 @@
     def to_b(self, a, flip_a, z):
         k = 4 * flip_a + z
         return remote(
-            self.mine[a].at[8 + k], self.from_b[a].at[k], self.b_send.at[a, k], self.b_recv.at[a, k], self.p.dev_b
+            self.own(a, 1, flip_a, z), self.from_b[a].at[k], self.b_send.at[a, k], self.b_recv.at[a, k], self.p.dev_b
         )
 
     def to_a(self, a, z):
         return remote(
-            self.mine[a].at[4 + z], self.from_a[a].at[z], self.a_send.at[a, z], self.a_recv.at[a, z], self.p.dev_a
+            self.own(a, 0, 1, z), self.from_a[a].at[z], self.a_send.at[a, z], self.a_recv.at[a, z], self.p.dev_a
         )
 
-    def to_z(self, a, z, sign):
-        dst, send, recv = (
-            (self.up, self.up_send, self.up_recv) if sign > 0 else (self.down, self.down_send, self.down_recv)
+    def to_z(self, a, z, sign, slot):
+        send, recv = (self.up_send, self.up_recv) if sign > 0 else (self.down_send, self.down_recv)
+        return remote(
+            self.own(a, 0, 0, z), self.line[a].at[slot], send.at[a, z], recv.at[a, z], self.p.me + 8 * sign
         )
-        return remote(self.mine[a].at[z], dst[a].at[z], send.at[a, z], recv.at[a, z], self.p.me + 8 * sign)
-
-    def each(self, step):
-        def run(z, carry):
-            for a in range(2):
-                step(a, z)
-            return carry
-
-        lax.fori_loop(0, 4, run, 0)
-
-    def begin(self):
+
+    def open(self, z):
+        for flip_b, flip_a in ((1, 1), (1, 0), (0, 1), (0, 0)):
+            for a in self.arrays:
+                self.lend(a, flip_b, flip_a, z).start()
+                if self.mine is not None:
+                    self.load(a, flip_b, flip_a, z).start()
+
+    def open_all(self):
         for z in ORDER:
-            for flip_b, flip_a in ((1, 1), (1, 0), (0, 1), (0, 0)):
-                for a in range(2):
-                    self.lend(a, flip_b, flip_a, z).start()
-                    self.load(a, flip_b, flip_a, z).start()
+            self.open(z)
 
     def pair(self, a, flip_b, flip_a, z):
+        if self.mine is not None:
+            self.load(a, flip_b, flip_a, z).wait()
+        self.lend(a, flip_b, flip_a, z).wait_recv()
         k = 8 * flip_b + 4 * flip_a + z
-        self.load(a, flip_b, flip_a, z).wait()
-        self.lend(a, flip_b, flip_a, z).wait_recv()
-        return self.mine[a][k].astype(jnp.float32) + self.sib[a][k].astype(jnp.float32)
+        return self.own(a, flip_b, flip_a, z)[...].astype(jnp.float32) + self.sib[a][k].astype(jnp.float32)
 
     def cross_b(self, z):
         for flip_a in (1, 0):
-            for a in range(2):
-                self.mine[a][8 + 4 * flip_a + z] = self.pair(a, 1, flip_a, z).astype(jnp.bfloat16)
+            for a in self.arrays:
+                self.own(a, 1, flip_a, z)[...] = self.pair(a, 1, flip_a, z).astype(jnp.bfloat16)
                 self.to_b(a, flip_a, z).start()
 
     def cross_a(self, z):
-        for a in range(2):
+        for a in self.arrays:
             value = self.pair(a, 0, 1, z)
             self.to_b(a, 1, z).wait_recv()
-            self.mine[a][4 + z] = (value + self.from_b[a][4 + z].astype(jnp.float32)).astype(jnp.bfloat16)
+            self.own(a, 0, 1, z)[...] = (value + self.from_b[a][4 + z].astype(jnp.float32)).astype(jnp.bfloat16)
             self.to_a(a, z).start()
 
     def along_z(self, z):
         place = self.p
-        for a in range(2):
+        for a in self.arrays:
             value = self.pair(a, 0, 0, z)
             self.to_b(a, 0, z).wait_recv()
             value = value + self.from_b[a][z].astype(jnp.float32)
@@ -767,25 +735,29 @@
 
             @pl.when(jnp.logical_and(place.z < z, place.z > 0))
             def _():
-                self.to_z(a, z, 1).wait_recv()
-                self.part[a][...] += self.up[a][z].astype(jnp.float32)
+                self.to_z(a, z, 1, z).wait_recv()
+                self.part[a][...] += self.line[a][z].astype(jnp.float32)
 
             @pl.when(jnp.logical_and(place.z > z, place.z < 3))
             def _():
-                self.to_z(a, z, -1).wait_recv()
-                self.part[a][...] += self.down[a][z].astype(jnp.float32)
+                self.to_z(a, z, -1, z).wait_recv()
+                self.part[a][...] += self.line[a][z].astype(jnp.float32)
 
             @pl.when(place.z != z)
             def _():
-                self.mine[a][z] = self.part[a][...].astype(jnp.bfloat16)
+                self.own(a, 0, 0, z)[...] = self.part[a][...].astype(jnp.bfloat16)
 
             @pl.when(place.z < z)
             def _():
-                self.to_z(a, z, 1).start()
-
-            @pl.when(place.z > z)
+                self.to_z(a, z, 1, z).start()
+
+            @pl.when(place.z > z + 1)
             def _():
-                self.to_z(a, z, -1).start()
+                self.to_z(a, z, -1, z).start()
+
+            @pl.when(place.z == z + 1)
+            def _():
+                self.to_z(a, z, -1, 4).start()
 
             @pl.when(place.z == z)
             def _():
@@ -809,88 +781,72 @@
 
     def close(self):
         place = self.p
-        for a in range(2):
+        for a in self.arrays:
 
             @pl.when(place.z > 0)
             def _():
-                self.to_z(a, place.z, 1).wait_recv()
-                self.last[a][...] += self.up[a][place.z].astype(jnp.float32)
+                self.to_z(a, place.z, 1, place.z).wait_recv()
+                self.last[a][...] += self.line[a][place.z].astype(jnp.float32)
 
             @pl.when(place.z < 3)
             def _():
-                self.to_z(a, place.z, -1).wait_recv()
-                self.last[a][...] += self.down[a][place.z].astype(jnp.float32)
+                self.to_z(a, place.z, -1, 4).wait_recv()
+                self.last[a][...] += self.line[a][4].astype(jnp.float32)
 
             for copy in self.end_copies(a):
                 copy.start()
 
-    def finish(self):
-        for a in range(2):
+    def end(self):
+        for a in self.arrays:
             for copy in self.end_copies(a):
                 copy.wait()
 
-        def step(a, z):
-            for flip_b in range(2):
+    def finish(self):
+        def step(z, carry):
+            for a in self.arrays:
+                for flip_b in range(2):
+                    for flip_a in range(2):
+                        self.lend(a, flip_b, flip_a, z).wait_send()
                 for flip_a in range(2):
-                    self.lend(a, flip_b, flip_a, z).wait_send()
-            for flip_a in range(2):
-                self.to_b(a, flip_a, z).wait_send()
-            self.to_a(a, z).wait_send()
-
-            @pl.when(self.p.z < z)
-            def _():
-                self.to_z(a, z, 1).wait_send()
-
-            @pl.when(self.p.z > z)
-            def _():
-                self.to_z(a, z, -1).wait_send()
-
-        self.each(step)
+                    self.to_b(a, flip_a, z).wait_send()
+                self.to_a(a, z).wait_send()
+
+                @pl.when(self.p.z < z)
+                def _():
+                    self.to_z(a, z, 1, z).wait_send()
+
+                @pl.when(self.p.z > z)
+                def _():
+                    self.to_z(a, z, -1, z).wait_send()
+
+            return carry
+
+        lax.fori_loop(0, 4, step, 0)
 
     def steps(self):
-        yield self.begin
+        out = []
         for k in range(6):
             if k < 4:
-                yield functools.partial(self.cross_b, ORDER[k])
+                out.append(functools.partial(self.cross_b, ORDER[k]))
             if 0 <= k - 1 < 4:
-                yield functools.partial(self.cross_a, ORDER[k - 1])
+                out.append(functools.partial(self.cross_a, ORDER[k - 1]))
             if 0 <= k - 2 < 4:
-                yield functools.partial(self.along_z, ORDER[k - 2])
-        yield self.close
-        yield self.finish
+                out.append(functools.partial(self.along_z, ORDER[k - 2]))
+        return out + [self.close, self.end, self.finish]
 
 
 def scatter_scratch(shapes):
     scratch = []
-    for count, kind in ((16, jnp.bfloat16), (16, jnp.bfloat16), (8, jnp.bfloat16), (4, jnp.bfloat16), (4, jnp.bfloat16),
-                        (4, jnp.bfloat16), (0, jnp.float32), (0, jnp.float32)):
+    for count, kind in ((16, jnp.bfloat16), (8, jnp.bfloat16), (4, jnp.bfloat16), (5, jnp.bfloat16),
+                        (0, jnp.float32), (0, jnp.float32)):
         scratch += [pltpu.VMEM(((count,) if count else ()) + shape, kind) for shape in shapes]
     counts = (16, 16, 16, 8, 8, 4, 4, 4, 4, 4, 4)
-    return scratch + [pltpu.SemaphoreType.DMA((2, n)) for n in counts] + [pltpu.SemaphoreType.DMA((2,))] * 3
-
-
-def scatter_kernel(*refs):
-    grad, total, bufs, sems = refs[:2], refs[2:4], refs[4:20], refs[20:]
-    place = Place()
-    place.greet()
-    for step in Scatter(place, grad, total, bufs, sems).steps():
-        step()
-
-
-def scatter_grads(grads, collective):
-    devices = lax.axis_size(AXIS)
-    shapes = [(a.shape[0] // devices, a.shape[1]) for a in grads]
-    return pl.pallas_call(
-        scatter_kernel,
-        out_shape=[jax.ShapeDtypeStruct(shape, jnp.float32) for shape in shapes],
-        in_specs=[pl.BlockSpec(memory_space=pl.ANY)] * 2,
-        out_specs=[pl.BlockSpec(memory_space=pltpu.VMEM)] * 2,
-        scratch_shapes=scatter_scratch(piece_shapes(shapes)),
-        compiler_params=pltpu.CompilerParams(
-            collective_id=collective, has_side_effects=True, vmem_limit_bytes=40 << 20
-        ),
-        name="scatter_grads",
-    )(*grads)
+    several = len(shapes)
+    return (
+        scratch
+        + [pltpu.SemaphoreType.DMA((several, n)) for n in counts]
+        + [pltpu.SemaphoreType.DMA((several,))] * 3
+    )
 
 
 def dot_nt(left, right):
@@ -1011,64 +967,62 @@
     return [first, second, third, fourth, last]
 
 
-def modulate_kernel(devices, *refs):
-    greet_all(devices)
-    for step in modulate_steps(devices, refs[:8], refs[8:16], refs[16:19], refs[19:]):
-        step()
-
-
-def modulate(ins):
-    devices = lax.axis_size(AXIS)
-    msg, wt1, wt2, wcls, wcond = ins[:5]
-    cols, images = wt1.shape[0], devices * msg.shape[0]
-    outs = [
-        (devices, msg.shape[0], wcond.shape[0]), (cols, images), (cols, images), (devices * cols, images),
-        (devices * cols, images), (images, FREQ), (images, 128), (devices,) + msg.shape,
-    ]
-    padded = -(-cols // 16) * 16
-    return pl.pallas_call(
-        functools.partial(modulate_kernel, devices),
-        out_shape=[jax.ShapeDtypeStruct(shape, jnp.float32) for shape in outs],
-        in_specs=[pl.BlockSpec(memory_space=pltpu.VMEM)] * 8,
-        out_specs=[pl.BlockSpec(memory_space=pltpu.VMEM)] * 8,
-        scratch_shapes=[
-            pltpu.VMEM((devices, padded, images), jnp.bfloat16),
-            pltpu.VMEM((devices, padded, images), jnp.bfloat16),
-            pltpu.VMEM((devices, msg.shape[0], wcond.shape[0]), jnp.float32),
-            pltpu.SemaphoreType.DMA((4, devices)),
-            pltpu.SemaphoreType.DMA((4, devices)),
-        ],
-        compiler_params=pltpu.CompilerParams(collective_id=3, has_side_effects=True, vmem_limit_bytes=24 << 20),
-        name="modulate",
-    )(*ins)
-
-
-def settle_steps(devices, ins, outs, bufs, sems):
-    d_mods, small, wt2, wcond, pre, cond, hid_all, low_all, feat_all, lab_all, squares = ins
+SETTLE_INS = ("d_mods", "wt2", "wcond", "pre", "cond", "hid_all", "low_all", "feat_all", "lab_all", "g_head", "g_hbias", "loss",
+              "g_patch", "g_pbias", "bin0", "bin1", "bout0", "bout1", "done_in", "done_out")
+
+
+def settle_steps(devices, ins, outs, bufs, sems, shards):
+    d_mods, pre, lab_all = ins["d_mods"], ins["pre"], ins["lab_all"]
     g_cond, g_t1, g_t2, g_cls, merged = outs
-    dm_got, dm_all, small_got, dc_part, dc_got, dh_part, dh_got, note = bufs
+    dm_got, dm_all, rows, small, small_got, dc_part, dc_got, dh_part, dh_got, note = bufs
     me = lax.axis_index(AXIS)
-    images, cols = d_mods.shape[1], wt2.shape[0]
-    width = d_mods.shape[2]
-
-    def rows_for(ref):
-        return lambda peer: ref.at[pl.ds(pl.multiple_of(peer * cols, 8), cols), :]
-
+    images, width = d_mods.shape[1:]
+    cols = pre.shape[0]
     swaps = [
         Swap(me, devices, 0, lambda peer: d_mods.at[peer], dm_got, *sems),
         Swap(me, devices, 1, lambda peer: small.at[peer], small_got, *sems),
-        Swap(me, devices, 2, rows_for(dc_part), dc_got, *sems),
-        Swap(me, devices, 3, rows_for(dh_part), dh_got, *sems),
+        Swap(me, devices, 2, lambda peer: dc_part.at[peer], dc_got, *sems),
+        Swap(me, devices, 3, lambda peer: dh_part.at[peer], dh_got, *sems),
         Swap(me, devices, 4, lambda peer: note, merged, *sems),
     ]
     keep = {}
 
+    def share(value, part, got):
+        pad = jnp.zeros((32 - cols, value.shape[1]), jnp.float32)
+        for j in range(devices):
+            part[j] = jnp.concatenate([value[cols * j : cols * (j + 1)], pad], 0).astype(jnp.bfloat16)
+        got[me] = part[me]
+
+    def collect(got):
+        return jnp.sum(got[...].astype(jnp.float32), 0)[:cols]
+
+    def parts_of(value):
+        return sum(
+            jnp.where(lax.broadcasted_iota(jnp.int32, (1, 128), 1) == k, part.astype(jnp.float32), 0.0)
+            for k, part in enumerate(thirds(value))
+        )
+
     def first():
         swaps[0].start()
+        dm_got[me] = d_mods[me]
+        dm_all[...] = jnp.zeros_like(dm_all)
+        rows[...] = jnp.zeros_like(rows)
+        for k in range(MODEL_WIDTH // 128):
+            span = slice(128 * k, 128 * (k + 1))
+            rows[16 * k : 16 * (k + 1), :] = ins["g_patch"][:, span]
+            rows[96 + 32 * k : 96 + 32 * (k + 1), :] = ins["g_head"][:, span]
+        at = 288
+        for name in ("g_pbias", "bin0", "bin1", "bout0", "bout1"):
+            for k in range(ins[name].shape[1] // 128):
+                rows[at : at + 1, :] = ins[name][:, 128 * k : 128 * (k + 1)]
+                at += 1
+        square = ins["g_hbias"].shape
+        diagonal = lax.broadcasted_iota(jnp.int32, square, 0) == lax.broadcasted_iota(jnp.int32, square, 1)
+        rows[at : at + 1, :] = jnp.sum(jnp.where(diagonal, ins["g_hbias"][...], 0.0), 0, keepdims=True)
+        for j in range(devices):
+            small[j] = rows[16 * j : 16 * (j + 1), :].astype(jnp.bfloat16)
         swaps[1].start()
-        dm_got[me] = d_mods[me]
         small_got[me] = small[me]
-        dm_all[...] = jnp.zeros_like(dm_all)
 
     def second():
         swaps[0].arrive()
@@ -1076,52 +1030,54 @@
             dm_all[images * j : images * (j + 1), :width] = dm_got[j]
         turned = dm_all[...].T[:width]
         parts = thirds(turned)
-        weight = wcond[...].astype(jnp.bfloat16)
-        dc_part[...] = sum(dot_tn(weight, part) for part in parts)
+        weight = ins["wcond"][...].astype(jnp.bfloat16)
+        share(sum(dot_tn(weight, part) for part in parts), dc_part, dc_got)
         swaps[2].start()
-        mine = pl.ds(pl.multiple_of(me * cols, 8), cols)
-        dc_got[me] = dc_part[mine, :]
-        low = low_all[...].astype(jnp.bfloat16)
+        low = ins["low_all"][...].astype(jnp.bfloat16)
         g_cond[...] = sum(dot_nt(part, low) for part in parts)
         swaps[1].arrive()
 
     def third():
         swaps[2].arrive()
-        d_cond = jnp.sum(dc_got[...], 0) * silu_slope(cond[...])
+        d_cond = collect(dc_got) * silu_slope(ins["cond"][...])
         parts = thirds(d_cond)
-        weight = wt2[...].astype(jnp.bfloat16)
-        dh_part[...] = sum(dot_tn(weight, part) for part in parts)
+        weight = ins["wt2"][...].astype(jnp.bfloat16)
+        share(sum(dot_tn(weight, part) for part in parts), dh_part, dh_got)
         swaps[3].start()
-        mine = pl.ds(pl.multiple_of(me * cols, 8), cols)
-        dh_got[me] = dh_part[mine, :]
         classes = lax.broadcasted_iota(jnp.int32, (lab_all.shape[0], g_cls.shape[1]), 1).astype(jnp.float32)
         labels = jnp.concatenate([lab_all[...]] * (g_cls.shape[1] // 128), 1)
         onehot = (labels == classes).astype(jnp.bfloat16)
         g_cls[...] = sum(jnp.dot(part, onehot, preferred_element_type=jnp.float32) for part in parts)
-        hidden = hid_all[...].astype(jnp.bfloat16)
+        hidden = ins["hid_all"][...].astype(jnp.bfloat16)
         g_t2[...] = sum(dot_nt(part, hidden) for part in parts)
         ones = jnp.ones((8, lab_all.shape[0]), jnp.bfloat16)
         keep["t2"] = sum(dot_nt(ones, part) for part in parts)
 
     def fourth():
         swaps[3].arrive()
-        d_pre = jnp.sum(dh_got[...], 0) * silu_slope(pre[...])
+        d_pre = collect(dh_got) * silu_slope(pre[...])
         parts = thirds(d_pre)
-        feats = feat_all[...].astype(jnp.bfloat16)
+        feats = ins["feat_all"][...].astype(jnp.bfloat16)
         g_t1[...] = sum(jnp.dot(part, feats, preferred_element_type=jnp.float32) for part in parts)
         ones = jnp.ones((8, lab_all.shape[0]), jnp.bfloat16)
-        bias_t1 = sum(dot_nt(ones, part) for part in parts)
-        total = squares[...]
-        for ref in (g_cond, g_t1, g_t2, g_cls):
+        keep["t1"] = sum(dot_nt(ones, part) for part in parts)
+        total = jnp.zeros((1, 1), jnp.float32)
+        for ref in (g_cond, g_t1, g_t2, g_cls, ins["done_in"], ins["done_out"]):
+            total = total + jnp.sum(ref[...] * ref[...])
+        keep["squares"] = total
+
+    def message():
+        total = keep["squares"]
+        for ref in shards:
             total = total + jnp.sum(ref[...] * ref[...])
         bias_cond = jnp.sum(dm_all[...], 0, keepdims=True)
-        note[...] = jnp.zeros_like(note)
-        note[0:16, :] = jnp.sum(small_got[...], 0)
-        note[16:17, :] = total
-        note[17:18, :cols] = bias_t1[0:1]
-        note[18:19, :cols] = keep["t2"][0:1]
-        for k in range(3):
-            note[19 + k : 20 + k, :] = bias_cond[:, 128 * k : 128 * (k + 1)]
+        blank = jnp.zeros((1, 128 - cols), jnp.float32)
+        lines = [jnp.concatenate([keep[name][0:1, :], blank], 1) for name in ("t1", "t2")]
+        lines.append(parts_of(total))
+        lines.append(parts_of(ins["loss"][0:1, :]))
+        lines += [bias_cond[:, 128 * k : 128 * (k + 1)] for k in range(3)]
+        lines.append(jnp.zeros((9, 128), jnp.float32))
+        note[...] = jnp.concatenate([jnp.sum(small_got[...].astype(jnp.float32), 0)] + lines, 0).astype(jnp.bfloat16)
         swaps[4].start()
         merged[me] = note[...]
 
@@ -1130,40 +1086,7 @@
         for swap in swaps:
             swap.sent()
 
-    return [first, second, third, fourth, last]
-
-
-def settle_kernel(devices, *refs):
-    greet_all(devices)
-    for step in settle_steps(devices, refs[:11], refs[11:16], refs[16:24], refs[24:]):
-        step()
-
-
-def settle(ins):
-    devices = lax.axis_size(AXIS)
-    d_mods, small, wt2, wcond, pre = ins[:5]
-    cols, images = pre.shape
-    outs = [(wcond.shape[0], devices * cols), (cols, FREQ), (cols, devices * cols), (cols, 1024), (devices, 24, 128)]
-    return pl.pallas_call(
-        functools.partial(settle_kernel, devices),
-        out_shape=[jax.ShapeDtypeStruct(shape, jnp.float32) for shape in outs],
-        in_specs=[pl.BlockSpec(memory_space=pltpu.VMEM)] * 11,
-        out_specs=[pl.BlockSpec(memory_space=pltpu.VMEM)] * 5,
-        scratch_shapes=[
-            pltpu.VMEM(d_mods.shape, jnp.float32),
-            pltpu.VMEM((images, 384), jnp.float32),
-            pltpu.VMEM(small.shape, jnp.float32),
-            pltpu.VMEM((devices * cols, images), jnp.float32),
-            pltpu.VMEM((devices, cols, images), jnp.float32),
-            pltpu.VMEM((devices * cols, images), jnp.float32),
-            pltpu.VMEM((devices, cols, images), jnp.float32),
-            pltpu.VMEM((24, 128), jnp.float32),
-            pltpu.SemaphoreType.DMA((5, devices)),
-            pltpu.SemaphoreType.DMA((5, devices)),
-        ],
-        compiler_params=pltpu.CompilerParams(collective_id=4, has_side_effects=True, vmem_limit_bytes=24 << 20),
-        name="settle",
-    )(*ins)
+    return [first, second, third, fourth, message, last]
 
 
 def dot_nn(left, right):
@@ -1224,16 +1147,18 @@
             self.copies[i].wait()
 
 
-def forward_image(x_ref, mod, weights, b_in, b_out, outs):
+def forward_image(x_ref, mod, weights, b_in, b_out, outs, hook=lambda: None):
     h1, qkv, probs, o, a, x1, h2, u, g, f = outs
     shift1, scale1, gate1, shift2, scale2, gate2 = (mod[0, i : i + 1, :] for i in range(6))
     width = MODEL_WIDTH
+    hook()
     x = x_ref[...]
     h1[...] = (norm_parts(x)[0] * (1 + scale1) + shift1).astype(jnp.bfloat16)
     weights.need(0)
     for j in range(3):
         span = slice(j * width, (j + 1) * width)
         qkv[:, span] = (dot_nt(h1[...], weights.w_in[span, :]) + b_in[:, span]).astype(jnp.bfloat16)
+    hook()
     for pair in range(HEADS // 2):
         lanes = slice(128 * pair, 128 * (pair + 1))
         q, k, v = (qkv[:, j * width + 128 * pair : j * width + 128 * (pair + 1)] for j in range(3))
@@ -1248,11 +1173,13 @@
             term = dot_nn(weight, jnp.where(mask, v, zero))
             mixed = term if mixed is None else mixed + term
         o[:, lanes] = mixed.astype(jnp.bfloat16)
+        hook()
     weights.need(1)
     branch = dot_nt(o[...], weights.w_out[:, :width]) + b_out[:, :width]
     a[...] = branch.astype(jnp.bfloat16)
     x1[...] = x + gate1 * branch
     h2[...] = (norm_parts(x1[...])[0] * (1 + scale2) + shift2).astype(jnp.bfloat16)
+    hook()
     weights.need(2)
     weights.need(3)
     total = None
@@ -1264,16 +1191,10 @@
         g[:, span] = gelu_value(value).astype(jnp.bfloat16)
         term = dot_nt(g[:, span], weights.w_out[:, (1 + j) * width : (2 + j) * width])
         total = term if total is None else total + term
+        hook()
     ffn = total + b_out[:, width:]
     f[...] = ffn.astype(jnp.bfloat16)
     return x1[...] + gate2 * ffn
-
-
-def forward_kernel(x, mod, w_in, w_out, b_in, b_out, *refs):
-    outs, x_out, vm_in, vm_out, sems = refs[:10], refs[10], refs[11], refs[12], refs[13]
-    weights = Weights((w_in, w_out), (vm_in, vm_out), sems)
-    weights.start((0, 1, 2, 3))
-    x_out[...] = forward_image(x, mod, weights, b_in, b_out, outs)
 
 
 def head_kernel(scale_out, x, mod, w_in, w_out, b_in, b_out, final, head_t, b_head, targets_t, *refs):
@@ -1335,21 +1256,6 @@
     any_block = pl.BlockSpec(memory_space=pl.ANY)
     return [token_block(MODEL_WIDTH), image_block(6, MODEL_WIDTH), any_block, any_block, whole_block(1, IW),
             whole_block(1, 2 * MODEL_WIDTH)]
-
-
-def forward_block(ins):
-    images = ins[1].shape[0]
-    shapes, specs = kept_shapes(images)
-    return pl.pallas_call(
-        forward_kernel,
-        grid=(images,),
-        out_shape=shapes + [jax.ShapeDtypeStruct((images * SEQ, MODEL_WIDTH), jnp.float32)],
-        in_specs=forward_specs(),
-        out_specs=specs + [token_block(MODEL_WIDTH)],
-        scratch_shapes=WEIGHT_SCRATCH,
-        compiler_params=pltpu.CompilerParams(vmem_limit_bytes=56 << 20),
-        name="forward_block",
-    )(*ins)
 
 
 def forward_head(ins, scale_out):
@@ -1371,7 +1277,7 @@
     )(*ins)
 
 
-def backward_image(refs, mod, weights, outs):
+def backward_image(refs, mod, weights, outs, hook=lambda: None):
     up_ref, x_ref, x1_ref, probs, qkv, a, f, u = refs
     dx, d_qkv, d_u, d_f, d_a, d_mod, g_bin, g_bout = outs
     width = MODEL_WIDTH
@@ -1385,6 +1291,7 @@
     def rows_sum(value):
         return jnp.sum(value.astype(jnp.float32), 0, keepdims=True)
 
+    hook()
     upstream = up_ref[...]
     d_f[...] = (gate2 * upstream).astype(jnp.bfloat16)
     d_mod[0, 5:6, :] = rows_sum(f[...].astype(jnp.float32) * upstream)
@@ -1400,6 +1307,7 @@
         g_bin[:, rows] += rows_sum(d_u[:, span])
         term = dot_nn(d_u[:, span], weights.w_in[rows, :])
         d_h2 = term if d_h2 is None else d_h2 + term
+        hook()
     normed, scale = norm_parts(x1_ref[...])
     d_mod[0, 3:4, :] = rows_sum(d_h2)
     d_mod[0, 4:5, :] = rows_sum(d_h2 * normed)
@@ -1410,6 +1318,7 @@
     dx[...] = upstream
     weights.need(1)
     d_o = dot_nn(d_a[...], weights.w_out[:, :width]).astype(jnp.bfloat16)
+    hook()
     root = HEAD_DIM**-0.5
     for pair in range(HEADS // 2):
         lanes = [slice(j * width + 128 * pair, j * width + 128 * (pair + 1)) for j in range(3)]
@@ -1432,6 +1341,7 @@
         d_qkv[:, lanes[0]] = (sums[0] * root).astype(jnp.bfloat16)
         d_qkv[:, lanes[1]] = (sums[1] * root).astype(jnp.bfloat16)
         d_qkv[:, lanes[2]] = sums[2].astype(jnp.bfloat16)
+        hook()
     weights.need(0)
     d_h1 = None
     for j in range(3):
@@ -1443,6 +1353,7 @@
     d_mod[0, 0:1, :] = rows_sum(d_h1)
     d_mod[0, 1:2, :] = rows_sum(d_h1 * normed)
     dx[...] += norm_back(normed, scale, d_h1 * (1 + scale1))
+    hook()
 
 
 def backward_kernel(mod, w_in, w_out, *refs):
@@ -1473,51 +1384,337 @@
     )(mods, w_in, w_out, *refs)
 
 
-GRAD_STEPS = tuple((0, j) for j in range(3)) + tuple((1, j) for j in range(4)) + ((2, 0),) + tuple((3, j) for j in range(4))
-
-
-def grads_kernel(*refs):
-    ins, (g_in, g_out), bufs, (keep_in, keep_out, load_sems, store_sems) = refs[:8], refs[8:10], refs[10:18], refs[18:]
-    width = MODEL_WIDTH
-    copies = [pltpu.make_async_copy(src, dst, load_sems.at[i]) for i, (src, dst) in enumerate(zip(ins, bufs))]
-    for copy in copies:
-        copy.start()
-    stores = []
-    for step, (kind, j) in enumerate(GRAD_STEPS):
-        left, right = bufs[2 * kind], bufs[2 * kind + 1]
-        if j == 0:
-            copies[2 * kind].wait()
-            copies[2 * kind + 1].wait()
-        span = pl.ds(j * width, width)
-        if kind < 2:
-            at = pl.ds((3 * kind + j) * width, width)
-            keep_in[at, :] = dot_tn(left[:, span], right[...]).astype(jnp.bfloat16)
-            store = pltpu.make_async_copy(keep_in.at[at, :], g_in.at[at, :], store_sems.at[step])
-        else:
-            at = pl.ds((kind - 2 + j) * width, width)
-            keep_out[:, at] = dot_tn(left[...], right[:, span]).astype(jnp.bfloat16)
-            store = pltpu.make_async_copy(keep_out.at[:, at], g_out.at[:, at], store_sems.at[step])
-        store.start()
-        stores.append(store)
-    for store in stores:
-        store.wait()
-
-
-def weight_grads(ins):
+def gather_steps(job):
+    steps = [job.begin, functools.partial(job.a_step, 0)]
+    for dist in (1, 2, 3):
+        steps += [functools.partial(job.z_step, dist), functools.partial(job.a_step, dist)]
+    for dist in range(4):
+        steps += [functools.partial(job.b_step, dist, flip) for flip in range(2)]
+    return steps + [job.finish]
+
+
+class Hooks:
+    def __init__(self, steps, slots, points):
+        self.points, self.table = points, {}
+        for step, slot in zip(steps, slots):
+            self.table.setdefault((slot // points, slot % points), []).append(step)
+        self.next = 0
+
+    def __call__(self):
+        point, self.next = self.next, self.next + 1
+        for (turn, where), steps in sorted(self.table.items(), key=lambda item: item[0]):
+            if where == point:
+
+                @pl.when(pl.program_id(0) == turn)
+                def _():
+                    for step in steps:
+                        step()
+
+
+def start_kernel(devices, *refs):
+    own, mod_ins, refs = refs[:2], refs[2:10], refs[10:]
+    full, mod_outs, refs = refs[:2], refs[2:10], refs[10:]
+    part, mod_bufs, mod_sems = refs[:10], refs[10:13], refs[13:]
+    greet_all(devices)
+    place = Place()
+    job = Gather(place, own, part[:2], part[2:4], full, part[4:])
+    first, second, third, fourth, last = modulate_steps(devices, mod_ins, mod_outs, mod_bufs, mod_sems)
+    moves = gather_steps(job)
+    for step in START_ORDER(first, second, third, fourth, last, moves):
+        step()
+
+
+def START_ORDER(first, second, third, fourth, last, moves):
+    return [first] + moves[:2] + [second] + moves[2:4] + [third] + moves[4:6] + [fourth] + moves[6:-1] + [last, moves[-1]]
+
+
+def gather_modulate(pair, ins):
+    devices = lax.axis_size(AXIS)
+    msg, wt1, wt2, wcls, wcond = ins[:5]
+    cols, images = wt1.shape[0], devices * msg.shape[0]
+    outs = [
+        (devices, msg.shape[0], wcond.shape[0]), (cols, images), (cols, images), (devices * cols, images),
+        (devices * cols, images), (images, FREQ), (images, 128), (devices,) + msg.shape,
+    ]
+    padded = -(-cols // 16) * 16
+    vmem = pl.BlockSpec(memory_space=pltpu.VMEM)
+    return pl.pallas_call(
+        functools.partial(start_kernel, devices),
+        out_shape=[jax.ShapeDtypeStruct((devices * a.shape[0], a.shape[1]), jnp.bfloat16) for a in pair]
+        + [jax.ShapeDtypeStruct(shape, jnp.float32) for shape in outs],
+        in_specs=[vmem] * 10,
+        out_specs=[pl.BlockSpec(memory_space=pl.ANY)] * 2 + [vmem] * 8,
+        scratch_shapes=gather_scratch(piece_shapes([a.shape for a in pair]))
+        + [
+            pltpu.VMEM((devices, padded, images), jnp.bfloat16),
+            pltpu.VMEM((devices, padded, images), jnp.bfloat16),
+            pltpu.VMEM((devices, msg.shape[0], wcond.shape[0]), jnp.float32),
+            pltpu.SemaphoreType.DMA((4, devices)),
+            pltpu.SemaphoreType.DMA((4, devices)),
+        ],
+        compiler_params=pltpu.CompilerParams(collective_id=3, has_side_effects=True, vmem_limit_bytes=56 << 20),
+        name="gather_modulate",
+    )(*pair, *ins)
+
+
+FORWARD_POINTS = 13
+
+
+def forward_gather_kernel(slots, x, mod, w_in, w_out, b_in, b_out, own_in, own_out, *refs):
+    outs, x_out, full, refs = refs[:10], refs[10], refs[11:13], refs[13:]
+    vm_in, vm_out, sems, part = refs[0], refs[1], refs[2], refs[3:]
+    place = Place()
+    job = Gather(place, (own_in, own_out), part[:2], part[2:4], full, part[4:])
+    hooks = Hooks([place.greet] + gather_steps(job), slots, FORWARD_POINTS)
+    weights = Weights((w_in, w_out), (vm_in, vm_out), sems)
+    weights.start((0, 1, 2, 3))
+    x_out[...] = forward_image(x, mod, weights, b_in, b_out, outs, hooks)
+
+
+GATHER_SLOTS = (0, 0, 13, 15, 26, 28, 39, 41, 50) + (34, 43, 48, 51, 51, 51, 51, 51, 51)
+
+
+def forward_gather(ins, pair):
+    images = ins[1].shape[0]
+    devices = lax.axis_size(AXIS)
+    shapes, specs = kept_shapes(images)
     any_block = pl.BlockSpec(memory_space=pl.ANY)
     return pl.pallas_call(
-        grads_kernel,
-        out_shape=[
-            jax.ShapeDtypeStruct((IW, MODEL_WIDTH), jnp.bfloat16), jax.ShapeDtypeStruct((MODEL_WIDTH, OW), jnp.bfloat16)
+        functools.partial(forward_gather_kernel, GATHER_SLOTS),
+        grid=(images,),
+        out_shape=shapes
+        + [jax.ShapeDtypeStruct((images * SEQ, MODEL_WIDTH), jnp.float32)]
+        + [jax.ShapeDtypeStruct((devices * a.shape[0], a.shape[1]), jnp.bfloat16) for a in pair],
+        in_specs=forward_specs() + [whole_block(*a.shape) for a in pair],
+        out_specs=specs + [token_block(MODEL_WIDTH)] + [any_block] * 2,
+        scratch_shapes=WEIGHT_SCRATCH + gather_scratch(piece_shapes([a.shape for a in pair])),
+        compiler_params=pltpu.CompilerParams(collective_id=1, has_side_effects=True, vmem_limit_bytes=58 << 20),
+        name="forward_gather",
+    )(*ins, *pair)
+
+
+GRAD_CUTS = [3 * MODEL_WIDTH // MODEL_WIDTH, FF // MODEL_WIDTH]
+
+
+class Grads:
+    def __init__(self, hbm, bufs, keep_in, keep_out, sems):
+        bufs = [bufs[0], bufs[4], *bufs[1:]]
+        self.bufs, self.keep_in, self.keep_out = bufs, keep_in, keep_out
+        self.copies = [pltpu.make_async_copy(src, dst, sems.at[i]) for i, (src, dst) in enumerate(zip(hbm, bufs))]
+        self.here = set()
+
+    def start(self):
+        for i in (4, 5, 6, 7, 2, 3, 0):
+            self.copies[i].start()
+
+    def need(self, *which):
+        for i in which:
+            if i not in self.here:
+                self.copies[i].wait()
+                self.here.add(i)
+
+    def rows_in(self, chunk):
+        width = MODEL_WIDTH
+        pair = 0 if chunk < 3 else 1
+        self.need(2 * pair, 2 * pair + 1)
+        left, right = self.bufs[2 * pair], self.bufs[2 * pair + 1]
+        at = (chunk - 3 * pair) * width
+        self.keep_in[chunk * width : (chunk + 1) * width, :] = dot_tn(left[:, at : at + width], right[...]).astype(
+            jnp.bfloat16
+        )
+
+    def rows_out(self, part):
+        width = MODEL_WIDTH
+        rows = slice(part * width // 2, (part + 1) * width // 2)
+        self.need(4, 5)
+        self.keep_out[rows, :width] = dot_tn(self.bufs[4][:, rows], self.bufs[5][...]).astype(jnp.bfloat16)
+        self.need(6, 7)
+        for j in range(FF // width):
+            span = slice(j * width, (j + 1) * width)
+            self.keep_out[rows, (1 + j) * width : (2 + j) * width] = dot_tn(
+                self.bufs[6][:, rows], self.bufs[7][:, span]
+            ).astype(jnp.bfloat16)
+        if part == 0:
+            self.copies[1].start()
+
+
+def grads_out_kernel(*refs):
+    ins, g_in, total, refs = refs[:8], refs[8], refs[9:10], refs[10:]
+    bufs, keep_in, keep_out, load_sems, store_sem, refs = refs[:7], refs[7], refs[8], refs[9], refs[10], refs[11:]
+    place = Place()
+    work = Grads(ins, bufs, keep_in, keep_out, load_sems)
+    work.start()
+    place.greet()
+    job = Scatter(place, [keep_out], total, refs[:6], refs[6:])
+    work.rows_out(1)
+    job.open(3)
+    job.open(2)
+    work.rows_out(0)
+    job.open(0)
+    job.open(1)
+    moves = job.steps()
+    for chunk in range(7):
+        moves[chunk]()
+        work.rows_in(chunk)
+    store = pltpu.make_async_copy(keep_in, g_in, store_sem)
+    store.start()
+    for move in moves[7:]:
+        move()
+    store.wait()
+
+
+def grad_bufs(ins):
+    return [pltpu.VMEM(a.shape, a.dtype) for i, a in enumerate(ins) if i != 1] + [
+        pltpu.VMEM((IW, MODEL_WIDTH), jnp.bfloat16),
+        pltpu.VMEM((MODEL_WIDTH, OW), jnp.bfloat16),
+        pltpu.SemaphoreType.DMA((8,)),
+    ]
+
+
+def weight_grads_out(ins, shape):
+    any_block = pl.BlockSpec(memory_space=pl.ANY)
+    return pl.pallas_call(
+        grads_out_kernel,
+        out_shape=[jax.ShapeDtypeStruct((IW, MODEL_WIDTH), jnp.bfloat16), jax.ShapeDtypeStruct(shape, jnp.float32)],
+        in_specs=[any_block] * 8,
+        out_specs=[any_block, pl.BlockSpec(memory_space=pltpu.VMEM)],
+        scratch_shapes=grad_bufs(ins) + [pltpu.SemaphoreType.DMA] + scatter_scratch(piece_shapes([shape])),
+        compiler_params=pltpu.CompilerParams(collective_id=5, has_side_effects=True, vmem_limit_bytes=58 << 20),
+        name="weight_grads_out",
+    )(*ins)
+
+
+BACKWARD_POINTS = 13
+
+
+def backward_scatter_kernel(slots, mod, w_in, w_out, grad, lat_t, *refs):
+    ins, outs, (g_patch, g_pbias, total), refs = refs[:8], refs[8:16], refs[16:19], refs[19:]
+    vm_in, vm_out, sems, mine, refs = refs[0], refs[1], refs[2], refs[3], refs[4:]
+    place = Place()
+    job = Scatter(place, [grad], [total], refs[:6], refs[6:], [mine])
+    hooks = Hooks([place.greet, job.open_all] + job.steps(), slots, BACKWARD_POINTS)
+    weights = Weights((w_in, w_out), (vm_in, vm_out), sems)
+    weights.start((3, 2, 1, 0))
+    backward_image(ins, mod, weights, outs, hooks)
+    d_patch = outs[0][...].astype(jnp.bfloat16)
+
+    @pl.when(pl.program_id(0) == 0)
+    def _():
+        g_patch[...] = jnp.zeros_like(g_patch)
+        g_pbias[...] = jnp.zeros_like(g_pbias)
+
+    g_patch[...] += dot_nn(lat_t[0], d_patch)
+    g_pbias[...] += jnp.sum(d_patch.astype(jnp.float32), 0, keepdims=True)
+
+
+SCATTER_SLOTS = (0, 0, 3, 6, 10, 14, 18, 22, 26, 29, 33, 37, 41, 45, 49, 51, 51)
+
+
+def backward_scatter(mods, w_in, w_out, refs, grad, lat_t, shape):
+    images, width, low, full = mods.shape[0], MODEL_WIDTH, jnp.bfloat16, jnp.float32
+    tokens = images * SEQ
+    any_block = pl.BlockSpec(memory_space=pl.ANY)
+    shapes = [((tokens, width), full), ((tokens, 3 * width), low), ((tokens, FF), low), ((tokens, width), low),
+              ((tokens, width), low), ((images, 6, width), full), ((1, IW), full), ((1, 2 * width), full),
+              ((PD, width), full), ((1, width), full), (shape, full)]
+    pieces = piece_shapes([shape])
+    return pl.pallas_call(
+        functools.partial(backward_scatter_kernel, SCATTER_SLOTS),
+        grid=(images,),
+        out_shape=[jax.ShapeDtypeStruct(s, t) for s, t in shapes],
+        in_specs=[image_block(6, width), any_block, any_block, any_block, image_block(PD, SEQ), token_block(width),
+                  token_block(width), token_block(width), image_block(HEADS, SEQ, SEQ), token_block(3 * width),
+                  token_block(width), token_block(width), token_block(FF)],
+        out_specs=[token_block(s[1]) for s, _ in shapes[:5]]
+        + [image_block(6, width)] + [whole_block(*s) for s, _ in shapes[6:-1]] + [any_block],
+        scratch_shapes=WEIGHT_SCRATCH
+        + [pltpu.VMEM((16,) + pieces[0], jnp.bfloat16)] + scatter_scratch(pieces),
+        compiler_params=pltpu.CompilerParams(collective_id=6, has_side_effects=True, vmem_limit_bytes=62 << 20),
+        name="backward_scatter",
+    )(mods, w_in, w_out, grad, lat_t, *refs)
+
+
+def finish_kernel(devices, *refs):
+    count = len(SETTLE_INS)
+    ins, set_ins, refs = refs[:8], dict(zip(SETTLE_INS, refs[8 : 8 + count])), refs[8 + count :]
+    totals, set_outs, refs = refs[:2], refs[2:7], refs[7:]
+    bufs, keep_in, keep_out, load_sems, refs = refs[:7], refs[7], refs[8], refs[9], refs[10:]
+    sc_bufs, sc_sems, refs = refs[:12], refs[12:26], refs[26:]
+    set_bufs, set_sems = refs[:10], refs[10:]
+    work = Grads(ins, bufs, keep_in, keep_out, load_sems)
+    work.start()
+    greet_all(devices)
+    place = Place()
+    job = Scatter(place, [keep_in, keep_out], totals, sc_bufs, sc_sems)
+    first, second, third, fourth, message, last = settle_steps(devices, set_ins, set_outs, set_bufs, set_sems, totals)
+    first()
+    work.rows_out(1)
+    work.rows_in(5)
+    work.rows_in(6)
+    job.open(3)
+    job.cross_b(3)
+    second()
+    work.rows_out(0)
+    work.rows_in(0)
+    work.rows_in(1)
+    job.open(0)
+    job.cross_b(0)
+    job.cross_a(3)
+    work.rows_in(3)
+    work.rows_in(4)
+    job.open(2)
+    job.cross_b(2)
+    third()
+    job.cross_a(0)
+    work.rows_in(2)
+    job.open(1)
+    job.along_z(3)
+    job.cross_b(1)
+    job.cross_a(2)
+    fourth()
+    job.along_z(0)
+    job.cross_a(1)
+    job.along_z(2)
+    job.along_z(1)
+    job.close()
+    job.end()
+    message()
+    job.finish()
+    last()
+
+
+def finish_grads(ins, shapes, set_ins):
+    devices = lax.axis_size(AXIS)
+    wcond, d_mods = set_ins["wcond"], set_ins["d_mods"]
+    cols, images = set_ins["pre"].shape
+    outs = [(wcond.shape[0], devices * cols), (cols, FREQ), (cols, devices * cols), (cols, 1024)]
+    vmem = pl.BlockSpec(memory_space=pltpu.VMEM)
+    low = jnp.bfloat16
+    return pl.pallas_call(
+        functools.partial(finish_kernel, devices),
+        out_shape=[jax.ShapeDtypeStruct(shape, jnp.float32) for shape in list(shapes) + outs]
+        + [jax.ShapeDtypeStruct((devices, 32, 128), low)],
+        in_specs=[pl.BlockSpec(memory_space=pl.ANY)] * 8 + [vmem] * len(SETTLE_INS),
+        out_specs=[vmem] * 7,
+        scratch_shapes=grad_bufs(ins)
+        + scatter_scratch(piece_shapes(shapes))
+        + [
+            pltpu.VMEM(d_mods.shape, jnp.float32),
+            pltpu.VMEM((images, 384), jnp.float32),
+            pltpu.VMEM((devices * 16, 128), jnp.float32),
+            pltpu.VMEM((devices, 16, 128), low),
+            pltpu.VMEM((devices, 16, 128), low),
+            pltpu.VMEM((devices, 32, images), low),
+            pltpu.VMEM((devices, 32, images), low),
+            pltpu.VMEM((devices, 32, images), low),
+            pltpu.VMEM((devices, 32, images), low),
+            pltpu.VMEM((32, 128), low),
+            pltpu.SemaphoreType.DMA((5, devices)),
+            pltpu.SemaphoreType.DMA((5, devices)),
         ],
-        in_specs=[any_block] * 8,
-        out_specs=[any_block] * 2,
-        scratch_shapes=[pltpu.VMEM(a.shape, a.dtype) for a in ins]
-        + [pltpu.VMEM((IW, MODEL_WIDTH), jnp.bfloat16), pltpu.VMEM((MODEL_WIDTH, OW), jnp.bfloat16),
-           pltpu.SemaphoreType.DMA((8,)), pltpu.SemaphoreType.DMA((len(GRAD_STEPS),))],
-        compiler_params=pltpu.CompilerParams(vmem_limit_bytes=56 << 20),
-        name="weight_grads",
-    )(*ins)
+        compiler_params=pltpu.CompilerParams(collective_id=4, has_side_effects=True, vmem_limit_bytes=63 << 20),
+        name="finish_grads",
+    )(*ins, *(set_ins[name] for name in SETTLE_INS))
 
 def code_table():
     quarter = MODEL_WIDTH // 4
@@ -1551,9 +1748,6 @@
     out_t = layer_output_weights.transpose(0, 2, 1)
     cols, cond_cols = embed_t.shape[0], cond_t.shape[0]
     time_one, time_two, patch_bias, cond_bias, block_input_bias, block_output_bias, head_bias = split_biases(biases)
-    fulls = gather_weights([(in_t[i], out_t[i]) for i in range(LAYERS)], 1)
-    w_in = [fulls[2 * i] for i in range(LAYERS)]
-    w_out = [fulls[2 * i + 1] for i in range(LAYERS)]
     features = time_features(timesteps).astype(jnp.bfloat16).astype(jnp.float32)
     label_rows = jnp.broadcast_to(labels.astype(jnp.float32)[:, None], (images, 128))
     own_patch_w = embed_t[:, FREQ + MODEL_WIDTH : FREQ + MODEL_WIDTH + PD].reshape(3, 128)
@@ -1568,8 +1762,9 @@
         return jnp.broadcast_to(part[:, None], (count, images_all))
 
     own_cond_bias = lax.dynamic_slice(cond_bias, (me * cond_cols,), (cond_cols,))[None]
-    mods, pre, cond, hid_all, low_all, feat_all, lab_all, notes = modulate(
-        [note, w_t1, w_t2, w_class, cond_t, own_bias(time_one, cols), own_bias(time_two, cols), own_cond_bias]
+    first_in, first_out, mods, pre, cond, hid_all, low_all, feat_all, lab_all, notes = gather_modulate(
+        [in_t[0], out_t[0]],
+        [note, w_t1, w_t2, w_class, cond_t, own_bias(time_one, cols), own_bias(time_two, cols), own_cond_bias],
     )
     chunks = mods.transpose(1, 0, 2).reshape(images, 6 * LAYERS + 2, MODEL_WIDTH)
     w_patch = notes[:, :3, FREQ + 128 :].reshape(MODEL_WIDTH, PD).astype(jnp.bfloat16)
@@ -1577,52 +1772,53 @@
     block_mods = [chunks[:, 6 * i : 6 * (i + 1)] for i in range(LAYERS)]
     head_t = head_w.T
     tokens_all = devices * images * SEQ * PO
-    kept_all, starts = [], []
-    for i in range(LAYERS):
-        ins = [x, block_mods[i], w_in[i], w_out[i], block_input_bias[i][None], block_output_bias[i][None]]
-        starts.append(x)
-        if i < LAYERS - 1:
-            *kept, x = forward_block(ins)
-        else:
-            ins += [chunks[:, 6 * LAYERS :], head_t, head_bias[:, None], targets.transpose(0, 2, 1)]
-            *kept, upstream, d_final, head_grad, head_bias_grad, loss_part = forward_head(ins, 2.0 / tokens_all)
-        kept_all.append(kept)
-    mod_grads, in_shards, out_shards = [None] * LAYERS, [None] * LAYERS, [None] * LAYERS
-    in_bias_grads, out_bias_grads = [None] * LAYERS, [None] * LAYERS
-    for i in reversed(range(LAYERS)):
-        h1, qkv, probs, o, a, x1, h2, u, g, f = kept_all[i]
-        upstream, d_qkv, d_u, d_f, d_a, mod_grads[i], in_bias_grads[i], out_bias_grads[i] = backward_block(
-            block_mods[i], w_in[i], w_out[i], [upstream, starts[i], x1, probs, qkv, a, f, u]
-        )
-        grads = weight_grads([d_qkv, h1, d_u, h2, d_a, o, d_f, g])
-        in_shards[i], out_shards[i] = scatter_grads(grads, 5 + i)
-    d_patch = upstream.astype(jnp.bfloat16)
-    patch_grad = jnp.dot(latents.reshape(images * SEQ, PD).T, d_patch, preferred_element_type=jnp.float32)
-    patch_bias_grad = jnp.sum(d_patch.astype(jnp.float32), 0)
+    lat_t = latents.transpose(0, 2, 1)
+    bias_rows = [(block_input_bias[i][None], block_output_bias[i][None]) for i in range(LAYERS)]
+    *kept0, x_mid, last_in, last_out = forward_gather(
+        [x, block_mods[0], first_in, first_out, *bias_rows[0]], [in_t[1], out_t[1]]
+    )
+    *kept1, upstream, d_final, head_grad, head_bias_grad, loss_part = forward_head(
+        [x_mid, block_mods[1], last_in, last_out, *bias_rows[1], chunks[:, 6 * LAYERS :], head_t, head_bias[:, None],
+         targets.transpose(0, 2, 1)],
+        2.0 / tokens_all,
+    )
+    h1, qkv, probs, o, a, x1, h2, u, g, f = kept1
+    upstream, d_qkv, d_u, d_f, d_a, mod_grad1, in_bias1, out_bias1 = backward_block(
+        block_mods[1], last_in, last_out, [upstream, x_mid, x1, probs, qkv, a, f, u]
+    )
+    in_shape, out_shape = in_t.shape[1:], out_t.shape[1:]
+    grad_in, out_shard1 = weight_grads_out([d_qkv, h1, d_u, h2, d_a, o, d_f, g], out_shape)
+    h1, qkv, probs, o, a, x1, h2, u, g, f = kept0
+    (upstream, d_qkv, d_u, d_f, d_a, mod_grad0, in_bias0, out_bias0, patch_grad, patch_bias_grad, in_shard1) = backward_scatter(
+        block_mods[0], first_in, first_out, [upstream, x, x1, probs, qkv, a, f, u], grad_in, lat_t, in_shape
+    )
+    mod_grads, in_bias_grads, out_bias_grads = [mod_grad0, mod_grad1], [in_bias0, in_bias1], [out_bias0, out_bias1]
     d_modulation = jnp.concatenate(mod_grads + [d_final], 1)
     d_mods = d_modulation.reshape(images, devices, cond_cols).transpose(1, 0, 2)
-    end_row = jnp.concatenate([head_bias_grad[:, 0], loss_part[0, :1], jnp.zeros((128 - PO - 1,), jnp.float32)])
-    rows = [
-        a.reshape(-1, 128) for a in [head_grad, patch_grad, patch_bias_grad] + in_bias_grads + out_bias_grads + [end_row]
-    ]
-    used = sum(a.shape[0] for a in rows)
-    small = jnp.concatenate(rows + [jnp.zeros((devices * 16 - used, 128), jnp.float32)], 0).reshape(devices, 16, 128)
-    squares = sum(jnp.sum(shard * shard) for shard in in_shards + out_shards)
-    g_cond, g_t1, g_t2, g_cls, merged = settle(
-        [d_mods, small, w_t2, cond_t, pre, cond, hid_all, low_all, feat_all, lab_all, jnp.full((1, 128), squares)]
-    )
-    flat = merged[:, :16].reshape(-1)
-    sizes = [MODEL_WIDTH * PO, PD * MODEL_WIDTH, MODEL_WIDTH, LAYERS * IW, LAYERS * 2 * MODEL_WIDTH, PO, 1]
-    places = [sum(sizes[:k]) for k in range(len(sizes) + 1)]
-    head_total = flat[: places[1]].reshape(PO, MODEL_WIDTH)
-    patch_total = flat[places[1] : places[2]].reshape(PD, MODEL_WIDTH)
-    loss_total = flat[places[6]]
+    in_shard0, out_shard0, g_cond, g_t1, g_t2, g_cls, merged = finish_grads(
+        [d_qkv, h1, d_u, h2, d_a, o, d_f, g],
+        [in_shape, out_shape],
+        {
+            "d_mods": d_mods, "wt2": w_t2, "wcond": cond_t, "pre": pre, "cond": cond, "hid_all": hid_all, "low_all": low_all,
+            "feat_all": feat_all, "lab_all": lab_all, "g_head": head_grad, "g_hbias": head_bias_grad, "loss": loss_part,
+            "g_patch": patch_grad, "g_pbias": patch_bias_grad, "bin0": in_bias_grads[0], "bin1": in_bias_grads[1],
+            "bout0": out_bias_grads[0], "bout1": out_bias_grads[1], "done_in": in_shard1, "done_out": out_shard1,
+        },
+    )
+    merged = merged.astype(jnp.float32)
+    wide = MODEL_WIDTH // 128
+    blocks = merged[:, :16]
+    patch_total = blocks[:wide].transpose(1, 0, 2).reshape(PD, MODEL_WIDTH)
+    head_total = blocks[wide : 3 * wide].reshape(wide, PO, 128).transpose(1, 0, 2).reshape(PO, MODEL_WIDTH)
+    flat = blocks[3 * wide :].reshape(-1)
+    rest = LAYERS * (IW + 2 * MODEL_WIDTH) + PO
+    loss_total = jnp.sum(merged[:, 19, :3])
     bias_total = jnp.concatenate(
-        [merged[:, 17, :cols].reshape(-1), merged[:, 18, :cols].reshape(-1), flat[places[2] : places[3]],
-         merged[:, 19:22].reshape(devices, 384)[:, :cond_cols].reshape(-1), flat[places[3] : places[6]]]
+        [merged[:, 16, :cols].reshape(-1), merged[:, 17, :cols].reshape(-1), flat[:MODEL_WIDTH],
+         merged[:, 20:23].reshape(devices, 384)[:, :cond_cols].reshape(-1), flat[MODEL_WIDTH : MODEL_WIDTH + rest]]
     )
     grad_norm = jnp.sqrt(
-        jnp.sum(merged[:, 16, 0])
+        jnp.sum(merged[:, 18, :3])
         + jnp.sum(head_total * head_total)
         + jnp.sum(patch_total * patch_total)
         + jnp.sum(bias_total * bias_total)
@@ -1635,11 +1831,11 @@
     turn = (0, 2, 1)
     in_up = [
         a.transpose(turn)
-        for a in adam_step(in_t, in_m.transpose(turn), in_v.transpose(turn), jnp.stack(in_shards) * factor)
+        for a in adam_step(in_t, in_m.transpose(turn), in_v.transpose(turn), jnp.stack([in_shard0, in_shard1]) * factor)
     ]
     out_up = [
         a.transpose(turn)
-        for a in adam_step(out_t, out_m.transpose(turn), out_v.transpose(turn), jnp.stack(out_shards) * factor)
+        for a in adam_step(out_t, out_m.transpose(turn), out_v.transpose(turn), jnp.stack([out_shard0, out_shard1]) * factor)
     ]
     head_up = [a.T for a in adam_step(head_t, head_m.T, head_v.T, head_total * factor)]
     bias_up = adam_step(biases, bias_m, bias_v, bias_total * factor)

time: 690 us -> 565 us (0.82)
  Pallas kernels: 594 us -> 504 us
  local copies, waits for them, and re-layouts: 48.3 us -> 24.9 us
    pallas_call x2 -> x1, Pallas kernels: 99.4 us -> 49.8 us  [backward_block(): pl.pallas_call(backward_kernel, grid=(images,), out_shape=[jax.ShapeDtype...]
    pallas_call x8 -> x5, Pallas kernels: 452 us -> 412 us  [the longest x1 129 us: finish_grads(): pl.pallas_call(functools.partial(finish_kernel, devices), out_shape=[jax....]
    unnamed x100 -> x59, local copies, waits for them, and re-layouts: 30.9 us -> 1.99 us
where the time goes in v3:
time: 565 us; the launch traced here: 556 us
  Pallas kernels  504 us (89%)
  local copies, waits for them, and re-layouts  24.9 us (4%)
  other arithmetic  19.1 us (3%)
    pallas_call x1, Pallas kernels, finish_grads(): pl.pallas_call(functools.partial(finish_kernel, devices), out_shape=[jax....  129 us
    pallas_call x1, Pallas kernels, gather_modulate(): pl.pallas_call(functools.partial(start_kernel, devices), out_shape=[jax.S...  86.1 us
    pallas_call x1, Pallas kernels, backward_scatter(): pl.pallas_call(functools.partial(backward_scatter_kernel, SCATTER_SLOTS),...  75.4 us
    pallas_call x1, Pallas kernels, forward_gather(): pl.pallas_call(functools.partial(forward_gather_kernel, GATHER_SLOTS), gr...  72.6 us
    pallas_call x1, Pallas kernels, backward_block(): pl.pallas_call(backward_kernel, grid=(images,), out_shape=[jax.ShapeDtype...  49.8 us
    pallas_call x1, Pallas kernels, weight_grads_out(): pl.pallas_call(grads_out_kernel, out_shape=[jax.ShapeDtypeStruct((IW, MOD...  48.1 us
    pallas_call x1, Pallas kernels, forward_head(): pl.pallas_call(functools.partial(head_kernel, scale_out), grid=(images,),...  42.6 us

profile of v3, /device:TPU:0, one launch (start us, length us, event | category | flops | bytes accessed | tf_op | source)
XLA Modules:
  0.0 555.6 jit_solution(8143901188734326146)
XLA Ops:
  0.7 0.8 fusion.24
  1.5 0.1 dynamic_slice.12
  1.5 0.7 broadcast_in_dim.15.refs_7_
  2.2 0.1 dynamic_slice.13
  2.3 0.7 broadcast_in_dim.16.refs_8_
  3.0 0.8 slice.130
  3.8 0.1 dynamic_slice.14
  3.8 0.6 broadcast_in_dim.17.refs_9_
  4.4 0.7 slice.161
  5.1 0.1 reshape.92
  5.2 0.7 convert_element_type.21
  5.9 0.1 fusion.18
  6.0 0.7 convert_element_type.23
  6.7 0.6 select_maximum_fusion.refs_2_
  7.3 1.5 slice.163.refs_4_.refs_9_
  8.9 1.0 slice.164
  9.8 0.6 pad.9.refs_5_
  10.5 1.3 slice.162.refs_3_
  11.8 2.2 slice_bitcast_fusion
  14.1 0.9 slice_bitcast_fusion.2
  15.0 86.1 %gather_modulate.1 = (bf16[5376,768]{1,0:T(8,128)(2,1)}, bf16[768,3840]{1,0:T(8,128)(2,1)}, f32[32,4,336]{2,1,0:T(4,128)}, f32[24,128]{1,0:T(8,128)}, f32[24,128...) custom-call(f32[168,768]{1,0:T(8,128)} %get-tuple-element.167.refs_0, ...), custom_call_target="tpu_custom_call" | custom-call | tf_op jit(solution)/shard_map/gather_modulate/pallas_call | solution.py:1441
  101.1 0.9 slice.199
  102.0 0.2 convert_element_type.24
  102.3 2.3 bitcast_add_fusion
  104.7 0.2 reshape.93
  104.9 0.7 fusion.21
  105.6 0.6 slice.136.b_in
  106.2 0.6 slice.138.b_out
  106.8 72.6 %forward_gather.1 = (bf16[1024,768]{1,0:T(8,128)(2,1)}, bf16[1024,2304]{1,0:T(8,128)(2,1)}, bf16[4,12,256,256]{3,2,1,0:T(8,128)(2,1)}, bf16[1024,768]{1,0:T(8,12...) custom-call(f32[1024,768]{1,0:T(8,128)} %bitcast.158, ...), custom_call_target="tpu_custom_call" | custom-call | tf_op jit(solution)/shard_map/forward_gather/pallas_call | solution.py:1482
  179.4 0.6 slice.170.final
  180.0 0.6 slice.142.b_in
  180.6 0.6 slice.144.b_out
  181.2 0.7 copy.50.b_head
  181.9 42.6 %forward_head.1 = (bf16[1024,768]{1,0:T(8,128)(2,1)}, bf16[1024,2304]{1,0:T(8,128)(2,1)}, bf16[4,12,256,256]{3,2,1,0:T(8,128)(2,1)}, bf16[1024,768]{1,0:T(8,128)...) custom-call(f32[1024,768]{1,0:T(8,128)} %get-tuple-element.91.x.refs, ...), custom_call_target="tpu_custom_call" | custom-call | tf_op jit(solution)/shard_map/forward_head/pallas_call | solution.py:1265
  224.6 49.8 %backward_block.1 = (f32[1024,768]{1,0:T(8,128)}, bf16[1024,2304]{1,0:T(8,128)(2,1)}, bf16[1024,3072]{1,0:T(8,128)(2,1)}, bf16[1024,768]{1,0:T(8,128)(2,1)}, bf1...) custom-call(f32[4,6,768]{2,1,0:T(8,128)} %get-tuple-element.176.mod, ...), custom_call_target="tpu_custom_call" | custom-call | tf_op jit(solution)/shard_map/backward_block/pallas_call | solution.py:1372
  274.4 48.1 %weight_grads_out.1 = (bf16[5376,768]{1,0:T(8,128)(2,1)}, f32[24,3840]{1,0:T(8,128)}) custom-call(bf16[1024,2304]{1,0:T(8,128)(2,1)} %get-tuple-element.99.refs_0_, bf16[1024,768]{1,0:T(8,128)(2,1)} %get-tuple-element.100.refs_1_, bf16[1024,3072]{1,0:T(8,128)(2,1)} %get-tuple-element.101.refs_2_, bf16[1024,768]{1,0:T(8,128)(2,1)} %get-tuple-element.102.refs_3_, ...), custom_call_target="tpu_custom_call" | custom-call | tf_op jit(solution)/shard_map/weight_grads_out/pallas_call | solution.py:1576
  322.5 75.4 %backward_scatter.1 = (f32[1024,768]{1,0:T(8,128)}, bf16[1024,2304]{1,0:T(8,128)(2,1)}, bf16[1024,3072]{1,0:T(8,128)(2,1)}, bf16[1024,768]{1,0:T(8,128)(2,1)}, b...) custom-call(f32[4,6,768]{2,1,0:T(8,128)} %get-tuple-element.177.mod,, ...), custom_call_target="tpu_custom_call" | custom-call | tf_op jit(solution)/shard_map/backward_scatter/pallas_call | solution.py:1621
  397.9 0.9 pad_maximum_fusion.1
  398.9 0.2 reshape.95
  399.0 0.8 copy.70
  399.8 129.4 %finish_grads.1 = (f32[168,768]{1,0:T(8,128)}, f32[24,3840]{1,0:T(8,128)}, f32[336,768]{1,0:T(8,128)}, f32[24,256]{1,0:T(8,128)}, f32[24,768]{1,0:T(8,128)}, /*i...) custom-call(bf16[1024,2304]{1,0:T(8,128)(2,1)} %get-tuple-element.115.refs_0_, ...), custom_call_target="tpu_custom_call" | custom-call | tf_op jit(solution)/shard_map/finish_grads/pallas_call | solution.py:1693
  529.3 1.1 convert_element_type.25
  530.5 0.1 slice_reduce_fusion
  530.6 0.1 reshape_squeeze.6
  530.7 0.1 reshape_squeeze.7
  530.8 0.8 slice.177
  531.6 0.6 copy-done.16
  532.3 0.9 slice.179
  533.1 0.6 copy.71
  533.7 0.9 reshape.98
  534.6 0.8 slice_dynamic-update-slice_fusion
  535.5 0.6 multiply_reduce_fusion
  536.1 0.7 slice_reduce_fusion.2
  536.8 0.6 multiply_reduce_fusion.1
  538.7 0.6 multiply_reduce_fusion.2
  540.7 1.7 multiply_subtract_fusion
  542.5 1.9 fusion.17
  544.4 2.9 fusion.15
  547.4 2.5 fusion.14
  549.9 0.6 copy-done.9
  550.5 2.4 fusion.4
  552.9 0.2 copy.52
  553.1 0.1 concatenate.24
  553.3 1.0 fusion.13
  (71 shorter events, 0.5 us)
Async XLA Ops:
  0.7 13.4 %copy-start.2 = (f32[2,3840,24]{1,2,0:T(8,128)S(1)}, f32[2,3840,24]{1,2,0:T(8,128)}, u32[]{:S(2)}) copy-start(f32[2,3840,24]{1,2,0:T(8,128)} %param.36) | copy-start | bytes 2211844
  9.8 92.3 %copy-start.21 = (f32[16,384]{1,0:T(8,128)S(1)}, f32[16,384]{1,0:T(8,128)}, u32[]{:S(2)}) copy-start(f32[16,384]{1,0:T(8,128)} %constant.37.clone) | copy-start | bytes 73732
  14.1 88.3 %copy-start.20 = (bf16[4,256,16]{1,2,0:T(8,128)(2,1)S(1)}, bf16[4,256,16]{1,2,0:T(8,128)(2,1)}, u32[]{:S(2)}) copy-start(bf16[4,256,16]{1,2,0:T(8,128)(2,1)} %param.23) | copy-start | bytes 98308
  102.2 2.5 copy-start.19
  102.2 3.4 copy-start.14
  322.5 75.4 %copy-start.23 = (f32[4,6,768]{2,1,0:T(8,128)S(1)}, f32[4,6,768]{2,1,0:T(8,128)}, u32[]{:S(2)}) copy-start(f32[4,6,768]{2,1,0:T(8,128)} %get-tuple-element.124) | copy-start | bytes 221188
  322.5 75.4 %copy-start.26 = (f32[4,2,768]{2,1,0:T(2,128)S(1)}, f32[4,2,768]{2,1,0:T(2,128)}, u32[]{:S(2)}) copy-start(f32[4,2,768]{2,1,0:T(2,128)} %get-tuple-element.125) | copy-start | bytes 73732
  529.3 13.3 %copy-start.15 = (f32[768,32]{0,1:T(8,128)S(1)}, f32[768,32]{0,1:T(8,128)}, u32[]{:S(2)}) copy-start(f32[768,32]{0,1:T(8,128)} %param.39) | copy-start | bytes 294916
  529.3 15.1 %copy-start.4 = (f32[24,3840]{1,0:T(8,128)S(1)}, f32[24,3840]{1,0:T(8,128)}, u32[]{:S(2)}) copy-start(f32[24,3840]{1,0:T(8,128)} %get-tuple-element.142.refs_27_) | copy-start | bytes 1105924
  529.3 15.1 %copy-start.11 = (f32[2,3840,24]{1,2,0:T(8,128)S(1)}, f32[2,3840,24]{1,2,0:T(8,128)}, u32[]{:S(2)}) copy-start(f32[2,3840,24]{1,2,0:T(8,128)} %param.38) | copy-start | bytes 2211844
  529.3 15.1 %copy-start.12 = (f32[2,3840,24]{1,2,0:T(8,128)S(1)}, f32[2,3840,24]{1,2,0:T(8,128)}, u32[]{:S(2)}) copy-start(f32[2,3840,24]{1,2,0:T(8,128)} %param.37) | copy-start | bytes 2211844
  531.6 0.6 copy-start.16
  542.4 4.9 copy-start.1
  542.4 4.9 copy-start.3
  542.4 4.9 copy-start.5
  542.4 4.9 copy-start.6
  542.4 4.9 copy-start.13
  547.4 2.5 copy-start
  547.4 2.5 copy-start.7
  547.4 2.5 copy-start.8
  547.4 3.0 copy-start.9
  550.4 2.7 copy-start.22
  550.4 2.7 copy-start.24
  550.5 2.7 copy-start.25
  550.5 2.8 copy-start.10
  550.5 2.8 copy-start.17
  550.5 2.8 copy-start.18

commit v4 on v3

--- a/solution.py
+++ b/solution.py
@@ -465,15 +465,15 @@
 
     def greet(self):
         barrier = pltpu.get_barrier_semaphore()
-        for device in (self.sibling, self.dev_a, self.dev_b):
+
+        def hello(device):
             pl.semaphore_signal(barrier, inc=1, device_id=(device,), device_id_type=MESH_ID)
-        for sign in (-1, 1):
-
-            @pl.when(self.valid(sign))
-            def _():
-                pl.semaphore_signal(barrier, inc=1, device_id=(self.me + 8 * sign,), device_id_type=MESH_ID)
-
-        pl.semaphore_wait(barrier, 4 + self.z * (3 - self.z) // 2)
+
+        for k in range(1, 8):
+            hello(8 * self.z + lax.rem(self.me + k, 8))
+        for k in range(1, 4):
+            hello(lax.rem(self.me + 8 * k, 32))
+        pl.semaphore_wait(barrier, 10)
 
 
 def remote(src, dst, send_sem, recv_sem, device):
@@ -642,8 +642,8 @@
         self.sib, self.from_b, self.from_a, self.line, self.part, self.last = (
             bufs[count * i : count * i + count] for i in range(6)
         )
-        (self.load_sem, self.sib_send, self.sib_recv, self.b_send, self.b_recv, self.a_send, self.a_recv, self.up_send,
-         self.up_recv, self.down_send, self.down_recv, self.end_send, self.end_recv, self.end_local) = sems
+        (self.load_sem, self.sib_send, self.sib_recv, self.b_send, self.b_recv, self.a_send, self.a_recv, self.z_send,
+         self.z_recv, self.end_send, self.end_recv, self.end_local) = sems
 
     def rows_of(self, a, chip, core):
         rows, half = self.part[a].shape
@@ -687,10 +687,13 @@
             self.own(a, 0, 1, z), self.from_a[a].at[z], self.a_send.at[a, z], self.a_recv.at[a, z], self.p.dev_a
         )
 
-    def to_z(self, a, z, sign, slot):
-        send, recv = (self.up_send, self.up_recv) if sign > 0 else (self.down_send, self.down_recv)
+    def to_z(self, a, target, source):
         return remote(
-            self.own(a, 0, 0, z), self.line[a].at[slot], send.at[a, z], recv.at[a, z], self.p.me + 8 * sign
+            self.own(a, 0, 0, target),
+            self.line[a].at[source],
+            self.z_send.at[a, target],
+            self.z_recv.at[a, source],
+            self.p.me + 8 * (target - self.p.z),
         )
 
     def open(self, z):
@@ -733,31 +736,10 @@
             self.to_a(a, z).wait_recv()
             self.part[a][...] = value + self.from_a[a][z].astype(jnp.float32)
 
-            @pl.when(jnp.logical_and(place.z < z, place.z > 0))
-            def _():
-                self.to_z(a, z, 1, z).wait_recv()
-                self.part[a][...] += self.line[a][z].astype(jnp.float32)
-
-            @pl.when(jnp.logical_and(place.z > z, place.z < 3))
-            def _():
-                self.to_z(a, z, -1, z).wait_recv()
-                self.part[a][...] += self.line[a][z].astype(jnp.float32)
-
             @pl.when(place.z != z)
             def _():
                 self.own(a, 0, 0, z)[...] = self.part[a][...].astype(jnp.bfloat16)
-
-            @pl.when(place.z < z)
-            def _():
-                self.to_z(a, z, 1, z).start()
-
-            @pl.when(place.z > z + 1)
-            def _():
-                self.to_z(a, z, -1, z).start()
-
-            @pl.when(place.z == z + 1)
-            def _():
-                self.to_z(a, z, -1, 4).start()
+                self.to_z(a, z, place.z).start()
 
             @pl.when(place.z == z)
             def _():
@@ -780,19 +762,15 @@
         return away, keep
 
     def close(self):
-        place = self.p
         for a in self.arrays:
 
-            @pl.when(place.z > 0)
-            def _():
-                self.to_z(a, place.z, 1, place.z).wait_recv()
-                self.last[a][...] += self.line[a][place.z].astype(jnp.float32)
-
-            @pl.when(place.z < 3)
-            def _():
-                self.to_z(a, place.z, -1, 4).wait_recv()
-                self.last[a][...] += self.line[a][4].astype(jnp.float32)
-
+            def add(k, carry):
+                source = lax.rem(self.p.z + k, 4)
+                self.to_z(a, self.p.z, source).wait_recv()
+                self.last[a][...] += self.line[a][source].astype(jnp.float32)
+                return carry
+
+            lax.fori_loop(1, 4, add, 0)
             for copy in self.end_copies(a):
                 copy.start()
 
@@ -811,36 +789,28 @@
                     self.to_b(a, flip_a, z).wait_send()
                 self.to_a(a, z).wait_send()
 
-                @pl.when(self.p.z < z)
+                @pl.when(self.p.z != z)
                 def _():
-                    self.to_z(a, z, 1, z).wait_send()
-
-                @pl.when(self.p.z > z)
-                def _():
-                    self.to_z(a, z, -1, z).wait_send()
+                    self.to_z(a, z, self.p.z).wait_send()
 
             return carry
 
         lax.fori_loop(0, 4, step, 0)
 
     def steps(self):
-        out = []
-        for k in range(6):
-            if k < 4:
-                out.append(functools.partial(self.cross_b, ORDER[k]))
-            if 0 <= k - 1 < 4:
-                out.append(functools.partial(self.cross_a, ORDER[k - 1]))
-            if 0 <= k - 2 < 4:
-                out.append(functools.partial(self.along_z, ORDER[k - 2]))
-        return out + [self.close, self.end, self.finish]
+        z0, z1, z2, z3 = ORDER
+        work = [(self.cross_b, z) for z in ORDER]
+        work += [(self.cross_a, z0), (self.cross_a, z1), (self.along_z, z0), (self.cross_a, z2), (self.along_z, z1)]
+        work += [(self.cross_a, z3), (self.along_z, z2), (self.along_z, z3)]
+        return [functools.partial(step, z) for step, z in work] + [self.close, self.end, self.finish]
 
 
 def scatter_scratch(shapes):
     scratch = []
-    for count, kind in ((16, jnp.bfloat16), (8, jnp.bfloat16), (4, jnp.bfloat16), (5, jnp.bfloat16),
+    for count, kind in ((16, jnp.bfloat16), (8, jnp.bfloat16), (4, jnp.bfloat16), (4, jnp.bfloat16),
                         (0, jnp.float32), (0, jnp.float32)):
         scratch += [pltpu.VMEM(((count,) if count else ()) + shape, kind) for shape in shapes]
-    counts = (16, 16, 16, 8, 8, 4, 4, 4, 4, 4, 4)
+    counts = (16, 16, 16, 8, 8, 4, 4, 4, 4)
     several = len(shapes)
     return (
         scratch
@@ -869,68 +839,100 @@
     return gate * (1 + value * (1 - gate))
 
 
+PLANE, LINE = 8, 4
+
+
 class Swap:
-    def __init__(self, me, devices, index, src_of, dst, send, recv):
-        self.me, self.n, self.i, self.src_of, self.dst, self.send, self.recv = me, devices, index, src_of, dst, send, recv
-
-    def copy(self, peer, slot):
-        return remote(self.src_of(peer), self.dst.at[slot], self.send.at[self.i, peer], self.recv.at[self.i, slot], peer)
-
-    def each(self, step):
+    def __init__(self, index, sems, full, away=None, mid=None, reduce=None):
+        self.i, self.sems, self.full, self.away, self.mid = index, sems, full, away, mid
+        self.second = mid if reduce is None else reduce
+        self.me = lax.axis_index(AXIS)
+        self.z, self.p = self.me // PLANE, self.me % PLANE
+        self.spread = away is None
+
+    def plane(self, peer, slot):
+        send, recv = self.sems
+        if self.spread:
+            src, dst = self.full.at[:, self.p], self.full.at[:, slot]
+        else:
+            src, dst = self.away.at[:, peer], self.mid.at[:, slot]
+        return remote(src, dst, send.at[self.i, peer], recv.at[self.i, slot], self.me + peer - self.p)
+
+    def line(self, peer, slot):
+        send, recv = self.sems
+        if self.spread:
+            src, dst = self.full.at[self.z, self.p], self.full.at[slot, self.p]
+        else:
+            src, dst = self.second.at[peer], self.full.at[slot]
+        return remote(
+            src, dst, send.at[self.i, PLANE + peer], recv.at[self.i, PLANE + slot], self.me + PLANE * (peer - self.z)
+        )
+
+    def each(self, in_plane, step):
+        mine, count = (self.p, PLANE) if in_plane else (self.z, LINE)
+
         def run(k, carry):
-            step(lax.rem(self.me + k, self.n))
+            step(lax.rem(mine + k, count))
             return carry
 
-        lax.fori_loop(1, self.n, run, 0)
+        lax.fori_loop(1, count, run, 0)
+
+    def hop(self, in_plane):
+        make, slot = (self.plane, self.p) if in_plane else (self.line, self.z)
+        self.each(in_plane, lambda peer: make(peer, slot).start())
+
+    def come(self, in_plane):
+        make = self.plane if in_plane else self.line
+        self.each(in_plane, lambda peer: make(peer, peer).wait_recv())
 
     def start(self):
-        self.each(lambda peer: self.copy(peer, self.me).start())
+        if not self.spread:
+            for k in range(LINE):
+                self.mid[k, self.p] = self.away[k, self.p]
+        self.hop(not self.spread)
+
+    def between(self, work=None):
+        self.come(not self.spread)
+        if work is not None:
+            work()
+        self.hop(self.spread)
+        if not self.spread:
+            self.full[self.z] = self.second[self.z]
 
     def arrive(self):
-        self.each(lambda peer: self.copy(peer, peer).wait_recv())
+        self.come(self.spread)
 
     def sent(self):
-        self.each(lambda peer: self.copy(peer, self.me).wait_send())
-
-
-def greet_all(devices):
-    barrier = pltpu.get_barrier_semaphore()
-    me = lax.axis_index(AXIS)
-
-    def hello(k, carry):
-        pl.semaphore_signal(barrier, inc=1, device_id=(lax.rem(me + k, devices),), device_id_type=MESH_ID)
-        return carry
-
-    lax.fori_loop(1, devices, hello, 0)
-    pl.semaphore_wait(barrier, devices - 1)
+        self.each(True, lambda peer: self.plane(peer, self.p).wait_send())
+        self.each(False, lambda peer: self.line(peer, self.z).wait_send())
 
 
 def modulate_steps(devices, ins, outs, bufs, sems):
     msg, wt1, wt2, wcls, wcond, bt1, bt2, bcond = ins
     mods, pre, cond, hid_all, low_all, feat_all, lab_all, got = outs
-    hid, low, away = bufs
+    hid, low, away, mid = bufs
     me = lax.axis_index(AXIS)
+    z, place = me // PLANE, me % PLANE
     images, cols = 4, wt1.shape[0]
-    swaps = [
-        Swap(me, devices, 0, lambda peer: msg, got, *sems),
-        Swap(me, devices, 1, lambda peer: hid.at[me], hid, *sems),
-        Swap(me, devices, 2, lambda peer: low.at[me], low, *sems),
-        Swap(me, devices, 3, lambda peer: away.at[peer], mods, *sems),
-    ]
+    swaps = [Swap(0, sems, got), Swap(1, sems, hid), Swap(2, sems, low), Swap(3, sems, mods, away, mid)]
 
     def first():
+        got[z, place] = msg[...]
         swaps[0].start()
-        got[me] = msg[...]
 
     def second():
         swaps[0].arrive()
         for j in range(devices):
-            feat_all[images * j : images * (j + 1), :] = got[j, :, :FREQ]
-            lab_all[images * j : images * (j + 1), :] = got[j, :, FREQ : FREQ + 128]
+            at = slice(images * j, images * (j + 1))
+            block = got[j // PLANE, j % PLANE].astype(jnp.float32)
+            feat_all[at, :128] = block[:images]
+            feat_all[at, 128:] = block[images : 2 * images]
+            digits = block[3 * images : 4 * images]
+            lab_all[at, :] = jnp.broadcast_to(32.0 * digits[:, :1] + digits[:, 64:65], (images, 128))
         pre[...] = dot_nt(wt1[...].astype(jnp.bfloat16), feat_all[...].astype(jnp.bfloat16)) + bt1[...]
         hidden = silu(pre[...])
-        pad = jnp.zeros((hid.shape[1] - cols, hidden.shape[1]), jnp.float32)
-        hid[me] = jnp.concatenate([hidden, pad], 0).astype(jnp.bfloat16)
+        pad = jnp.zeros((hid.shape[2] - cols, hidden.shape[1]), jnp.float32)
+        hid[z, place] = jnp.concatenate([hidden, pad], 0).astype(jnp.bfloat16)
         swaps[1].start()
         classes = lax.broadcasted_iota(jnp.int32, (lab_all.shape[0], wcls.shape[1]), 1).astype(jnp.float32)
         labels = jnp.concatenate([lab_all[...]] * (wcls.shape[1] // 128), 1)
@@ -940,31 +942,31 @@
     def third():
         swaps[1].arrive()
         for j in range(devices):
-            hid_all[cols * j : cols * (j + 1), :] = hid[j].astype(jnp.float32)[:cols]
+            hid_all[cols * j : cols * (j + 1), :] = hid[j // PLANE, j % PLANE].astype(jnp.float32)[:cols]
         cond[...] += jnp.dot(
             wt2[...].astype(jnp.bfloat16), hid_all[...].astype(jnp.bfloat16), preferred_element_type=jnp.float32
         )
         value = silu(cond[...])
-        pad = jnp.zeros((low.shape[1] - cols, value.shape[1]), jnp.float32)
-        low[me] = jnp.concatenate([value, pad], 0).astype(jnp.bfloat16)
+        pad = jnp.zeros((low.shape[2] - cols, value.shape[1]), jnp.float32)
+        low[z, place] = jnp.concatenate([value, pad], 0).astype(jnp.bfloat16)
         swaps[2].start()
 
     def fourth():
         swaps[2].arrive()
         for j in range(devices):
-            low_all[cols * j : cols * (j + 1), :] = low[j].astype(jnp.float32)[:cols]
+            low_all[cols * j : cols * (j + 1), :] = low[j // PLANE, j % PLANE].astype(jnp.float32)[:cols]
         rows = dot_nt(low_all[...].T.astype(jnp.bfloat16), wcond[...].astype(jnp.bfloat16)) + bcond[...]
         for j in range(devices):
-            away[j] = rows[images * j : images * (j + 1)]
+            away[j // PLANE, j % PLANE] = rows[images * j : images * (j + 1)]
         swaps[3].start()
-        mods[me] = away[me]
 
     def last():
         swaps[3].arrive()
         for swap in swaps:
             swap.sent()
 
-    return [first, second, third, fourth, last]
+    between = [swap.between for swap in swaps]
+    return [first, between[0], second, between[1], third, between[2], fourth, between[3], last]
 
 
 SETTLE_INS = ("d_mods", "wt2", "wcond", "pre", "cond", "hid_all", "low_all", "feat_all", "lab_all", "g_head", "g_hbias", "loss",
@@ -974,27 +976,37 @@
 def settle_steps(devices, ins, outs, bufs, sems, shards):
     d_mods, pre, lab_all = ins["d_mods"], ins["pre"], ins["lab_all"]
     g_cond, g_t1, g_t2, g_cls, merged = outs
-    dm_got, dm_all, rows, small, small_got, dc_part, dc_got, dh_part, dh_got, note = bufs
+    dm_mid, dm_got, dm_all, rows, small, small_mid, small_sum, small_got = bufs[:8]
+    dc_part, dc_mid, dc_sum, dc_got, dh_part, dh_mid, dh_sum, dh_got = bufs[8:]
     me = lax.axis_index(AXIS)
-    images, width = d_mods.shape[1:]
+    images, width = d_mods.shape[2:]
     cols = pre.shape[0]
     swaps = [
-        Swap(me, devices, 0, lambda peer: d_mods.at[peer], dm_got, *sems),
-        Swap(me, devices, 1, lambda peer: small.at[peer], small_got, *sems),
-        Swap(me, devices, 2, lambda peer: dc_part.at[peer], dc_got, *sems),
-        Swap(me, devices, 3, lambda peer: dh_part.at[peer], dh_got, *sems),
-        Swap(me, devices, 4, lambda peer: note, merged, *sems),
+        Swap(0, sems, dm_got, d_mods, dm_mid),
+        Swap(1, sems, small_got, small, small_mid, small_sum),
+        Swap(2, sems, dc_got, dc_part, dc_mid, dc_sum),
+        Swap(3, sems, dh_got, dh_part, dh_mid, dh_sum),
+        Swap(4, sems, merged),
     ]
     keep = {}
 
-    def share(value, part, got):
+    def share(value, part):
         pad = jnp.zeros((32 - cols, value.shape[1]), jnp.float32)
         for j in range(devices):
-            part[j] = jnp.concatenate([value[cols * j : cols * (j + 1)], pad], 0).astype(jnp.bfloat16)
-        got[me] = part[me]
-
-    def collect(got):
-        return jnp.sum(got[...].astype(jnp.float32), 0)[:cols]
+            part[j // PLANE, j % PLANE] = jnp.concatenate([value[cols * j : cols * (j + 1)], pad], 0).astype(jnp.bfloat16)
+
+    def add_plane(mid, total):
+        for k in range(LINE):
+            total[k] = jnp.sum(mid[k].astype(jnp.float32), 0)
+
+    def add_small():
+        add_plane(small_mid, small_sum)
+
+    def add_dc():
+        add_plane(dc_mid, dc_sum)
+
+    def add_dh():
+        add_plane(dh_mid, dh_sum)
 
     def parts_of(value):
         return sum(
@@ -1004,7 +1016,6 @@
 
     def first():
         swaps[0].start()
-        dm_got[me] = d_mods[me]
         dm_all[...] = jnp.zeros_like(dm_all)
         rows[...] = jnp.zeros_like(rows)
         for k in range(MODEL_WIDTH // 128):
@@ -1020,29 +1031,27 @@
         diagonal = lax.broadcasted_iota(jnp.int32, square, 0) == lax.broadcasted_iota(jnp.int32, square, 1)
         rows[at : at + 1, :] = jnp.sum(jnp.where(diagonal, ins["g_hbias"][...], 0.0), 0, keepdims=True)
         for j in range(devices):
-            small[j] = rows[16 * j : 16 * (j + 1), :].astype(jnp.bfloat16)
-        swaps[1].start()
-        small_got[me] = small[me]
+            small[j // PLANE, j % PLANE] = rows[16 * j : 16 * (j + 1), :].astype(jnp.bfloat16)
 
     def second():
         swaps[0].arrive()
         for j in range(devices):
-            dm_all[images * j : images * (j + 1), :width] = dm_got[j]
+            dm_all[images * j : images * (j + 1), :width] = dm_got[j // PLANE, j % PLANE]
         turned = dm_all[...].T[:width]
         parts = thirds(turned)
         weight = ins["wcond"][...].astype(jnp.bfloat16)
-        share(sum(dot_tn(weight, part) for part in parts), dc_part, dc_got)
+        share(sum(dot_tn(weight, part) for part in parts), dc_part)
         swaps[2].start()
+        swaps[1].start()
         low = ins["low_all"][...].astype(jnp.bfloat16)
         g_cond[...] = sum(dot_nt(part, low) for part in parts)
-        swaps[1].arrive()
 
     def third():
         swaps[2].arrive()
-        d_cond = collect(dc_got) * silu_slope(ins["cond"][...])
+        d_cond = jnp.sum(dc_got[...], 0)[:cols] * silu_slope(ins["cond"][...])
         parts = thirds(d_cond)
         weight = ins["wt2"][...].astype(jnp.bfloat16)
-        share(sum(dot_tn(weight, part) for part in parts), dh_part, dh_got)
+        share(sum(dot_tn(weight, part) for part in parts), dh_part)
         swaps[3].start()
         classes = lax.broadcasted_iota(jnp.int32, (lab_all.shape[0], g_cls.shape[1]), 1).astype(jnp.float32)
         labels = jnp.concatenate([lab_all[...]] * (g_cls.shape[1] // 128), 1)
@@ -1054,8 +1063,9 @@
         keep["t2"] = sum(dot_nt(ones, part) for part in parts)
 
     def fourth():
+        swaps[1].arrive()
         swaps[3].arrive()
-        d_pre = collect(dh_got) * silu_slope(pre[...])
+        d_pre = jnp.sum(dh_got[...], 0)[:cols] * silu_slope(pre[...])
         parts = thirds(d_pre)
         feats = ins["feat_all"][...].astype(jnp.bfloat16)
         g_t1[...] = sum(jnp.dot(part, feats, preferred_element_type=jnp.float32) for part in parts)
@@ -1077,16 +1087,23 @@
         lines.append(parts_of(ins["loss"][0:1, :]))
         lines += [bias_cond[:, 128 * k : 128 * (k + 1)] for k in range(3)]
         lines.append(jnp.zeros((9, 128), jnp.float32))
-        note[...] = jnp.concatenate([jnp.sum(small_got[...].astype(jnp.float32), 0)] + lines, 0).astype(jnp.bfloat16)
+        lines.insert(0, jnp.sum(small_got[...], 0))
+        merged[me // PLANE, me % PLANE] = jnp.concatenate(lines, 0).astype(jnp.bfloat16)
         swaps[4].start()
-        merged[me] = note[...]
+        swaps[4].between()
 
     def last():
         swaps[4].arrive()
         for swap in swaps:
             swap.sent()
 
-    return [first, second, third, fourth, message, last]
+    betweens = [
+        swaps[0].between,
+        functools.partial(swaps[1].between, add_small),
+        functools.partial(swaps[2].between, add_dc),
+        functools.partial(swaps[3].between, add_dh),
+    ]
+    return [first, second, third, fourth, message, last], betweens
 
 
 def dot_nn(left, right):
@@ -1414,43 +1431,44 @@
 def start_kernel(devices, *refs):
     own, mod_ins, refs = refs[:2], refs[2:10], refs[10:]
     full, mod_outs, refs = refs[:2], refs[2:10], refs[10:]
-    part, mod_bufs, mod_sems = refs[:10], refs[10:13], refs[13:]
-    greet_all(devices)
+    part, mod_bufs, mod_sems = refs[:10], refs[10:14], refs[14:]
     place = Place()
-    job = Gather(place, own, part[:2], part[2:4], full, part[4:])
-    first, second, third, fourth, last = modulate_steps(devices, mod_ins, mod_outs, mod_bufs, mod_sems)
+    place.greet()
+    job = Gather(place, [ref.at[0] for ref in own], part[:2], part[2:4], full, part[4:])
+    parts = modulate_steps(devices, mod_ins, mod_outs, mod_bufs, mod_sems)
     moves = gather_steps(job)
-    for step in START_ORDER(first, second, third, fourth, last, moves):
-        step()
-
-
-def START_ORDER(first, second, third, fourth, last, moves):
-    return [first] + moves[:2] + [second] + moves[2:4] + [third] + moves[4:6] + [fourth] + moves[6:-1] + [last, moves[-1]]
+    for kind in START_ORDER:
+        (parts if kind == "a" else moves).pop(0)()
+
+
+START_ORDER = "ag" "aa" "gg" "a" "g" "a" "g" "a" "g" "a" "gg" "a" "gggggggg" "a" "g"
 
 
 def gather_modulate(pair, ins):
     devices = lax.axis_size(AXIS)
     msg, wt1, wt2, wcls, wcond = ins[:5]
-    cols, images = wt1.shape[0], devices * msg.shape[0]
+    cols, images = wt1.shape[0], ins[5].shape[1]
     outs = [
-        (devices, msg.shape[0], wcond.shape[0]), (cols, images), (cols, images), (devices * cols, images),
-        (devices * cols, images), (images, FREQ), (images, 128), (devices,) + msg.shape,
+        (LINE, PLANE, images // devices, wcond.shape[0]), (cols, images), (cols, images), (devices * cols, images),
+        (devices * cols, images), (images, FREQ), (images, 128),
     ]
     padded = -(-cols // 16) * 16
     vmem = pl.BlockSpec(memory_space=pltpu.VMEM)
     return pl.pallas_call(
         functools.partial(start_kernel, devices),
-        out_shape=[jax.ShapeDtypeStruct((devices * a.shape[0], a.shape[1]), jnp.bfloat16) for a in pair]
-        + [jax.ShapeDtypeStruct(shape, jnp.float32) for shape in outs],
+        out_shape=[full_shape(a) for a in pair]
+        + [jax.ShapeDtypeStruct(shape, jnp.float32) for shape in outs]
+        + [jax.ShapeDtypeStruct((LINE, PLANE) + msg.shape, jnp.bfloat16)],
         in_specs=[vmem] * 10,
         out_specs=[pl.BlockSpec(memory_space=pl.ANY)] * 2 + [vmem] * 8,
-        scratch_shapes=gather_scratch(piece_shapes([a.shape for a in pair]))
+        scratch_shapes=gather_scratch(piece_shapes([a.shape[1:] for a in pair]))
         + [
-            pltpu.VMEM((devices, padded, images), jnp.bfloat16),
-            pltpu.VMEM((devices, padded, images), jnp.bfloat16),
-            pltpu.VMEM((devices, msg.shape[0], wcond.shape[0]), jnp.float32),
-            pltpu.SemaphoreType.DMA((4, devices)),
-            pltpu.SemaphoreType.DMA((4, devices)),
+            pltpu.VMEM((LINE, PLANE, padded, images), jnp.bfloat16),
+            pltpu.VMEM((LINE, PLANE, padded, images), jnp.bfloat16),
+            pltpu.VMEM((LINE, PLANE, images // devices, wcond.shape[0]), jnp.float32),
+            pltpu.VMEM((LINE, PLANE, images // devices, wcond.shape[0]), jnp.float32),
+            pltpu.SemaphoreType.DMA((4, LINE + PLANE)),
+            pltpu.SemaphoreType.DMA((4, LINE + PLANE)),
         ],
         compiler_params=pltpu.CompilerParams(collective_id=3, has_side_effects=True, vmem_limit_bytes=56 << 20),
         name="gather_modulate",
@@ -1464,7 +1482,7 @@
     outs, x_out, full, refs = refs[:10], refs[10], refs[11:13], refs[13:]
     vm_in, vm_out, sems, part = refs[0], refs[1], refs[2], refs[3:]
     place = Place()
-    job = Gather(place, (own_in, own_out), part[:2], part[2:4], full, part[4:])
+    job = Gather(place, (own_in.at[0], own_out.at[0]), part[:2], part[2:4], full, part[4:])
     hooks = Hooks([place.greet] + gather_steps(job), slots, FORWARD_POINTS)
     weights = Weights((w_in, w_out), (vm_in, vm_out), sems)
     weights.start((0, 1, 2, 3))
@@ -1474,9 +1492,16 @@
 GATHER_SLOTS = (0, 0, 13, 15, 26, 28, 39, 41, 50) + (34, 43, 48, 51, 51, 51, 51, 51, 51)
 
 
-def forward_gather(ins, pair):
+def layer_block(array, layer):
+    return pl.BlockSpec((1,) + array.shape[1:], lambda i: (layer, 0, 0))
+
+
+def full_shape(array):
+    return jax.ShapeDtypeStruct((lax.axis_size(AXIS) * array.shape[1], array.shape[2]), jnp.bfloat16)
+
+
+def forward_gather(ins, pair, layer):
     images = ins[1].shape[0]
-    devices = lax.axis_size(AXIS)
     shapes, specs = kept_shapes(images)
     any_block = pl.BlockSpec(memory_space=pl.ANY)
     return pl.pallas_call(
@@ -1484,10 +1509,10 @@
         grid=(images,),
         out_shape=shapes
         + [jax.ShapeDtypeStruct((images * SEQ, MODEL_WIDTH), jnp.float32)]
-        + [jax.ShapeDtypeStruct((devices * a.shape[0], a.shape[1]), jnp.bfloat16) for a in pair],
-        in_specs=forward_specs() + [whole_block(*a.shape) for a in pair],
+        + [full_shape(a) for a in pair],
+        in_specs=forward_specs() + [layer_block(a, layer) for a in pair],
         out_specs=specs + [token_block(MODEL_WIDTH)] + [any_block] * 2,
-        scratch_shapes=WEIGHT_SCRATCH + gather_scratch(piece_shapes([a.shape for a in pair])),
+        scratch_shapes=WEIGHT_SCRATCH + gather_scratch(piece_shapes([a.shape[1:] for a in pair])),
         compiler_params=pltpu.CompilerParams(collective_id=1, has_side_effects=True, vmem_limit_bytes=58 << 20),
         name="forward_gather",
     )(*ins, *pair)
@@ -1607,7 +1632,7 @@
     g_pbias[...] += jnp.sum(d_patch.astype(jnp.float32), 0, keepdims=True)
 
 
-SCATTER_SLOTS = (0, 0, 3, 6, 10, 14, 18, 22, 26, 29, 33, 37, 41, 45, 49, 51, 51)
+SCATTER_SLOTS = (0, 0, 3, 6, 10, 13, 18, 25, 27, 32, 34, 38, 42, 51, 51, 51, 51)
 
 
 def backward_scatter(mods, w_in, w_out, refs, grad, lat_t, shape):
@@ -1639,42 +1664,48 @@
     ins, set_ins, refs = refs[:8], dict(zip(SETTLE_INS, refs[8 : 8 + count])), refs[8 + count :]
     totals, set_outs, refs = refs[:2], refs[2:7], refs[7:]
     bufs, keep_in, keep_out, load_sems, refs = refs[:7], refs[7], refs[8], refs[9], refs[10:]
-    sc_bufs, sc_sems, refs = refs[:12], refs[12:26], refs[26:]
-    set_bufs, set_sems = refs[:10], refs[10:]
+    sc_bufs, sc_sems, refs = refs[:12], refs[12:24], refs[24:]
+    set_bufs, set_sems = refs[:16], refs[16:]
     work = Grads(ins, bufs, keep_in, keep_out, load_sems)
     work.start()
-    greet_all(devices)
     place = Place()
+    place.greet()
     job = Scatter(place, [keep_in, keep_out], totals, sc_bufs, sc_sems)
-    first, second, third, fourth, message, last = settle_steps(devices, set_ins, set_outs, set_bufs, set_sems, totals)
+    (first, second, third, fourth, message, last), betweens = settle_steps(
+        devices, set_ins, set_outs, set_bufs, set_sems, totals
+    )
     first()
     work.rows_out(1)
+    betweens[0]()
     work.rows_in(5)
     work.rows_in(6)
+    second()
     job.open(3)
+    work.rows_out(0)
+    betweens[2]()
     job.cross_b(3)
-    second()
-    work.rows_out(0)
     work.rows_in(0)
     work.rows_in(1)
     job.open(0)
+    third()
+    work.rows_in(3)
     job.cross_b(0)
-    job.cross_a(3)
-    work.rows_in(3)
     work.rows_in(4)
     job.open(2)
+    job.cross_a(3)
+    work.rows_in(2)
     job.cross_b(2)
-    third()
+    job.open(1)
     job.cross_a(0)
-    work.rows_in(2)
-    job.open(1)
     job.along_z(3)
     job.cross_b(1)
+    betweens[1]()
+    betweens[3]()
     job.cross_a(2)
-    fourth()
     job.along_z(0)
     job.cross_a(1)
     job.along_z(2)
+    fourth()
     job.along_z(1)
     job.close()
     job.end()
@@ -1693,24 +1724,31 @@
     return pl.pallas_call(
         functools.partial(finish_kernel, devices),
         out_shape=[jax.ShapeDtypeStruct(shape, jnp.float32) for shape in list(shapes) + outs]
-        + [jax.ShapeDtypeStruct((devices, 32, 128), low)],
+        + [jax.ShapeDtypeStruct((LINE, PLANE, 32, 128), low)],
         in_specs=[pl.BlockSpec(memory_space=pl.ANY)] * 8 + [vmem] * len(SETTLE_INS),
         out_specs=[vmem] * 7,
         scratch_shapes=grad_bufs(ins)
         + scatter_scratch(piece_shapes(shapes))
         + [
             pltpu.VMEM(d_mods.shape, jnp.float32),
+            pltpu.VMEM(d_mods.shape, jnp.float32),
             pltpu.VMEM((images, 384), jnp.float32),
             pltpu.VMEM((devices * 16, 128), jnp.float32),
-            pltpu.VMEM((devices, 16, 128), low),
-            pltpu.VMEM((devices, 16, 128), low),
-            pltpu.VMEM((devices, 32, images), low),
-            pltpu.VMEM((devices, 32, images), low),
-            pltpu.VMEM((devices, 32, images), low),
-            pltpu.VMEM((devices, 32, images), low),
-            pltpu.VMEM((32, 128), low),
-            pltpu.SemaphoreType.DMA((5, devices)),
-            pltpu.SemaphoreType.DMA((5, devices)),
+            pltpu.VMEM((LINE, PLANE, 16, 128), low),
+            pltpu.VMEM((LINE, PLANE, 16, 128), low),
+            pltpu.VMEM((LINE, 16, 128), jnp.float32),
+            pltpu.VMEM((LINE, 16, 128), jnp.float32),
+        ]
+        + [
+            pltpu.VMEM((LINE, PLANE, 32, images), low),
+            pltpu.VMEM((LINE, PLANE, 32, images), low),
+            pltpu.VMEM((LINE, 32, images), jnp.float32),
+            pltpu.VMEM((LINE, 32, images), jnp.float32),
+        ]
+        * 2
+        + [
+            pltpu.SemaphoreType.DMA((5, LINE + PLANE)),
+            pltpu.SemaphoreType.DMA((5, LINE + PLANE)),
         ],
         compiler_params=pltpu.CompilerParams(collective_id=4, has_side_effects=True, vmem_limit_bytes=63 << 20),
         name="finish_grads",
@@ -1748,10 +1786,11 @@
     out_t = layer_output_weights.transpose(0, 2, 1)
     cols, cond_cols = embed_t.shape[0], cond_t.shape[0]
     time_one, time_two, patch_bias, cond_bias, block_input_bias, block_output_bias, head_bias = split_biases(biases)
-    features = time_features(timesteps).astype(jnp.bfloat16).astype(jnp.float32)
-    label_rows = jnp.broadcast_to(labels.astype(jnp.float32)[:, None], (images, 128))
-    own_patch_w = embed_t[:, FREQ + MODEL_WIDTH : FREQ + MODEL_WIDTH + PD].reshape(3, 128)
-    note = jnp.concatenate([features, label_rows, jnp.pad(own_patch_w, ((0, images - 3), (0, 0)))], 1)
+    features = time_features(timesteps)
+    own_patch_w = jnp.pad(embed_t[:, FREQ + MODEL_WIDTH : FREQ + MODEL_WIDTH + PD].reshape(3, 128), ((0, 1), (0, 0)))
+    digits = jnp.stack([labels // 32, labels % 32], 1).astype(jnp.float32)
+    digits = jnp.broadcast_to(digits[:, :, None], (images, 2, 64)).reshape(images, 128)
+    note = jnp.concatenate([features[:, :128], features[:, 128:], own_patch_w, digits], 0).astype(jnp.bfloat16)
     w_t1 = embed_t[:, :FREQ]
     w_t2 = embed_t[:, FREQ : FREQ + MODEL_WIDTH]
     w_class = jnp.pad(embed_t[:, FREQ + MODEL_WIDTH + PD :], ((0, 0), (0, 1024 - NCLS)))
@@ -1763,11 +1802,11 @@
 
     own_cond_bias = lax.dynamic_slice(cond_bias, (me * cond_cols,), (cond_cols,))[None]
     first_in, first_out, mods, pre, cond, hid_all, low_all, feat_all, lab_all, notes = gather_modulate(
-        [in_t[0], out_t[0]],
+        [in_t, out_t],
         [note, w_t1, w_t2, w_class, cond_t, own_bias(time_one, cols), own_bias(time_two, cols), own_cond_bias],
     )
-    chunks = mods.transpose(1, 0, 2).reshape(images, 6 * LAYERS + 2, MODEL_WIDTH)
-    w_patch = notes[:, :3, FREQ + 128 :].reshape(MODEL_WIDTH, PD).astype(jnp.bfloat16)
+    chunks = mods.reshape(devices, images, cond_cols).transpose(1, 0, 2).reshape(images, 6 * LAYERS + 2, MODEL_WIDTH)
+    w_patch = notes[:, :, 8:11].reshape(MODEL_WIDTH, PD)
     x = (rows_t(latents, w_patch) + patch_bias + position_sum()).reshape(images * SEQ, MODEL_WIDTH)
     block_mods = [chunks[:, 6 * i : 6 * (i + 1)] for i in range(LAYERS)]
     head_t = head_w.T
@@ -1775,7 +1814,7 @@
     lat_t = latents.transpose(0, 2, 1)
     bias_rows = [(block_input_bias[i][None], block_output_bias[i][None]) for i in range(LAYERS)]
     *kept0, x_mid, last_in, last_out = forward_gather(
-        [x, block_mods[0], first_in, first_out, *bias_rows[0]], [in_t[1], out_t[1]]
+        [x, block_mods[0], first_in, first_out, *bias_rows[0]], [in_t, out_t], 1
     )
     *kept1, upstream, d_final, head_grad, head_bias_grad, loss_part = forward_head(
         [x_mid, block_mods[1], last_in, last_out, *bias_rows[1], chunks[:, 6 * LAYERS :], head_t, head_bias[:, None],
@@ -1795,6 +1834,7 @@
     mod_grads, in_bias_grads, out_bias_grads = [mod_grad0, mod_grad1], [in_bias0, in_bias1], [out_bias0, out_bias1]
     d_modulation = jnp.concatenate(mod_grads + [d_final], 1)
     d_mods = d_modulation.reshape(images, devices, cond_cols).transpose(1, 0, 2)
+    d_mods = d_mods.reshape(LINE, PLANE, images, cond_cols)
     in_shard0, out_shard0, g_cond, g_t1, g_t2, g_cls, merged = finish_grads(
         [d_qkv, h1, d_u, h2, d_a, o, d_f, g],
         [in_shape, out_shape],
@@ -1805,7 +1845,7 @@
             "bout0": out_bias_grads[0], "bout1": out_bias_grads[1], "done_in": in_shard1, "done_out": out_shard1,
         },
     )
-    merged = merged.astype(jnp.float32)
+    merged = merged.astype(jnp.float32).reshape(devices, 32, 128)
     wide = MODEL_WIDTH // 128
     blocks = merged[:, :16]
     patch_total = blocks[:wide].transpose(1, 0, 2).reshape(PD, MODEL_WIDTH)

time: 565 us -> 541 us (0.958)
  Pallas kernels: 504 us -> 485 us
    pallas_call x1, Pallas kernels: 75.4 us -> 66.1 us  [backward_scatter(): pl.pallas_call(functools.partial(backward_scatter_kernel, SCATTER_SLOTS),...]
    pallas_call x1, Pallas kernels: 129 us -> 121 us  [finish_grads(): pl.pallas_call(functools.partial(finish_kernel, devices), out_shape=[jax....]
where the time goes in v4:
time: 541 us; the launch traced here: 532 us
  Pallas kernels  485 us (90%)
  local copies, waits for them, and re-layouts  20.3 us (4%)
  other arithmetic  19.1 us (4%)
  between operations  5.45 us (1%)
    pallas_call x1, Pallas kernels, finish_grads(): pl.pallas_call(functools.partial(finish_kernel, devices), out_shape=[jax....  121 us
    pallas_call x1, Pallas kernels, gather_modulate(): pl.pallas_call(functools.partial(start_kernel, devices), out_shape=[full_...  87.2 us
    pallas_call x1, Pallas kernels, forward_gather(): pl.pallas_call(functools.partial(forward_gather_kernel, GATHER_SLOTS), gr...  74.4 us
    pallas_call x1, Pallas kernels, backward_scatter(): pl.pallas_call(functools.partial(backward_scatter_kernel, SCATTER_SLOTS),...  66.1 us
    pallas_call x1, Pallas kernels, backward_block(): pl.pallas_call(backward_kernel, grid=(images,), out_shape=[jax.ShapeDtype...  49.8 us
    pallas_call x1, Pallas kernels, weight_grads_out(): pl.pallas_call(grads_out_kernel, out_shape=[jax.ShapeDtypeStruct((IW, MOD...  43.8 us
    pallas_call x1, Pallas kernels, forward_head(): pl.pallas_call(functools.partial(head_kernel, scale_out), grid=(images,),...  42.5 us

profile of v4, /device:TPU:0, one launch (start us, length us, event | category | flops | bytes accessed | tf_op | source)
XLA Modules:
  0.0 531.9 jit_solution(14534540019897381202)
XLA Ops:
  0.7 0.8 fusion.31
  1.5 0.1 dynamic_slice.12
  1.5 0.7 broadcast_in_dim.15.refs_7_
  2.2 0.1 dynamic_slice.13
  2.3 0.7 broadcast_in_dim.16.refs_8_
  3.0 0.8 slice.116
  3.8 0.1 dynamic_slice.14
  3.8 0.6 broadcast_in_dim.17.refs_9_
  4.4 0.7 slice.174
  5.1 0.1 reshape.126
  5.2 0.7 fusion.26
  5.9 0.1 copy.56
  6.0 0.1 broadcast_in_dim.14
  6.1 0.1 reshape.127
  6.1 0.7 convert_element_type.16
  6.8 0.1 fusion.22
  6.9 0.6 fusion.21.refs_2_
  7.5 1.5 slice.145.refs_4_.refs_9_
  9.1 1.0 slice.146
  10.1 0.7 pad.10.refs_5_
  10.7 1.3 slice.144.refs_3_
  12.1 87.2 %gather_modulate.1 = (bf16[5376,768]{1,0:T(8,128)(2,1)}, bf16[768,3840]{1,0:T(8,128)(2,1)}, f32[4,8,4,336]{3,2,1,0:T(4,128)}, f32[24,128]{1,0:T(8,128)}, f32[24,...) custom-call(f32[2,168,768]{2,1,0:T(8,128)} %bitcast.164, ...), custom_call_target="tpu_custom_call" | custom-call | tf_op jit(solution)/shard_map/gather_modulate/pallas_call | solution.py:1457
  99.3 0.9 slice.119
  100.1 0.2 reshape.130
  100.4 0.1 pad_maximum_fusion
  100.5 2.3 bitcast_add_fusion
  102.8 0.2 reshape.129
  103.1 0.7 fusion.28
  103.8 0.6 slice.122.b_in
  104.4 0.6 slice.124.b_out
  105.0 74.4 %forward_gather.1 = (bf16[1024,768]{1,0:T(8,128)(2,1)}, bf16[1024,2304]{1,0:T(8,128)(2,1)}, bf16[4,12,256,256]{3,2,1,0:T(8,128)(2,1)}, bf16[1024,768]{1,0:T(8,12...) custom-call(f32[1024,768]{1,0:T(8,128)} %bitcast.160, ...), custom_call_target="tpu_custom_call" | custom-call | tf_op jit(solution)/shard_map/forward_gather/pallas_call | solution.py:1507
  179.4 0.6 slice.149.final
  180.1 0.6 slice.126.b_in
  180.7 0.6 slice.128.b_out
  181.3 0.7 copy.59.b_head
  182.0 42.5 %forward_head.1 = (bf16[1024,768]{1,0:T(8,128)(2,1)}, bf16[1024,2304]{1,0:T(8,128)(2,1)}, bf16[4,12,256,256]{3,2,1,0:T(8,128)(2,1)}, bf16[1024,768]{1,0:T(8,128)...) custom-call(f32[1024,768]{1,0:T(8,128)} %get-tuple-element.91.x.refs, ...), custom_call_target="tpu_custom_call" | custom-call | tf_op jit(solution)/shard_map/forward_head/pallas_call | solution.py:1282
  224.5 49.8 %backward_block.1 = (f32[1024,768]{1,0:T(8,128)}, bf16[1024,2304]{1,0:T(8,128)(2,1)}, bf16[1024,3072]{1,0:T(8,128)(2,1)}, bf16[1024,768]{1,0:T(8,128)(2,1)}, bf1...) custom-call(f32[4,6,768]{2,1,0:T(8,128)} %get-tuple-element.172.mod, ...), custom_call_target="tpu_custom_call" | custom-call | tf_op jit(solution)/shard_map/backward_block/pallas_call | solution.py:1389
  274.3 43.8 %weight_grads_out.1 = (bf16[5376,768]{1,0:T(8,128)(2,1)}, f32[24,3840]{1,0:T(8,128)}) custom-call(bf16[1024,2304]{1,0:T(8,128)(2,1)} %get-tuple-element.99.refs_0_, bf16[1024,768]{1,0:T(8,128)(2,1)} %get-tuple-element.100.refs_1_, bf16[1024,3072]{1,0:T(8,128)(2,1)} %get-tuple-element.101.refs_2_, bf16[1024,768]{1,0:T(8,128)(2,1)} %get-tuple-element.102.refs_3_, ...), custom_call_target="tpu_custom_call" | custom-call | tf_op jit(solution)/shard_map/weight_grads_out/pallas_call | solution.py:1601
  318.2 66.1 %backward_scatter.1 = (f32[1024,768]{1,0:T(8,128)}, bf16[1024,2304]{1,0:T(8,128)(2,1)}, bf16[1024,3072]{1,0:T(8,128)(2,1)}, bf16[1024,768]{1,0:T(8,128)(2,1)}, b...) custom-call(f32[4,6,768]{2,1,0:T(8,128)} %get-tuple-element.173.mod,, ...), custom_call_target="tpu_custom_call" | custom-call | tf_op jit(solution)/shard_map/backward_scatter/pallas_call | solution.py:1646
  384.3 0.9 pad_maximum_fusion.1
  385.2 0.2 reshape.132
  385.4 0.8 copy.60
  386.2 120.8 %finish_grads.1 = (f32[168,768]{1,0:T(8,128)}, f32[24,3840]{1,0:T(8,128)}, f32[336,768]{1,0:T(8,128)}, f32[24,256]{1,0:T(8,128)}, f32[24,768]{1,0:T(8,128)}, /*i...) custom-call(bf16[1024,2304]{1,0:T(8,128)(2,1)} %get-tuple-element.115.refs_0_, ...), custom_call_target="tpu_custom_call" | custom-call | tf_op jit(solution)/shard_map/finish_grads/pallas_call | solution.py:1724
  507.1 1.2 bitcast_convert_fusion
  508.3 0.1 slice_reduce_fusion
  508.4 0.1 reshape_squeeze.6
  508.5 0.1 reshape_squeeze.7
  508.6 0.6 copy-done.16
  509.3 0.6 copy.80
  509.9 0.9 reshape.138
  510.8 0.8 slice_dynamic-update-slice_fusion
  511.6 0.6 multiply_reduce_fusion
  512.3 0.7 slice_reduce_fusion.2
  512.9 0.6 multiply_reduce_fusion.1
  514.8 0.6 multiply_reduce_fusion.2
  516.8 1.7 multiply_subtract_fusion
  518.6 1.9 fusion.16
  520.5 2.9 fusion.17
  523.5 2.5 fusion.14
  526.0 0.6 copy-done.9
  526.6 2.4 fusion.4
  529.0 0.2 copy.61
  529.2 0.1 concatenate.24
  529.4 1.0 fusion.13
  (70 shorter events, 0.3 us)
Async XLA Ops:
  0.7 99.6 %copy-start.21 = (f32[16,384]{1,0:T(8,128)S(1)}, f32[16,384]{1,0:T(8,128)}, u32[]{:S(2)}) copy-start(f32[16,384]{1,0:T(8,128)} %constant.58.clone) | copy-start | bytes 73732
  7.5 92.9 %copy-start.20 = (bf16[4,256,16]{1,2,0:T(8,128)(2,1)S(1)}, bf16[4,256,16]{1,2,0:T(8,128)(2,1)}, u32[]{:S(2)}) copy-start(bf16[4,256,16]{1,2,0:T(8,128)(2,1)} %param.23) | copy-start | bytes 98308
  100.3 2.5 copy-start.19
  100.4 3.4 copy-start.14
  318.1 66.1 %copy-start.23 = (f32[4,6,768]{2,1,0:T(8,128)S(1)}, f32[4,6,768]{2,1,0:T(8,128)}, u32[]{:S(2)}) copy-start(f32[4,6,768]{2,1,0:T(8,128)} %get-tuple-element.124) | copy-start | bytes 221188
  318.2 66.1 %copy-start.26 = (f32[4,2,768]{2,1,0:T(2,128)S(1)}, f32[4,2,768]{2,1,0:T(2,128)}, u32[]{:S(2)}) copy-start(f32[4,2,768]{2,1,0:T(2,128)} %get-tuple-element.125) | copy-start | bytes 73732
  386.2 132.4 %copy-start.15 = (f32[768,32]{0,1:T(8,128)S(1)}, f32[768,32]{0,1:T(8,128)}, u32[]{:S(2)}) copy-start(f32[768,32]{0,1:T(8,128)} %param.39) | copy-start | bytes 294916
  507.1 13.4 %copy-start.2 = (f32[2,3840,24]{1,2,0:T(8,128)S(1)}, f32[2,3840,24]{1,2,0:T(8,128)}, u32[]{:S(2)}) copy-start(f32[2,3840,24]{1,2,0:T(8,128)} %param.36) | copy-start | bytes 2211844
  507.1 13.4 %copy-start.4 = (f32[24,3840]{1,0:T(8,128)S(1)}, f32[24,3840]{1,0:T(8,128)}, u32[]{:S(2)}) copy-start(f32[24,3840]{1,0:T(8,128)} %get-tuple-element.142.refs_27_) | copy-start | bytes 1105924
  507.1 13.4 %copy-start.11 = (f32[2,3840,24]{1,2,0:T(8,128)S(1)}, f32[2,3840,24]{1,2,0:T(8,128)}, u32[]{:S(2)}) copy-start(f32[2,3840,24]{1,2,0:T(8,128)} %param.38) | copy-start | bytes 2211844
  507.1 13.4 %copy-start.12 = (f32[2,3840,24]{1,2,0:T(8,128)S(1)}, f32[2,3840,24]{1,2,0:T(8,128)}, u32[]{:S(2)}) copy-start(f32[2,3840,24]{1,2,0:T(8,128)} %param.37) | copy-start | bytes 2211844
  508.6 0.6 copy-start.16
  518.6 4.9 copy-start.1
  518.6 4.9 copy-start.3
  518.6 4.9 copy-start.5
  518.6 4.9 copy-start.6
  518.6 4.9 copy-start.13
  523.5 2.5 copy-start
  523.5 2.5 copy-start.7
  523.5 2.5 copy-start.8
  523.5 3.0 copy-start.9
  526.5 2.7 copy-start.22
  526.5 2.7 copy-start.24
  526.5 2.7 copy-start.25
  526.5 2.8 copy-start.10
  526.6 2.8 copy-start.17
  526.6 2.8 copy-start.18

commit v5 on v4

--- a/solution.py
+++ b/solution.py
@@ -908,16 +908,19 @@
 
 
 def modulate_steps(devices, ins, outs, bufs, sems):
-    msg, wt1, wt2, wcls, wcond, bt1, bt2, bcond = ins
+    msg, emb, wcond, bt1, bt2, bcond = ins
     mods, pre, cond, hid_all, low_all, feat_all, lab_all, got = outs
-    hid, low, away, mid = bufs
+    hid, low, away, mid, wcls = bufs
     me = lax.axis_index(AXIS)
     z, place = me // PLANE, me % PLANE
-    images, cols = 4, wt1.shape[0]
+    images, cols = 4, emb.shape[0]
+    wt1, wt2 = emb.at[:, :FREQ], emb.at[:, FREQ : FREQ + MODEL_WIDTH]
     swaps = [Swap(0, sems, got), Swap(1, sems, hid), Swap(2, sems, low), Swap(3, sems, mods, away, mid)]
 
     def first():
         got[z, place] = msg[...]
+        wcls[...] = jnp.zeros_like(wcls)
+        wcls[:, : emb.shape[1] - FREQ - MODEL_WIDTH] = emb[:, FREQ + MODEL_WIDTH :]
         swaps[0].start()
 
     def second():
@@ -935,7 +938,7 @@
         hid[z, place] = jnp.concatenate([hidden, pad], 0).astype(jnp.bfloat16)
         swaps[1].start()
         classes = lax.broadcasted_iota(jnp.int32, (lab_all.shape[0], wcls.shape[1]), 1).astype(jnp.float32)
-        labels = jnp.concatenate([lab_all[...]] * (wcls.shape[1] // 128), 1)
+        labels = jnp.concatenate([lab_all[...] + PD] * (wcls.shape[1] // 128), 1)
         onehot = (labels == classes).astype(jnp.bfloat16)
         cond[...] = dot_nt(wcls[...].astype(jnp.bfloat16), onehot) + bt2[...]
 
@@ -969,7 +972,7 @@
     return [first, between[0], second, between[1], third, between[2], fourth, between[3], last]
 
 
-SETTLE_INS = ("d_mods", "wt2", "wcond", "pre", "cond", "hid_all", "low_all", "feat_all", "lab_all", "g_head", "g_hbias", "loss",
+SETTLE_INS = ("d_mods", "emb", "wcond", "pre", "cond", "hid_all", "low_all", "feat_all", "lab_all", "g_head", "g_hbias", "loss",
               "g_patch", "g_pbias", "bin0", "bin1", "bout0", "bout1", "done_in", "done_out")
 
 
@@ -1050,11 +1053,11 @@
         swaps[2].arrive()
         d_cond = jnp.sum(dc_got[...], 0)[:cols] * silu_slope(ins["cond"][...])
         parts = thirds(d_cond)
-        weight = ins["wt2"][...].astype(jnp.bfloat16)
+        weight = ins["emb"][:, FREQ : FREQ + MODEL_WIDTH].astype(jnp.bfloat16)
         share(sum(dot_tn(weight, part) for part in parts), dh_part)
         swaps[3].start()
         classes = lax.broadcasted_iota(jnp.int32, (lab_all.shape[0], g_cls.shape[1]), 1).astype(jnp.float32)
-        labels = jnp.concatenate([lab_all[...]] * (g_cls.shape[1] // 128), 1)
+        labels = jnp.concatenate([lab_all[...] + PD] * (g_cls.shape[1] // 128), 1)
         onehot = (labels == classes).astype(jnp.bfloat16)
         g_cls[...] = sum(jnp.dot(part, onehot, preferred_element_type=jnp.float32) for part in parts)
         hidden = ins["hid_all"][...].astype(jnp.bfloat16)
@@ -1176,20 +1179,23 @@
         span = slice(j * width, (j + 1) * width)
         qkv[:, span] = (dot_nt(h1[...], weights.w_in[span, :]) + b_in[:, span]).astype(jnp.bfloat16)
     hook()
-    for pair in range(HEADS // 2):
-        lanes = slice(128 * pair, 128 * (pair + 1))
-        q, k, v = (qkv[:, j * width + 128 * pair : j * width + 128 * (pair + 1)] for j in range(3))
+    def scores_of(pair):
+        q, k = (qkv[:, j * width + 128 * pair : j * width + 128 * (pair + 1)] for j in range(2))
         q = q * jnp.bfloat16(HEAD_DIM**-0.5)
         zero = jnp.zeros_like(q)
-        mixed = None
-        for half, mask in enumerate(head_masks(q.shape)):
-            scores = dot_nt(jnp.where(mask, q, zero), k)
-            expo = jnp.exp(scores - jnp.max(scores, -1, keepdims=True))
-            weight = (expo * pl.reciprocal(jnp.sum(expo, -1, keepdims=True))).astype(jnp.bfloat16)
-            probs[0, 2 * pair + half] = weight
-            term = dot_nn(weight, jnp.where(mask, v, zero))
-            mixed = term if mixed is None else mixed + term
-        o[:, lanes] = mixed.astype(jnp.bfloat16)
+        return dot_nt(jnp.concatenate([jnp.where(mask, q, zero) for mask in head_masks(q.shape)], 0), k)
+
+    ahead = scores_of(0)
+    for pair in range(HEADS // 2):
+        scores, ahead = ahead, scores_of(pair + 1) if pair + 1 < HEADS // 2 else None
+        v = qkv[:, 2 * width + 128 * pair : 2 * width + 128 * (pair + 1)]
+        expo = jnp.exp(scores - jnp.max(scores, -1, keepdims=True))
+        weight = (expo * pl.reciprocal(jnp.sum(expo, -1, keepdims=True))).astype(jnp.bfloat16)
+        probs[0, 2 * pair] = weight[:SEQ]
+        probs[0, 2 * pair + 1] = weight[SEQ:]
+        both = dot_nn(weight, v)
+        mixed = jnp.where(head_masks(v.shape)[0], both[:SEQ], both[SEQ:])
+        o[:, 128 * pair : 128 * (pair + 1)] = mixed.astype(jnp.bfloat16)
         hook()
     weights.need(1)
     branch = dot_nt(o[...], weights.w_out[:, :width]) + b_out[:, :width]
@@ -1199,14 +1205,18 @@
     hook()
     weights.need(2)
     weights.need(3)
-    total = None
+    def up_part(j):
+        rows = slice((3 + j) * width, (4 + j) * width)
+        return dot_nt(h2[...], weights.w_in[rows, :]) + b_in[:, rows]
+
+    total, ahead = None, up_part(0)
     for j in range(FF // width):
         span = slice(j * width, (j + 1) * width)
-        rows = slice((3 + j) * width, (4 + j) * width)
-        value = dot_nt(h2[...], weights.w_in[rows, :]) + b_in[:, rows]
+        value, ahead = ahead, up_part(j + 1) if j + 1 < FF // width else None
         u[:, span] = value.astype(jnp.bfloat16)
-        g[:, span] = gelu_value(value).astype(jnp.bfloat16)
-        term = dot_nt(g[:, span], weights.w_out[:, (1 + j) * width : (2 + j) * width])
+        active = gelu_value(value).astype(jnp.bfloat16)
+        g[:, span] = active
+        term = dot_nt(active, weights.w_out[:, (1 + j) * width : (2 + j) * width])
         total = term if total is None else total + term
         hook()
     ffn = total + b_out[:, width:]
@@ -1337,27 +1347,28 @@
     d_o = dot_nn(d_a[...], weights.w_out[:, :width]).astype(jnp.bfloat16)
     hook()
     root = HEAD_DIM**-0.5
+
+    def probs_back(pair):
+        d_mixed = d_o[:, 128 * pair : 128 * (pair + 1)]
+        zero = jnp.zeros_like(d_mixed)
+        both = jnp.concatenate([jnp.where(mask, d_mixed, zero) for mask in head_masks(d_mixed.shape)], 0)
+        return both, dot_nt(both, qkv[:, 2 * width + 128 * pair : 2 * width + 128 * (pair + 1)])
+
     for pair in range(HEADS // 2):
         lanes = [slice(j * width + 128 * pair, j * width + 128 * (pair + 1)) for j in range(3)]
-        q, k, v = (qkv[:, s] for s in lanes)
-        d_mixed = d_o[:, 128 * pair : 128 * (pair + 1)]
+        d_masked, d_probs = probs_back(pair)
+        q, k = qkv[:, lanes[0]], qkv[:, lanes[1]]
         zero = jnp.zeros_like(q)
-        sums = [None] * 3
-        for half, mask in enumerate(head_masks(q.shape)):
-            weight = probs[0, 2 * pair + half]
-            full = weight.astype(jnp.float32)
-            d_masked = jnp.where(mask, d_mixed, zero)
-            d_probs = dot_nt(d_masked, v)
-            d_scores = (full * (d_probs - jnp.sum(full * d_probs, -1, keepdims=True))).astype(jnp.bfloat16)
-            terms = (
-                dot_nn(d_scores, jnp.where(mask, k, zero)),
-                dot_tn(d_scores, jnp.where(mask, q, zero)),
-                dot_tn(weight, d_masked),
-            )
-            sums = [t if s is None else s + t for s, t in zip(sums, terms)]
-        d_qkv[:, lanes[0]] = (sums[0] * root).astype(jnp.bfloat16)
-        d_qkv[:, lanes[1]] = (sums[1] * root).astype(jnp.bfloat16)
-        d_qkv[:, lanes[2]] = sums[2].astype(jnp.bfloat16)
+        masks = head_masks(q.shape)
+        weight = probs[0, 2 * pair : 2 * pair + 2].reshape(2 * SEQ, SEQ)
+        full = weight.astype(jnp.float32)
+        d_scores = (full * (d_probs - jnp.sum(full * d_probs, -1, keepdims=True))).astype(jnp.bfloat16)
+        both = dot_nn(d_scores, k)
+        d_q = jnp.where(masks[0], both[:SEQ], both[SEQ:])
+        d_k = dot_tn(d_scores, jnp.concatenate([jnp.where(mask, q, zero) for mask in masks], 0))
+        d_qkv[:, lanes[0]] = (d_q * root).astype(jnp.bfloat16)
+        d_qkv[:, lanes[1]] = (d_k * root).astype(jnp.bfloat16)
+        d_qkv[:, lanes[2]] = dot_tn(weight, d_masked).astype(jnp.bfloat16)
         hook()
     weights.need(0)
     d_h1 = None
@@ -1429,9 +1440,9 @@
 
 
 def start_kernel(devices, *refs):
-    own, mod_ins, refs = refs[:2], refs[2:10], refs[10:]
+    own, mod_ins, refs = refs[:2], refs[2:8], refs[8:]
     full, mod_outs, refs = refs[:2], refs[2:10], refs[10:]
-    part, mod_bufs, mod_sems = refs[:10], refs[10:14], refs[14:]
+    part, mod_bufs, mod_sems = refs[:10], refs[10:15], refs[15:]
     place = Place()
     place.greet()
     job = Gather(place, [ref.at[0] for ref in own], part[:2], part[2:4], full, part[4:])
@@ -1446,8 +1457,8 @@
 
 def gather_modulate(pair, ins):
     devices = lax.axis_size(AXIS)
-    msg, wt1, wt2, wcls, wcond = ins[:5]
-    cols, images = wt1.shape[0], ins[5].shape[1]
+    msg, _, wcond, rows = ins[:4]
+    cols, images = rows.shape
     outs = [
         (LINE, PLANE, images // devices, wcond.shape[0]), (cols, images), (cols, images), (devices * cols, images),
         (devices * cols, images), (images, FREQ), (images, 128),
@@ -1459,7 +1470,7 @@
         out_shape=[full_shape(a) for a in pair]
         + [jax.ShapeDtypeStruct(shape, jnp.float32) for shape in outs]
         + [jax.ShapeDtypeStruct((LINE, PLANE) + msg.shape, jnp.bfloat16)],
-        in_specs=[vmem] * 10,
+        in_specs=[vmem] * 8,
         out_specs=[pl.BlockSpec(memory_space=pl.ANY)] * 2 + [vmem] * 8,
         scratch_shapes=gather_scratch(piece_shapes([a.shape[1:] for a in pair]))
         + [
@@ -1467,6 +1478,7 @@
             pltpu.VMEM((LINE, PLANE, padded, images), jnp.bfloat16),
             pltpu.VMEM((LINE, PLANE, images // devices, wcond.shape[0]), jnp.float32),
             pltpu.VMEM((LINE, PLANE, images // devices, wcond.shape[0]), jnp.float32),
+            pltpu.VMEM((cols, 1024), jnp.float32),
             pltpu.SemaphoreType.DMA((4, LINE + PLANE)),
             pltpu.SemaphoreType.DMA((4, LINE + PLANE)),
         ],
@@ -1791,9 +1803,6 @@
     digits = jnp.stack([labels // 32, labels % 32], 1).astype(jnp.float32)
     digits = jnp.broadcast_to(digits[:, :, None], (images, 2, 64)).reshape(images, 128)
     note = jnp.concatenate([features[:, :128], features[:, 128:], own_patch_w, digits], 0).astype(jnp.bfloat16)
-    w_t1 = embed_t[:, :FREQ]
-    w_t2 = embed_t[:, FREQ : FREQ + MODEL_WIDTH]
-    w_class = jnp.pad(embed_t[:, FREQ + MODEL_WIDTH + PD :], ((0, 0), (0, 1024 - NCLS)))
     images_all = devices * images
 
     def own_bias(vector, count):
@@ -1803,7 +1812,7 @@
     own_cond_bias = lax.dynamic_slice(cond_bias, (me * cond_cols,), (cond_cols,))[None]
     first_in, first_out, mods, pre, cond, hid_all, low_all, feat_all, lab_all, notes = gather_modulate(
         [in_t, out_t],
-        [note, w_t1, w_t2, w_class, cond_t, own_bias(time_one, cols), own_bias(time_two, cols), own_cond_bias],
+        [note, embed_t, cond_t, own_bias(time_one, cols), own_bias(time_two, cols), own_cond_bias],
     )
     chunks = mods.reshape(devices, images, cond_cols).transpose(1, 0, 2).reshape(images, 6 * LAYERS + 2, MODEL_WIDTH)
     w_patch = notes[:, :, 8:11].reshape(MODEL_WIDTH, PD)
@@ -1839,7 +1848,7 @@
         [d_qkv, h1, d_u, h2, d_a, o, d_f, g],
         [in_shape, out_shape],
         {
-            "d_mods": d_mods, "wt2": w_t2, "wcond": cond_t, "pre": pre, "cond": cond, "hid_all": hid_all, "low_all": low_all,
+            "d_mods": d_mods, "emb": embed_t, "wcond": cond_t, "pre": pre, "cond": cond, "hid_all": hid_all, "low_all": low_all,
             "feat_all": feat_all, "lab_all": lab_all, "g_head": head_grad, "g_hbias": head_bias_grad, "loss": loss_part,
             "g_patch": patch_grad, "g_pbias": patch_bias_grad, "bin0": in_bias_grads[0], "bin1": in_bias_grads[1],
             "bout0": out_bias_grads[0], "bout1": out_bias_grads[1], "done_in": in_shard1, "done_out": out_shard1,
@@ -1865,7 +1874,7 @@
     )
     factor = jnp.minimum(1.0, clip_limit / grad_norm)
     own_patch = lax.dynamic_slice(patch_total, (0, me * cols), (PD, cols)).T
-    embed_grad = jnp.concatenate([g_t1, g_t2, own_patch, g_cls[:, :NCLS]], 1)
+    embed_grad = jnp.concatenate([g_t1, g_t2, own_patch, g_cls[:, PD : PD + NCLS]], 1)
     embed_up = [a.T for a in adam_step(embed_t, embed_m.T, embed_v.T, embed_grad * factor)]
     cond_up = [a.T for a in adam_step(cond_t, cond_m.T, cond_v.T, g_cond * factor)]
     turn = (0, 2, 1)

time: 541 us -> 526 us (0.972)
  Pallas kernels: 485 us -> 474 us
where the time goes in v5:
time: 526 us; the launch traced here: 517 us
  Pallas kernels  474 us (90%)
  other arithmetic  19.1 us (4%)
  local copies, waits for them, and re-layouts  15.9 us (3%)
  between operations  5.46 us (1%)
    pallas_call x1, Pallas kernels, finish_grads(): pl.pallas_call(functools.partial(finish_kernel, devices), out_shape=[jax....  121 us
    pallas_call x1, Pallas kernels, gather_modulate(): pl.pallas_call(functools.partial(start_kernel, devices), out_shape=[full_...  87.3 us
    pallas_call x1, Pallas kernels, forward_gather(): pl.pallas_call(functools.partial(forward_gather_kernel, GATHER_SLOTS), gr...  73.6 us
    pallas_call x1, Pallas kernels, backward_scatter(): pl.pallas_call(functools.partial(backward_scatter_kernel, SCATTER_SLOTS),...  65 us
    pallas_call x1, Pallas kernels, backward_block(): pl.pallas_call(backward_kernel, grid=(images,), out_shape=[jax.ShapeDtype...  46.2 us
    pallas_call x1, Pallas kernels, weight_grads_out(): pl.pallas_call(grads_out_kernel, out_shape=[jax.ShapeDtypeStruct((IW, MOD...  43.6 us
    pallas_call x1, Pallas kernels, forward_head(): pl.pallas_call(functools.partial(head_kernel, scale_out), grid=(images,),...  37.5 us

profile of v5, /device:TPU:0, one launch (start us, length us, event | category | flops | bytes accessed | tf_op | source)
XLA Modules:
  0.0 516.7 jit_solution(3273414771300231233)
XLA Ops:
  0.7 0.0 copy-start.21
  0.7 0.0 copy-start.20
  0.7 0.8 fusion.31
  1.5 0.1 dynamic_slice.12
  1.5 0.7 broadcast_in_dim.15.refs_5_
  2.2 0.1 dynamic_slice.13
  2.3 0.7 broadcast_in_dim.16.refs_6_
  3.0 0.8 slice.104
  3.8 0.1 dynamic_slice.14
  3.8 0.6 broadcast_in_dim.17.refs_7_
  4.4 0.7 slice.159
  5.1 0.1 reshape.126
  5.2 0.7 fusion.26
  5.9 0.1 copy.56
  6.0 0.1 broadcast_in_dim.14
  6.1 0.1 reshape.127
  6.2 0.7 convert_element_type.14
  6.8 0.1 fusion.22
  6.9 0.6 fusion.21.refs_2_
  7.6 87.3 %gather_modulate.1 = (bf16[5376,768]{1,0:T(8,128)(2,1)}, bf16[768,3840]{1,0:T(8,128)(2,1)}, f32[4,8,4,336]{3,2,1,0:T(4,128)}, f32[24,128]{1,0:T(8,128)}, f32[24,...) custom-call(f32[2,168,768]{2,1,0:T(8,128)} %bitcast.163, ...), custom_call_target="tpu_custom_call" | custom-call | tf_op jit(solution)/shard_map/gather_modulate/pallas_call | solution.py:1468
  94.8 0.9 slice.107
  95.7 0.2 reshape.130
  95.9 0.0 copy-start.14
  96.0 0.1 pad_maximum_fusion
  96.0 2.3 bitcast_add_fusion
  98.4 0.2 reshape.129
  98.6 0.7 fusion.28
  99.3 0.6 slice.110.b_in
  99.9 0.6 slice.112.b_out
  100.5 73.6 %forward_gather.1 = (bf16[1024,768]{1,0:T(8,128)(2,1)}, bf16[1024,2304]{1,0:T(8,128)(2,1)}, bf16[4,12,256,256]{3,2,1,0:T(8,128)(2,1)}, bf16[1024,768]{1,0:T(8,12...) custom-call(f32[1024,768]{1,0:T(8,128)} %bitcast.159, ...), custom_call_target="tpu_custom_call" | custom-call | tf_op jit(solution)/shard_map/forward_gather/pallas_call | solution.py:1519
  174.2 0.6 slice.134.final
  174.8 0.6 slice.114.b_in
  175.4 0.6 slice.116.b_out
  176.0 0.7 copy.59.b_head
  176.7 37.5 %forward_head.1 = (bf16[1024,768]{1,0:T(8,128)(2,1)}, bf16[1024,2304]{1,0:T(8,128)(2,1)}, bf16[4,12,256,256]{3,2,1,0:T(8,128)(2,1)}, bf16[1024,768]{1,0:T(8,128)...) custom-call(f32[1024,768]{1,0:T(8,128)} %get-tuple-element.91.x.refs, ...), custom_call_target="tpu_custom_call" | custom-call | tf_op jit(solution)/shard_map/forward_head/pallas_call | solution.py:1292
  214.2 46.2 %backward_block.1 = (f32[1024,768]{1,0:T(8,128)}, bf16[1024,2304]{1,0:T(8,128)(2,1)}, bf16[1024,3072]{1,0:T(8,128)(2,1)}, bf16[1024,768]{1,0:T(8,128)(2,1)}, bf1...) custom-call(f32[4,6,768]{2,1,0:T(8,128)} %get-tuple-element.172.mod, ...), custom_call_target="tpu_custom_call" | custom-call | tf_op jit(solution)/shard_map/backward_block/pallas_call | solution.py:1400
  260.4 43.6 %weight_grads_out.1 = (bf16[5376,768]{1,0:T(8,128)(2,1)}, f32[24,3840]{1,0:T(8,128)}) custom-call(bf16[1024,2304]{1,0:T(8,128)(2,1)} %get-tuple-element.99.refs_0_, bf16[1024,768]{1,0:T(8,128)(2,1)} %get-tuple-element.100.refs_1_, bf16[1024,3072]{1,0:T(8,128)(2,1)} %get-tuple-element.101.refs_2_, bf16[1024,768]{1,0:T(8,128)(2,1)} %get-tuple-element.102.refs_3_, ...), custom_call_target="tpu_custom_call" | custom-call | tf_op jit(solution)/shard_map/weight_grads_out/pallas_call | solution.py:1613
  304.0 65.0 %backward_scatter.1 = (f32[1024,768]{1,0:T(8,128)}, bf16[1024,2304]{1,0:T(8,128)(2,1)}, bf16[1024,3072]{1,0:T(8,128)(2,1)}, bf16[1024,768]{1,0:T(8,128)(2,1)}, b...) custom-call(f32[4,6,768]{2,1,0:T(8,128)} %get-tuple-element.173.mod,, ...), custom_call_target="tpu_custom_call" | custom-call | tf_op jit(solution)/shard_map/backward_scatter/pallas_call | solution.py:1658
  369.0 0.9 pad_maximum_fusion.1
  370.0 0.2 reshape.132
  370.2 0.8 copy.60
  371.0 120.8 %finish_grads.1 = (f32[168,768]{1,0:T(8,128)}, f32[24,3840]{1,0:T(8,128)}, f32[336,768]{1,0:T(8,128)}, f32[24,256]{1,0:T(8,128)}, f32[24,768]{1,0:T(8,128)}, /*i...) custom-call(bf16[1024,2304]{1,0:T(8,128)(2,1)} %get-tuple-element.115.refs_0_, ...), custom_call_target="tpu_custom_call" | custom-call | tf_op jit(solution)/shard_map/finish_grads/pallas_call | solution.py:1736
  491.9 1.2 bitcast_convert_fusion
  493.0 0.1 slice_reduce_fusion
  493.1 0.1 reshape_squeeze.6
  493.2 0.1 reshape_squeeze.7
  493.4 0.6 copy-done.16
  494.0 0.6 copy.80
  494.6 0.9 reshape.138
  495.6 0.8 slice_dynamic-update-slice_fusion
  496.4 0.6 multiply_reduce_fusion
  497.0 0.7 slice_reduce_fusion.2
  497.7 0.6 multiply_reduce_fusion.1
  499.6 0.6 multiply_reduce_fusion.2
  501.6 1.7 multiply_subtract_fusion
  503.4 1.9 fusion.16
  505.3 2.9 fusion.17
  508.3 2.5 fusion.14
  510.7 0.6 copy-done.10
  511.3 2.4 fusion.4
  513.8 0.2 copy.61
  514.0 0.1 slice.130
  514.1 0.1 concatenate.24
  514.2 1.0 fusion.13
  (67 shorter events, 0.3 us)
Async XLA Ops:
  0.7 95.2 %copy-start.21 = (f32[16,384]{1,0:T(8,128)S(1)}, f32[16,384]{1,0:T(8,128)}, u32[]{:S(2)}) copy-start(f32[16,384]{1,0:T(8,128)} %constant.58.clone) | copy-start | bytes 73732
  0.7 95.4 %copy-start.20 = (bf16[4,256,16]{1,2,0:T(8,128)(2,1)S(1)}, bf16[4,256,16]{1,2,0:T(8,128)(2,1)}, u32[]{:S(2)}) copy-start(bf16[4,256,16]{1,2,0:T(8,128)(2,1)} %param.23) | copy-start | bytes 98308
  95.9 2.5 copy-start.19
  95.9 3.4 copy-start.14
  304.0 65.0 %copy-start.23 = (f32[4,6,768]{2,1,0:T(8,128)S(1)}, f32[4,6,768]{2,1,0:T(8,128)}, u32[]{:S(2)}) copy-start(f32[4,6,768]{2,1,0:T(8,128)} %get-tuple-element.124) | copy-start | bytes 221188
  304.0 65.0 %copy-start.26 = (f32[4,2,768]{2,1,0:T(2,128)S(1)}, f32[4,2,768]{2,1,0:T(2,128)}, u32[]{:S(2)}) copy-start(f32[4,2,768]{2,1,0:T(2,128)} %get-tuple-element.125) | copy-start | bytes 73732
  371.0 132.4 %copy-start.15 = (f32[768,32]{0,1:T(8,128)S(1)}, f32[768,32]{0,1:T(8,128)}, u32[]{:S(2)}) copy-start(f32[768,32]{0,1:T(8,128)} %param.39) | copy-start | bytes 294916
  491.8 13.4 %copy-start.2 = (f32[2,3840,24]{1,2,0:T(8,128)S(1)}, f32[2,3840,24]{1,2,0:T(8,128)}, u32[]{:S(2)}) copy-start(f32[2,3840,24]{1,2,0:T(8,128)} %param.36) | copy-start | bytes 2211844
  491.8 13.4 %copy-start.5 = (f32[24,3840]{1,0:T(8,128)S(1)}, f32[24,3840]{1,0:T(8,128)}, u32[]{:S(2)}) copy-start(f32[24,3840]{1,0:T(8,128)} %get-tuple-element.142.refs_27_) | copy-start | bytes 1105924
  491.8 13.4 %copy-start.11 = (f32[2,3840,24]{1,2,0:T(8,128)S(1)}, f32[2,3840,24]{1,2,0:T(8,128)}, u32[]{:S(2)}) copy-start(f32[2,3840,24]{1,2,0:T(8,128)} %param.38) | copy-start | bytes 2211844
  491.8 13.4 %copy-start.12 = (f32[2,3840,24]{1,2,0:T(8,128)S(1)}, f32[2,3840,24]{1,2,0:T(8,128)}, u32[]{:S(2)}) copy-start(f32[2,3840,24]{1,2,0:T(8,128)} %param.37) | copy-start | bytes 2211844
  493.3 0.6 copy-start.16
  503.3 4.9 copy-start.1
  503.3 4.9 copy-start.3
  503.3 4.9 copy-start.6
  503.3 4.9 copy-start.7
  503.3 4.9 copy-start.13
  508.2 2.5 copy-start
  508.2 2.5 copy-start.8
  508.2 2.5 copy-start.9
  508.2 3.0 copy-start.10
  511.3 2.7 copy-start.22
  511.3 2.8 copy-start.24
  511.3 2.8 copy-start.25
  511.3 2.9 copy-start.4
  511.3 2.9 copy-start.17
  511.3 2.9 copy-start.18

commit v6 on v5

--- a/solution.py
+++ b/solution.py
@@ -1167,9 +1167,9 @@
             self.copies[i].wait()
 
 
-def forward_image(x_ref, mod, weights, b_in, b_out, outs, hook=lambda: None):
+def forward_image(x_ref, mod, base, weights, b_in, b_out, outs, hook=lambda: None):
     h1, qkv, probs, o, a, x1, h2, u, g, f = outs
-    shift1, scale1, gate1, shift2, scale2, gate2 = (mod[0, i : i + 1, :] for i in range(6))
+    shift1, scale1, gate1, shift2, scale2, gate2 = (mod[0, base + i : base + i + 1, :] for i in range(6))
     width = MODEL_WIDTH
     hook()
     x = x_ref[...]
@@ -1224,13 +1224,13 @@
     return x1[...] + gate2 * ffn
 
 
-def head_kernel(scale_out, x, mod, w_in, w_out, b_in, b_out, final, head_t, b_head, targets_t, *refs):
+def head_kernel(scale_out, x, mod, w_in, w_out, b_in, b_out, head_t, b_head, targets_t, *refs):
     outs, (dx, d_final, g_head, g_bias, loss), (vm_in, vm_out, sems) = refs[:10], refs[10:15], refs[15:]
     weights = Weights((w_in, w_out), (vm_in, vm_out), sems)
     weights.start((0, 1, 2, 3))
-    last = forward_image(x, mod, weights, b_in, b_out, outs)
+    last = forward_image(x, mod, 6 * (LAYERS - 1), weights, b_in.at[0], b_out.at[0], outs)
     normed, scale = norm_parts(last)
-    shift_row, scale_row = final[0, 0:1, :], final[0, 1:2, :]
+    shift_row, scale_row = mod[0, 6 * LAYERS : 6 * LAYERS + 1, :], mod[0, 6 * LAYERS + 1 :, :]
     shaped = (normed * (1 + scale_row) + shift_row).astype(jnp.bfloat16)
     low = head_t[...].astype(jnp.bfloat16)
     error = dot_nt(low, shaped) + b_head[...] - targets_t[0]
@@ -1279,10 +1279,14 @@
     return [jax.ShapeDtypeStruct(s, t) for s, t in shapes], specs
 
 
-def forward_specs():
+def layer_block(array, layer):
+    return pl.BlockSpec((1,) + array.shape[1:], lambda i: (layer, 0, 0))
+
+
+def forward_specs(ins, layer):
     any_block = pl.BlockSpec(memory_space=pl.ANY)
-    return [token_block(MODEL_WIDTH), image_block(6, MODEL_WIDTH), any_block, any_block, whole_block(1, IW),
-            whole_block(1, 2 * MODEL_WIDTH)]
+    return [token_block(MODEL_WIDTH), image_block(*ins[1].shape[1:]), any_block, any_block, layer_block(ins[4], layer),
+            layer_block(ins[5], layer)]
 
 
 def forward_head(ins, scale_out):
@@ -1293,8 +1297,8 @@
         functools.partial(head_kernel, scale_out),
         grid=(images,),
         out_shape=shapes + [jax.ShapeDtypeStruct(s, jnp.float32) for s in extra],
-        in_specs=forward_specs()
-        + [image_block(2, MODEL_WIDTH), whole_block(PO, MODEL_WIDTH), whole_block(PO, 1), image_block(PO, SEQ)],
+        in_specs=forward_specs(ins, LAYERS - 1)
+        + [whole_block(PO, MODEL_WIDTH), whole_block(PO, 1), image_block(PO, SEQ)],
         out_specs=specs
         + [token_block(MODEL_WIDTH), image_block(2, MODEL_WIDTH), whole_block(PO, MODEL_WIDTH), whole_block(PO, 128),
            whole_block(8, 128)],
@@ -1304,11 +1308,11 @@
     )(*ins)
 
 
-def backward_image(refs, mod, weights, outs, hook=lambda: None):
+def backward_image(refs, mod, base, weights, outs, hook=lambda: None):
     up_ref, x_ref, x1_ref, probs, qkv, a, f, u = refs
     dx, d_qkv, d_u, d_f, d_a, d_mod, g_bin, g_bout = outs
     width = MODEL_WIDTH
-    shift1, scale1, gate1, shift2, scale2, gate2 = (mod[0, i : i + 1, :] for i in range(6))
+    shift1, scale1, gate1, shift2, scale2, gate2 = (mod[0, base + i : base + i + 1, :] for i in range(6))
 
     @pl.when(pl.program_id(0) == 0)
     def _():
@@ -1388,7 +1392,7 @@
     ins, outs, (vm_in, vm_out, sems) = refs[:8], refs[8:16], refs[16:]
     weights = Weights((w_in, w_out), (vm_in, vm_out), sems)
     weights.start((3, 2, 1, 0))
-    backward_image(ins, mod, weights, outs)
+    backward_image(ins, mod, 6 * (LAYERS - 1), weights, outs)
 
 
 def backward_block(mods, w_in, w_out, refs):
@@ -1401,7 +1405,7 @@
         backward_kernel,
         grid=(images,),
         out_shape=[jax.ShapeDtypeStruct(s, t) for s, t in shapes],
-        in_specs=[image_block(6, width), any_block, any_block, token_block(width), token_block(width), token_block(width),
+        in_specs=[image_block(*mods.shape[1:]), any_block, any_block, token_block(width), token_block(width), token_block(width),
                   image_block(HEADS, SEQ, SEQ), token_block(3 * width), token_block(width), token_block(width),
                   token_block(FF)],
         out_specs=[token_block(s[1]) for s, _ in shapes[:5]]
@@ -1490,44 +1494,55 @@
 FORWARD_POINTS = 13
 
 
-def forward_gather_kernel(slots, x, mod, w_in, w_out, b_in, b_out, own_in, own_out, *refs):
-    outs, x_out, full, refs = refs[:10], refs[10], refs[11:13], refs[13:]
-    vm_in, vm_out, sems, part = refs[0], refs[1], refs[2], refs[3:]
+def forward_gather_kernel(slots, lat_t, mod, w_in, w_out, b_in, b_out, w_patch, b_patch, table, own_in, own_out, *refs):
+    outs, x_out, full, x, refs = refs[:10], refs[10], refs[11:13], refs[13], refs[14:]
+    pos, vm_in, vm_out, sems, part = refs[0], refs[1], refs[2], refs[3], refs[4:]
     place = Place()
     job = Gather(place, (own_in.at[0], own_out.at[0]), part[:2], part[2:4], full, part[4:])
     hooks = Hooks([place.greet] + gather_steps(job), slots, FORWARD_POINTS)
     weights = Weights((w_in, w_out), (vm_in, vm_out), sems)
     weights.start((0, 1, 2, 3))
-    x_out[...] = forward_image(x, mod, weights, b_in, b_out, outs, hooks)
+
+    @pl.when(pl.program_id(0) == 0)
+    def _():
+        half = table.shape[1]
+        for row in range(GRID):
+            at = slice(GRID * row, GRID * (row + 1))
+            pos[at, :half] = jnp.broadcast_to(table[row : row + 1, :], (GRID, half))
+            pos[at, half:] = table[...]
+
+    latents = lat_t[0].astype(jnp.float32).T.astype(jnp.bfloat16)
+    x[...] = dot_nt(latents, w_patch[...]) + b_patch[...] + pos[...]
+    x_out[...] = forward_image(x, mod, 0, weights, b_in.at[0], b_out.at[0], outs, hooks)
 
 
 GATHER_SLOTS = (0, 0, 13, 15, 26, 28, 39, 41, 50) + (34, 43, 48, 51, 51, 51, 51, 51, 51)
-
-
-def layer_block(array, layer):
-    return pl.BlockSpec((1,) + array.shape[1:], lambda i: (layer, 0, 0))
 
 
 def full_shape(array):
     return jax.ShapeDtypeStruct((lax.axis_size(AXIS) * array.shape[1], array.shape[2]), jnp.bfloat16)
 
 
-def forward_gather(ins, pair, layer):
+def forward_gather(ins, patch, pair, layer):
     images = ins[1].shape[0]
     shapes, specs = kept_shapes(images)
+    tokens = jax.ShapeDtypeStruct((images * SEQ, MODEL_WIDTH), jnp.float32)
     any_block = pl.BlockSpec(memory_space=pl.ANY)
     return pl.pallas_call(
         functools.partial(forward_gather_kernel, GATHER_SLOTS),
         grid=(images,),
-        out_shape=shapes
-        + [jax.ShapeDtypeStruct((images * SEQ, MODEL_WIDTH), jnp.float32)]
-        + [full_shape(a) for a in pair],
-        in_specs=forward_specs() + [layer_block(a, layer) for a in pair],
-        out_specs=specs + [token_block(MODEL_WIDTH)] + [any_block] * 2,
-        scratch_shapes=WEIGHT_SCRATCH + gather_scratch(piece_shapes([a.shape[1:] for a in pair])),
+        out_shape=shapes + [tokens] + [full_shape(a) for a in pair] + [tokens],
+        in_specs=[image_block(PD, SEQ)]
+        + forward_specs(ins, 0)[1:]
+        + [whole_block(*a.shape) for a in patch]
+        + [layer_block(a, layer) for a in pair],
+        out_specs=specs + [token_block(MODEL_WIDTH)] + [any_block] * 2 + [token_block(MODEL_WIDTH)],
+        scratch_shapes=[pltpu.VMEM((SEQ, MODEL_WIDTH), jnp.float32)]
+        + WEIGHT_SCRATCH
+        + gather_scratch(piece_shapes([a.shape[1:] for a in pair])),
         compiler_params=pltpu.CompilerParams(collective_id=1, has_side_effects=True, vmem_limit_bytes=58 << 20),
         name="forward_gather",
-    )(*ins, *pair)
+    )(*ins, *patch, *pair)
 
 
 GRAD_CUTS = [3 * MODEL_WIDTH // MODEL_WIDTH, FF // MODEL_WIDTH]
@@ -1632,7 +1647,7 @@
     hooks = Hooks([place.greet, job.open_all] + job.steps(), slots, BACKWARD_POINTS)
     weights = Weights((w_in, w_out), (vm_in, vm_out), sems)
     weights.start((3, 2, 1, 0))
-    backward_image(ins, mod, weights, outs, hooks)
+    backward_image(ins, mod, 0, weights, outs, hooks)
     d_patch = outs[0][...].astype(jnp.bfloat16)
 
     @pl.when(pl.program_id(0) == 0)
@@ -1659,7 +1674,7 @@
         functools.partial(backward_scatter_kernel, SCATTER_SLOTS),
         grid=(images,),
         out_shape=[jax.ShapeDtypeStruct(s, t) for s, t in shapes],
-        in_specs=[image_block(6, width), any_block, any_block, any_block, image_block(PD, SEQ), token_block(width),
+        in_specs=[image_block(*mods.shape[1:]), any_block, any_block, any_block, image_block(PD, SEQ), token_block(width),
                   token_block(width), token_block(width), image_block(HEADS, SEQ, SEQ), token_block(3 * width),
                   token_block(width), token_block(width), token_block(FF)],
         out_specs=[token_block(s[1]) for s, _ in shapes[:5]]
@@ -1773,18 +1788,6 @@
     return np.concatenate([np.sin(angles), np.cos(angles)], 1).astype(np.float32)
 
 
-def position_sum():
-    table = jnp.asarray(code_table())
-    half = MODEL_WIDTH // 2
-    rows_pos = jnp.broadcast_to(table[:, None, :], (GRID, GRID, half))
-    cols_pos = jnp.broadcast_to(table[None, :, :], (GRID, GRID, half))
-    return jnp.concatenate([rows_pos, cols_pos], -1).reshape(SEQ, MODEL_WIDTH)
-
-
-def rows_t(left, right):
-    return jnp.einsum("bsd,ed->bse", left, right, preferred_element_type=jnp.float32)
-
-
 def body(
     latents, targets, timesteps, labels, embed_w, embed_m, embed_v, cond_w, cond_m, cond_v, layer_input_weights, in_m,
     in_v, layer_output_weights, out_m, out_v, head_w, head_m, head_v, biases, bias_m, bias_v,
@@ -1816,29 +1819,30 @@
     )
     chunks = mods.reshape(devices, images, cond_cols).transpose(1, 0, 2).reshape(images, 6 * LAYERS + 2, MODEL_WIDTH)
     w_patch = notes[:, :, 8:11].reshape(MODEL_WIDTH, PD)
-    x = (rows_t(latents, w_patch) + patch_bias + position_sum()).reshape(images * SEQ, MODEL_WIDTH)
-    block_mods = [chunks[:, 6 * i : 6 * (i + 1)] for i in range(LAYERS)]
     head_t = head_w.T
     tokens_all = devices * images * SEQ * PO
     lat_t = latents.transpose(0, 2, 1)
-    bias_rows = [(block_input_bias[i][None], block_output_bias[i][None]) for i in range(LAYERS)]
-    *kept0, x_mid, last_in, last_out = forward_gather(
-        [x, block_mods[0], first_in, first_out, *bias_rows[0]], [in_t, out_t], 1
+    bias_rows = [block_input_bias[:, None], block_output_bias[:, None]]
+    *kept0, x_mid, last_in, last_out, x = forward_gather(
+        [lat_t, chunks, first_in, first_out, *bias_rows],
+        [w_patch, patch_bias[None], jnp.asarray(code_table())],
+        [in_t, out_t],
+        1,
     )
     *kept1, upstream, d_final, head_grad, head_bias_grad, loss_part = forward_head(
-        [x_mid, block_mods[1], last_in, last_out, *bias_rows[1], chunks[:, 6 * LAYERS :], head_t, head_bias[:, None],
+        [x_mid, chunks, last_in, last_out, *bias_rows, head_t, head_bias[:, None],
          targets.transpose(0, 2, 1)],
         2.0 / tokens_all,
     )
     h1, qkv, probs, o, a, x1, h2, u, g, f = kept1
     upstream, d_qkv, d_u, d_f, d_a, mod_grad1, in_bias1, out_bias1 = backward_block(
-        block_mods[1], last_in, last_out, [upstream, x_mid, x1, probs, qkv, a, f, u]
+        chunks, last_in, last_out, [upstream, x_mid, x1, probs, qkv, a, f, u]
     )
     in_shape, out_shape = in_t.shape[1:], out_t.shape[1:]
     grad_in, out_shard1 = weight_grads_out([d_qkv, h1, d_u, h2, d_a, o, d_f, g], out_shape)
     h1, qkv, probs, o, a, x1, h2, u, g, f = kept0
     (upstream, d_qkv, d_u, d_f, d_a, mod_grad0, in_bias0, out_bias0, patch_grad, patch_bias_grad, in_shard1) = backward_scatter(
-        block_mods[0], first_in, first_out, [upstream, x, x1, probs, qkv, a, f, u], grad_in, lat_t, in_shape
+        chunks, first_in, first_out, [upstream, x, x1, probs, qkv, a, f, u], grad_in, lat_t, in_shape
     )
     mod_grads, in_bias_grads, out_bias_grads = [mod_grad0, mod_grad1], [in_bias0, in_bias1], [out_bias0, out_bias1]
     d_modulation = jnp.concatenate(mod_grads + [d_final], 1)

time: 526 us -> 524 us (level)
  no operation moved by 1% of the time
where the time goes in v6:
time: 524 us; the launch traced here: 516 us
  Pallas kernels  475 us (91%)
  other arithmetic  19 us (4%)
  local copies, waits for them, and re-layouts  16.3 us (3%)
    pallas_call x1, Pallas kernels, finish_grads(): pl.pallas_call(functools.partial(finish_kernel, devices), out_shape=[jax....  121 us
    pallas_call x1, Pallas kernels, gather_modulate(): pl.pallas_call(functools.partial(start_kernel, devices), out_shape=[full_...  87.3 us
    pallas_call x1, Pallas kernels, forward_gather(): pl.pallas_call(functools.partial(forward_gather_kernel, GATHER_SLOTS), gr...  74.1 us
    pallas_call x1, Pallas kernels, backward_scatter(): pl.pallas_call(functools.partial(backward_scatter_kernel, SCATTER_SLOTS),...  65.6 us
    pallas_call x1, Pallas kernels, backward_block(): pl.pallas_call(backward_kernel, grid=(images,), out_shape=[jax.ShapeDtype...  46.3 us
    pallas_call x1, Pallas kernels, weight_grads_out(): pl.pallas_call(grads_out_kernel, out_shape=[jax.ShapeDtypeStruct((IW, MOD...  43.5 us
    pallas_call x1, Pallas kernels, forward_head(): pl.pallas_call(functools.partial(head_kernel, scale_out), grid=(images,),...  37.5 us

profile of v6, /device:TPU:0, one launch (start us, length us, event | category | flops | bytes accessed | tf_op | source)
XLA Modules:
  0.0 515.7 jit_solution(1965738806936573149)
XLA Ops:
  0.7 0.0 copy-start.14
  0.7 0.8 fusion.27
  1.5 0.1 dynamic_slice.12
  1.6 0.7 broadcast_in_dim.13.refs_5_
  2.2 0.1 dynamic_slice.13
  2.3 0.7 broadcast_in_dim.14.refs_6_
  3.0 0.9 fusion.28
  3.9 0.1 dynamic_slice.14
  4.0 0.6 broadcast_in_dim.15.refs_7_
  4.5 0.7 slice.114
  5.2 0.1 reshape.113
  5.3 0.7 fusion.25
  6.0 0.1 copy.54
  6.1 0.1 broadcast_in_dim.12
  6.2 0.1 reshape.114
  6.3 0.7 convert_element_type.14
  6.9 0.1 fusion.21
  7.1 0.6 fusion.20.refs_2_
  7.7 87.3 %gather_modulate.1 = (bf16[5376,768]{1,0:T(8,128)(2,1)}, bf16[768,3840]{1,0:T(8,128)(2,1)}, f32[4,8,4,336]{3,2,1,0:T(4,128)}, f32[24,128]{1,0:T(8,128)}, f32[24,...) custom-call(f32[2,168,768]{2,1,0:T(8,128)} %bitcast.152, ...), custom_call_target="tpu_custom_call" | custom-call | tf_op jit(solution)/shard_map/gather_modulate/pallas_call | solution.py:1472
  94.9 0.9 copy.74
  95.9 0.9 reshape.116.mod
  96.8 0.8 slice.74
  97.6 0.9 reshape.117.w_patch
  98.5 0.7 broadcast_in_dim_reshape.6.b_in
  99.1 0.6 broadcast_in_dim.16.b_patch
  99.7 0.6 slice.73
  100.3 74.1 %forward_gather.1 = (bf16[1024,768]{1,0:T(8,128)(2,1)}, bf16[1024,2304]{1,0:T(8,128)(2,1)}, bf16[4,12,256,256]{3,2,1,0:T(8,128)(2,1)}, bf16[1024,768]{1,0:T(8,12...) custom-call(bf16[4,16,256]{2,1,0:T(8,128)(2,1)} %bitcast.177, ...), custom_call_target="tpu_custom_call" | custom-call | tf_op jit(solution)/shard_map/forward_gather/pallas_call | solution.py:1531
  174.4 0.7 copy.56.b_head
  175.1 37.5 %forward_head.1 = (bf16[1024,768]{1,0:T(8,128)(2,1)}, bf16[1024,2304]{1,0:T(8,128)(2,1)}, bf16[4,12,256,256]{3,2,1,0:T(8,128)(2,1)}, bf16[1024,768]{1,0:T(8,128)...) custom-call(f32[1024,768]{1,0:T(8,128)} %get-tuple-element.92.x.refs, ...), custom_call_target="tpu_custom_call" | custom-call | tf_op jit(solution)/shard_map/forward_head/pallas_call | solution.py:1296
  212.6 46.3 %backward_block.1 = (f32[1024,768]{1,0:T(8,128)}, bf16[1024,2304]{1,0:T(8,128)(2,1)}, bf16[1024,3072]{1,0:T(8,128)(2,1)}, bf16[1024,768]{1,0:T(8,128)(2,1)}, bf1...) custom-call(f32[4,14,768]{2,1,0:T(8,128)} %reshape.116.mod, ...), custom_call_target="tpu_custom_call" | custom-call | tf_op jit(solution)/shard_map/backward_block/pallas_call | solution.py:1404
  258.9 43.5 %weight_grads_out.1 = (bf16[5376,768]{1,0:T(8,128)(2,1)}, f32[24,3840]{1,0:T(8,128)}) custom-call(bf16[1024,2304]{1,0:T(8,128)(2,1)} %get-tuple-element.100.refs_0_, bf16[1024,768]{1,0:T(8,128)(2,1)} %get-tuple-element.101.refs_1_, bf16[1024,3072]{1,0:T(8,128)(2,1)} %get-tuple-element.102.refs_2_, bf16[1024,768]{1,0:T(8,128)(2,1)} %get-tuple-element.103.refs_3_, ...), custom_call_target="tpu_custom_call" | custom-call | tf_op jit(solution)/shard_map/weight_grads_out/pallas_call | solution.py:1628
  302.4 0.0 copy-start.19
  302.4 0.0 copy-start.22
  302.4 65.6 %backward_scatter.1 = (f32[1024,768]{1,0:T(8,128)}, bf16[1024,2304]{1,0:T(8,128)(2,1)}, bf16[1024,3072]{1,0:T(8,128)(2,1)}, bf16[1024,768]{1,0:T(8,128)(2,1)}, b...) custom-call(f32[4,14,768]{2,1,0:T(8,128)} %reshape.116.mod, ...), custom_call_target="tpu_custom_call" | custom-call | tf_op jit(solution)/shard_map/backward_scatter/pallas_call | solution.py:1673
  368.0 0.9 pad_maximum_fusion
  369.0 0.2 reshape.118
  369.2 0.8 copy.57
  370.0 121.0 %finish_grads.1 = (f32[168,768]{1,0:T(8,128)}, f32[24,3840]{1,0:T(8,128)}, f32[336,768]{1,0:T(8,128)}, f32[24,256]{1,0:T(8,128)}, f32[24,768]{1,0:T(8,128)}, /*i...) custom-call(bf16[1024,2304]{1,0:T(8,128)(2,1)} %get-tuple-element.117.refs_0_, ...), custom_call_target="tpu_custom_call" | custom-call | tf_op jit(solution)/shard_map/finish_grads/pallas_call | solution.py:1751
  491.0 0.0 copy-start.2
  491.0 0.0 copy-start.11
  491.0 0.0 copy-start.12
  491.1 1.2 bitcast_convert_fusion
  492.2 0.1 slice_reduce_fusion
  492.3 0.1 reshape_squeeze.6
  492.4 0.1 reshape_squeeze.7
  492.6 0.6 copy.75
  493.2 1.5 reshape.124
  494.7 0.8 constant_dynamic-update-slice_fusion
  495.5 0.6 multiply_reduce_fusion
  496.2 0.7 slice_reduce_fusion.2
  496.8 0.6 multiply_reduce_fusion.1
  498.7 0.6 multiply_reduce_fusion.2
  500.7 1.7 multiply_subtract_fusion
  502.5 1.9 fusion.15
  504.4 2.9 fusion.16
  507.4 0.0 copy-start.1
  507.4 0.0 copy-start.8
  507.4 2.5 fusion.13
  509.9 0.6 copy-done.10
  510.5 2.4 fusion.4
  512.9 0.2 copy.58
  513.1 0.1 slice.88
  513.2 0.1 concatenate.20
  513.4 1.0 fusion.12
  (50 shorter events, 0.2 us)
Async XLA Ops:
  0.7 99.1 %copy-start.14 = (f32[26912]{0:T(1024)S(1)}, f32[26912]{0:T(1024)}, u32[]{:S(2)}) copy-start(f32[26912]{0:T(1024)} %param.42) | copy-start | bytes 322948
  302.4 65.6 %copy-start.19 = (f32[4,6,768]{2,1,0:T(8,128)S(1)}, f32[4,6,768]{2,1,0:T(8,128)}, u32[]{:S(2)}) copy-start(f32[4,6,768]{2,1,0:T(8,128)} %get-tuple-element.126) | copy-start | bytes 221188
  302.4 65.6 %copy-start.22 = (f32[4,2,768]{2,1,0:T(2,128)S(1)}, f32[4,2,768]{2,1,0:T(2,128)}, u32[]{:S(2)}) copy-start(f32[4,2,768]{2,1,0:T(2,128)} %get-tuple-element.127) | copy-start | bytes 73732
  370.0 132.5 %copy-start.15 = (f32[768,32]{0,1:T(8,128)S(1)}, f32[768,32]{0,1:T(8,128)}, u32[]{:S(2)}) copy-start(f32[768,32]{0,1:T(8,128)} %param.39) | copy-start | bytes 294916
  491.0 13.4 %copy-start.2 = (f32[2,3840,24]{1,2,0:T(8,128)S(1)}, f32[2,3840,24]{1,2,0:T(8,128)}, u32[]{:S(2)}) copy-start(f32[2,3840,24]{1,2,0:T(8,128)} %param.36) | copy-start | bytes 2211844
  491.0 13.4 %copy-start.5 = (f32[24,3840]{1,0:T(8,128)S(1)}, f32[24,3840]{1,0:T(8,128)}, u32[]{:S(2)}) copy-start(f32[24,3840]{1,0:T(8,128)} %get-tuple-element.144.refs_27_) | copy-start | bytes 1105924
  491.0 13.4 %copy-start.11 = (f32[2,3840,24]{1,2,0:T(8,128)S(1)}, f32[2,3840,24]{1,2,0:T(8,128)}, u32[]{:S(2)}) copy-start(f32[2,3840,24]{1,2,0:T(8,128)} %param.38) | copy-start | bytes 2211844
  491.0 13.3 %copy-start.12 = (f32[2,3840,24]{1,2,0:T(8,128)S(1)}, f32[2,3840,24]{1,2,0:T(8,128)}, u32[]{:S(2)}) copy-start(f32[2,3840,24]{1,2,0:T(8,128)} %param.37) | copy-start | bytes 2211844
  502.5 4.9 copy-start
  502.5 4.9 copy-start.3
  502.5 4.9 copy-start.6
  502.5 4.9 copy-start.7
  502.5 4.9 copy-start.13
  507.4 2.5 copy-start.1
  507.4 2.5 copy-start.8
  507.4 2.5 copy-start.9
  507.4 3.0 copy-start.10
  510.4 2.7 copy-start.18
  510.4 2.8 copy-start.20
  510.4 2.8 copy-start.21
  510.5 2.9 copy-start.4
  510.5 2.9 copy-start.16
  510.5 2.9 copy-start.17

commit v7 on v6

--- a/solution.py
+++ b/solution.py
@@ -1308,7 +1308,7 @@
     )(*ins)
 
 
-def backward_image(refs, mod, base, weights, outs, hook=lambda: None):
+def backward_image(refs, mod, base, weights, outs, hook=lambda: None, early=False):
     up_ref, x_ref, x1_ref, probs, qkv, a, f, u = refs
     dx, d_qkv, d_u, d_f, d_a, d_mod, g_bin, g_bout = outs
     width = MODEL_WIDTH
@@ -1358,9 +1358,13 @@
         both = jnp.concatenate([jnp.where(mask, d_mixed, zero) for mask in head_masks(d_mixed.shape)], 0)
         return both, dot_nt(both, qkv[:, 2 * width + 128 * pair : 2 * width + 128 * (pair + 1)])
 
+    ahead = probs_back(0) if early else None
     for pair in range(HEADS // 2):
         lanes = [slice(j * width + 128 * pair, j * width + 128 * (pair + 1)) for j in range(3)]
-        d_masked, d_probs = probs_back(pair)
+        if early:
+            (d_masked, d_probs), ahead = ahead, probs_back(pair + 1) if pair + 1 < HEADS // 2 else None
+        else:
+            d_masked, d_probs = probs_back(pair)
         q, k = qkv[:, lanes[0]], qkv[:, lanes[1]]
         zero = jnp.zeros_like(q)
         masks = head_masks(q.shape)
@@ -1647,7 +1651,7 @@
     hooks = Hooks([place.greet, job.open_all] + job.steps(), slots, BACKWARD_POINTS)
     weights = Weights((w_in, w_out), (vm_in, vm_out), sems)
     weights.start((3, 2, 1, 0))
-    backward_image(ins, mod, 0, weights, outs, hooks)
+    backward_image(ins, mod, 0, weights, outs, hooks, True)
     d_patch = outs[0][...].astype(jnp.bfloat16)
 
     @pl.when(pl.program_id(0) == 0)

time: 524 us -> 521 us (level)
  no operation moved by 1% of the time
where the time goes in v7:
time: 521 us; the launch traced here: 513 us
  Pallas kernels  472 us (91%)
  other arithmetic  19 us (4%)
  local copies, waits for them, and re-layouts  16.3 us (3%)
    pallas_call x1, Pallas kernels, finish_grads(): pl.pallas_call(functools.partial(finish_kernel, devices), out_shape=[jax....  120 us
    pallas_call x1, Pallas kernels, gather_modulate(): pl.pallas_call(functools.partial(start_kernel, devices), out_shape=[full_...  87.3 us
    pallas_call x1, Pallas kernels, forward_gather(): pl.pallas_call(functools.partial(forward_gather_kernel, GATHER_SLOTS), gr...  74.1 us
    pallas_call x1, Pallas kernels, backward_scatter(): pl.pallas_call(functools.partial(backward_scatter_kernel, SCATTER_SLOTS),...  63 us
    pallas_call x1, Pallas kernels, backward_block(): pl.pallas_call(backward_kernel, grid=(images,), out_shape=[jax.ShapeDtype...  46.3 us
    pallas_call x1, Pallas kernels, weight_grads_out(): pl.pallas_call(grads_out_kernel, out_shape=[jax.ShapeDtypeStruct((IW, MOD...  43.5 us
    pallas_call x1, Pallas kernels, forward_head(): pl.pallas_call(functools.partial(head_kernel, scale_out), grid=(images,),...  37.5 us

profile of v7, /device:TPU:0, one launch (start us, length us, event | category | flops | bytes accessed | tf_op | source)
XLA Modules:
  0.0 512.6 jit_solution(5068074813621856507)
XLA Ops:
  0.7 0.0 copy-start.14
  0.7 0.8 fusion.27
  1.5 0.1 dynamic_slice.12
  1.6 0.7 broadcast_in_dim.13.refs_5_
  2.2 0.1 dynamic_slice.13
  2.3 0.7 broadcast_in_dim.14.refs_6_
  3.0 0.9 fusion.28
  3.9 0.1 dynamic_slice.14
  4.0 0.6 broadcast_in_dim.15.refs_7_
  4.5 0.7 slice.114
  5.2 0.1 reshape.113
  5.3 0.7 fusion.25
  6.0 0.1 copy.54
  6.1 0.1 broadcast_in_dim.12
  6.2 0.1 reshape.114
  6.3 0.7 convert_element_type.14
  6.9 0.1 fusion.21
  7.1 0.6 fusion.20.refs_2_
  7.7 87.3 %gather_modulate.1 = (bf16[5376,768]{1,0:T(8,128)(2,1)}, bf16[768,3840]{1,0:T(8,128)(2,1)}, f32[4,8,4,336]{3,2,1,0:T(4,128)}, f32[24,128]{1,0:T(8,128)}, f32[24,...) custom-call(f32[2,168,768]{2,1,0:T(8,128)} %bitcast.152, ...), custom_call_target="tpu_custom_call" | custom-call | tf_op jit(solution)/shard_map/gather_modulate/pallas_call | solution.py:1476
  94.9 0.9 copy.74
  95.9 0.9 reshape.116.mod
  96.8 0.8 slice.74
  97.6 0.9 reshape.117.w_patch
  98.5 0.7 broadcast_in_dim_reshape.6.b_in
  99.1 0.6 broadcast_in_dim.16.b_patch
  99.7 0.6 slice.73
  100.3 74.1 %forward_gather.1 = (bf16[1024,768]{1,0:T(8,128)(2,1)}, bf16[1024,2304]{1,0:T(8,128)(2,1)}, bf16[4,12,256,256]{3,2,1,0:T(8,128)(2,1)}, bf16[1024,768]{1,0:T(8,12...) custom-call(bf16[4,16,256]{2,1,0:T(8,128)(2,1)} %bitcast.177, ...), custom_call_target="tpu_custom_call" | custom-call | tf_op jit(solution)/shard_map/forward_gather/pallas_call | solution.py:1535
  174.4 0.7 copy.56.b_head
  175.1 37.5 %forward_head.1 = (bf16[1024,768]{1,0:T(8,128)(2,1)}, bf16[1024,2304]{1,0:T(8,128)(2,1)}, bf16[4,12,256,256]{3,2,1,0:T(8,128)(2,1)}, bf16[1024,768]{1,0:T(8,128)...) custom-call(f32[1024,768]{1,0:T(8,128)} %get-tuple-element.92.x.refs, ...), custom_call_target="tpu_custom_call" | custom-call | tf_op jit(solution)/shard_map/forward_head/pallas_call | solution.py:1296
  212.6 46.3 %backward_block.1 = (f32[1024,768]{1,0:T(8,128)}, bf16[1024,2304]{1,0:T(8,128)(2,1)}, bf16[1024,3072]{1,0:T(8,128)(2,1)}, bf16[1024,768]{1,0:T(8,128)(2,1)}, bf1...) custom-call(f32[4,14,768]{2,1,0:T(8,128)} %reshape.116.mod, ...), custom_call_target="tpu_custom_call" | custom-call | tf_op jit(solution)/shard_map/backward_block/pallas_call | solution.py:1408
  258.9 43.5 %weight_grads_out.1 = (bf16[5376,768]{1,0:T(8,128)(2,1)}, f32[24,3840]{1,0:T(8,128)}) custom-call(bf16[1024,2304]{1,0:T(8,128)(2,1)} %get-tuple-element.100.refs_0_, bf16[1024,768]{1,0:T(8,128)(2,1)} %get-tuple-element.101.refs_1_, bf16[1024,3072]{1,0:T(8,128)(2,1)} %get-tuple-element.102.refs_2_, bf16[1024,768]{1,0:T(8,128)(2,1)} %get-tuple-element.103.refs_3_, ...), custom_call_target="tpu_custom_call" | custom-call | tf_op jit(solution)/shard_map/weight_grads_out/pallas_call | solution.py:1632
  302.4 0.0 copy-start.19
  302.4 0.0 copy-start.22
  302.4 63.0 %backward_scatter.1 = (f32[1024,768]{1,0:T(8,128)}, bf16[1024,2304]{1,0:T(8,128)(2,1)}, bf16[1024,3072]{1,0:T(8,128)(2,1)}, bf16[1024,768]{1,0:T(8,128)(2,1)}, b...) custom-call(f32[4,14,768]{2,1,0:T(8,128)} %reshape.116.mod, ...), custom_call_target="tpu_custom_call" | custom-call | tf_op jit(solution)/shard_map/backward_scatter/pallas_call | solution.py:1677
  365.5 0.9 pad_maximum_fusion
  366.4 0.2 reshape.118
  366.6 0.8 copy.57
  367.4 120.5 %finish_grads.1 = (f32[168,768]{1,0:T(8,128)}, f32[24,3840]{1,0:T(8,128)}, f32[336,768]{1,0:T(8,128)}, f32[24,256]{1,0:T(8,128)}, f32[24,768]{1,0:T(8,128)}, /*i...) custom-call(bf16[1024,2304]{1,0:T(8,128)(2,1)} %get-tuple-element.117.refs_0_, ...), custom_call_target="tpu_custom_call" | custom-call | tf_op jit(solution)/shard_map/finish_grads/pallas_call | solution.py:1755
  487.9 0.0 copy-start.2
  487.9 0.0 copy-start.11
  487.9 1.2 bitcast_convert_fusion
  489.1 0.1 slice_reduce_fusion
  489.2 0.1 reshape_squeeze.6
  489.3 0.1 reshape_squeeze.7
  489.5 0.6 copy.75
  490.1 1.5 reshape.124
  491.6 0.8 constant_dynamic-update-slice_fusion
  492.4 0.6 multiply_reduce_fusion
  493.1 0.7 slice_reduce_fusion.2
  493.7 0.6 multiply_reduce_fusion.1
  495.6 0.6 multiply_reduce_fusion.2
  497.6 1.7 multiply_subtract_fusion
  499.4 1.9 fusion.15
  501.3 2.9 fusion.16
  504.3 0.0 copy-start.8
  504.3 0.0 copy-start.9
  504.3 2.5 fusion.13
  506.8 0.6 copy-done.10
  507.3 0.0 copy-start.16
  507.4 2.4 fusion.4
  509.8 0.2 copy.58
  510.0 0.1 slice.88
  510.1 0.1 concatenate.20
  510.3 1.0 fusion.12
  (50 shorter events, 0.2 us)
Async XLA Ops:
  0.7 99.1 %copy-start.14 = (f32[26912]{0:T(1024)S(1)}, f32[26912]{0:T(1024)}, u32[]{:S(2)}) copy-start(f32[26912]{0:T(1024)} %param.42) | copy-start | bytes 322948
  302.4 63.0 %copy-start.19 = (f32[4,6,768]{2,1,0:T(8,128)S(1)}, f32[4,6,768]{2,1,0:T(8,128)}, u32[]{:S(2)}) copy-start(f32[4,6,768]{2,1,0:T(8,128)} %get-tuple-element.126) | copy-start | bytes 221188
  302.4 63.0 %copy-start.22 = (f32[4,2,768]{2,1,0:T(2,128)S(1)}, f32[4,2,768]{2,1,0:T(2,128)}, u32[]{:S(2)}) copy-start(f32[4,2,768]{2,1,0:T(2,128)} %get-tuple-element.127) | copy-start | bytes 73732
  367.4 132.0 %copy-start.15 = (f32[768,32]{0,1:T(8,128)S(1)}, f32[768,32]{0,1:T(8,128)}, u32[]{:S(2)}) copy-start(f32[768,32]{0,1:T(8,128)} %param.39) | copy-start | bytes 294916
  487.9 13.4 %copy-start.2 = (f32[2,3840,24]{1,2,0:T(8,128)S(1)}, f32[2,3840,24]{1,2,0:T(8,128)}, u32[]{:S(2)}) copy-start(f32[2,3840,24]{1,2,0:T(8,128)} %param.36) | copy-start | bytes 2211844
  487.9 13.4 %copy-start.5 = (f32[24,3840]{1,0:T(8,128)S(1)}, f32[24,3840]{1,0:T(8,128)}, u32[]{:S(2)}) copy-start(f32[24,3840]{1,0:T(8,128)} %get-tuple-element.144.refs_27_) | copy-start | bytes 1105924
  487.9 13.4 %copy-start.11 = (f32[2,3840,24]{1,2,0:T(8,128)S(1)}, f32[2,3840,24]{1,2,0:T(8,128)}, u32[]{:S(2)}) copy-start(f32[2,3840,24]{1,2,0:T(8,128)} %param.38) | copy-start | bytes 2211844
  487.9 13.3 %copy-start.12 = (f32[2,3840,24]{1,2,0:T(8,128)S(1)}, f32[2,3840,24]{1,2,0:T(8,128)}, u32[]{:S(2)}) copy-start(f32[2,3840,24]{1,2,0:T(8,128)} %param.37) | copy-start | bytes 2211844
  499.3 4.9 copy-start
  499.4 4.9 copy-start.3
  499.4 4.9 copy-start.6
  499.4 4.9 copy-start.7
  499.4 4.9 copy-start.13
  504.2 2.5 copy-start.1
  504.3 2.5 copy-start.8
  504.3 2.5 copy-start.9
  504.3 3.0 copy-start.10
  507.3 2.7 copy-start.18
  507.3 2.8 copy-start.20
  507.3 2.8 copy-start.21
  507.3 2.9 copy-start.4
  507.3 2.9 copy-start.16
  507.4 2.9 copy-start.17
